TPU v7x, 256 devices: a whole 4x4x8 slice. The times are simulated.
256 devices in a mesh: dp: 8 (over z), ctx: 32 (over y, x, core).
Axes of the slice: x: 4, y: 4, z: 8, core: 2. Of those that a mesh axis runs over, the one named last changes fastest.
Arguments:
- query: bfloat16 [8, 8192, 1792], P('dp', 'ctx'), may hold values from -8 to 8
- keys_values: bfloat16 [8, 8192, 512], P('dp', 'ctx'), may hold values from -8 to 8
- beacon_query: bfloat16 [8, 512, 1792], P('dp', 'ctx'), may hold values from -8 to 8
- beacon_hidden: bfloat16 [8, 512, 3584], P('dp', 'ctx'), may hold values from -6 to 6
- beacon_weight: bfloat16 [3584, 512], P('ctx'), may hold values from -0.09375 to 0.09375
- grad_tokens: bfloat16 [8, 8192, 1792], P('dp', 'ctx'), may hold values from -6 to 6
- grad_beacons: bfloat16 [8, 512, 1792], P('dp', 'ctx'), may hold values from -6 to 6
Outputs:
- tokens_out: bfloat16 [8, 8192, 1792], P('dp', 'ctx')
- beacons_out: bfloat16 [8, 512, 1792], P('dp', 'ctx')
- grad_query: bfloat16 [8, 8192, 1792], P('dp', 'ctx')
- grad_keys_values: bfloat16 [8, 8192, 512], P('dp', 'ctx')
- grad_beacon_query: bfloat16 [8, 512, 1792], P('dp', 'ctx')
- grad_beacon_hidden: bfloat16 [8, 512, 3584], P('dp', 'ctx')
- grad_weight: float32 [3584, 512], P('ctx')
All inputs are finite; a program needn't handle non-finite values.
Results may differ from a plain program's by a relative error of at most 0.03.
Values may be sent and summed in bfloat16 or wider, within the bound.
No kernel may reach another device: no remote copies, remote signals or barrier semaphores. Data moves between devices by JAX's collectives and lax.ppermute only.
A program may use at most 128 MiB of HBM per device.

v0:
```python
import jax
import jax.numpy as jnp
from jax import lax
from jax.sharding import PartitionSpec as P

KVH = 2
HD = 128
GROUP = 7


def allowed_keys(span_len, beacon_count, total_beacons, position):
    row_ids = jnp.arange(span_len + beacon_count, dtype=jnp.int32)[:, None]
    col_ids = jnp.arange(total_beacons + span_len, dtype=jnp.int32)[None, :]
    beacon_row = row_ids >= span_len
    own_start = position * beacon_count
    beacon_rank = row_ids - span_len
    prefix_cols = col_ids < own_start
    own_cols = (
        beacon_row
        & (col_ids >= own_start)
        & (col_ids - own_start <= beacon_rank)
        & (col_ids < total_beacons)
    )
    token_cols = (col_ids >= total_beacons) & (beacon_row | (col_ids - total_beacons <= row_ids))
    return prefix_cols | own_cols | token_cols


def interval_pass(tok_query, tok_kv, bea_query, all_kv, cot_tok, cot_bea, position):
    span_len = tok_query.shape[0]
    total_beacons = all_kv.shape[0]
    row_query = jnp.concatenate([tok_query, bea_query], 0)
    row_cot = jnp.concatenate([cot_tok, cot_bea], 0)
    key_rows = jnp.concatenate([all_kv, tok_kv], 0)
    allowed = allowed_keys(span_len, bea_query.shape[0], total_beacons, position)
    factor = HD ** (-0.5)
    width = GROUP * HD
    out_parts, dq_parts, dk_parts, dv_parts = ([], [], [], [])
    for kv_group in range(KVH):
        q_group = row_query[:, kv_group * width : (kv_group + 1) * width].reshape(-1, GROUP, HD)
        c_group = row_cot[:, kv_group * width : (kv_group + 1) * width].reshape(-1, GROUP, HD)
        k_group = key_rows[:, kv_group * HD : (kv_group + 1) * HD]
        v_group = key_rows[:, (KVH + kv_group) * HD : (KVH + kv_group + 1) * HD]
        scores = (
            jnp.einsum("rjd,cd->jrc", q_group, k_group, preferred_element_type=jnp.float32) * factor
        )
        scores = jnp.where(allowed[None], scores, -jnp.inf)
        highest = jnp.max(scores, -1, keepdims=True)
        expo_terms = jnp.exp(scores - highest)
        probs = expo_terms / jnp.sum(expo_terms, -1, keepdims=True)
        weights = probs.astype(jnp.bfloat16)
        out_parts.append(
            jnp.einsum("jrc,cd->rjd", weights, v_group, preferred_element_type=jnp.float32).reshape(
                -1, width
            )
        )
        dv_parts.append(
            jnp.einsum("jrc,rjd->cd", weights, c_group, preferred_element_type=jnp.float32)
        )
        dweights = jnp.einsum("rjd,cd->jrc", c_group, v_group, preferred_element_type=jnp.float32)
        centre = jnp.sum(probs * dweights, -1, keepdims=True)
        dscores = (probs * (dweights - centre)).astype(jnp.bfloat16)
        dq_parts.append(
            jnp.einsum("jrc,cd->rjd", dscores, k_group, preferred_element_type=jnp.float32).reshape(
                -1, width
            )
            * factor
        )
        dk_parts.append(
            jnp.einsum("jrc,rjd->cd", dscores, q_group, preferred_element_type=jnp.float32) * factor
        )
    attended = jnp.concatenate(out_parts, -1).astype(jnp.bfloat16)
    query_grad = jnp.concatenate(dq_parts, -1).astype(jnp.bfloat16)
    key_grad = jnp.concatenate(dk_parts + dv_parts, -1)
    return (
        attended[:span_len],
        attended[span_len:],
        query_grad[:span_len],
        query_grad[span_len:],
        key_grad[total_beacons:].astype(jnp.bfloat16),
        key_grad[:total_beacons],
    )


def shards(
    query, keys_values, beacon_query, beacon_hidden, beacon_weight, grad_tokens, grad_beacons
):
    position = lax.axis_index("ctx")
    hidden_rows = beacon_hidden[0]
    full_weight = lax.all_gather(beacon_weight, "ctx", axis=0, tiled=True)
    own_kv = jnp.dot(hidden_rows, full_weight, preferred_element_type=jnp.float32).astype(
        jnp.bfloat16
    )
    all_kv = lax.all_gather(own_kv, "ctx", axis=0, tiled=True)
    result = interval_pass(
        query[0], keys_values[0], beacon_query[0], all_kv, grad_tokens[0], grad_beacons[0], position
    )
    tokens_out, beacons_out, query_grad, beacon_qgrad, token_kvgrad, contrib = result
    own_grad = lax.psum_scatter(
        contrib.astype(jnp.bfloat16), "ctx", scatter_dimension=0, tiled=True
    )
    hidden_grad = lax.dot_general(
        own_grad, full_weight, (((1,), (1,)), ((), ())), preferred_element_type=jnp.float32
    ).astype(jnp.bfloat16)
    weight_part = lax.psum_scatter(
        lax.dot_general(
            hidden_rows, own_grad, (((0,), (0,)), ((), ())), preferred_element_type=jnp.float32
        ).astype(jnp.bfloat16),
        "ctx",
        scatter_dimension=0,
        tiled=True,
    )
    grad_weight = lax.psum(weight_part, "dp").astype(jnp.float32)
    return (
        tokens_out[None],
        beacons_out[None],
        query_grad[None],
        token_kvgrad[None],
        beacon_qgrad[None],
        hidden_grad[None],
        grad_weight,
    )


def solution(mesh):
    placed = (
        P("dp", "ctx", None),
        P("dp", "ctx", None),
        P("dp", "ctx", None),
        P("dp", "ctx", None),
        P("ctx", None),
        P("dp", "ctx", None),
        P("dp", "ctx", None),
    )
    return jax.shard_map(
        shards,
        mesh=mesh,
        in_specs=placed,
        out_specs=(
            P("dp", "ctx", None),
            P("dp", "ctx", None),
            P("dp", "ctx", None),
            P("dp", "ctx", None),
            P("dp", "ctx", None),
            P("dp", "ctx", None),
            P("ctx", None),
        ),
        check_vma=False,
    )
```

profile of v0, /device:TPU:2, one launch (start us, length us, event | category | flops | bytes accessed | tf_op | source)
XLA Modules:
  0.0 388.7 jit_solution(17404205105764046721)
XLA Ops:
  7.2 0.7 all-gather.2.cloned.1.call-update
  8.0 1.3 fusion.85
  9.3 1.6 fusion.84
  11.0 0.4 fusion.53
  11.4 52.3 %all-gather.2.cloned.1.call-done = bf16[3584,512]{1,0:T(8,128)(2,1)} async-done(((bf16[112,512]{1,0:T(8,128)(2,1)}), bf16[3584,512]{1,0:T(8,128)(2,1)}) %all-gather.2.cloned.1.call-update) | async-done | bytes 3670032 | tf_op jit(solution)/shard_map/all_gather | solution.py:89
  63.7 2.6 convolution_convert_fusion.2
  66.4 23.3 %all_gather.7 = bf16[512,512]{1,0:T(8,128)(2,1)S(1)} all-gather(bf16[16,512]{1,0:T(8,128)(2,1)S(1)} %convolution_convert_fusion.2), channel_id=1, replica_groups=mesh['dp'=8,'ctx'=32] {'ctx'}, dimensions={0}, use_global_device_ids=true | all-gather | bytes 540672 | tf_op jit(solution)/shard_map/all_gather | solution.py:93
  89.7 4.7 %fusion.136 = (f32[7,272]{1,0:T(8,128)S(1)}, f32[7,272,768]{2,1,0:T(8,128)}) fusion(pred[272,768]{1,0:T(8,128)(4,1)S(1)} %fusion.53, bf16[768,128,1]{1,0,2:T(8,128)(2,1)S(1)} %fusion.107, bf16[34,7,8,128]{3,2,1,0:T(8,128)(2,1)S(1)} %get-tuple-element.30), kind=kOutput, calls=%fused_computation.144 | convolution fusion | flops 380191488 | bytes 6749632 | tf_op jit(solution)/shard_map/sub | solution.py:48
  94.4 3.8 fusion.45
  98.2 0.6 copy-done.3
  98.8 3.5 fusion.2
  102.3 4.7 %fusion.127 = (f32[7,272]{1,0:T(8,128)S(1)}, f32[7,272,768]{2,1,0:T(8,128)}) fusion(pred[272,768]{1,0:T(8,128)(4,1)S(1)} %fusion.53, bf16[34,7,8,128]{3,2,1,0:T(8,128)(2,1)S(1)} %get-tuple-element.31, bf16[512,512]{1,0:T(8,128)(2,1)S(1)} %all_gather.7, bf16[256,512]{1,0:T(8,128)(2,1)S(1)} %bitcast.192), kind=kOutput, calls=%fused_computation.143 | convolution fusion | flops 380584704 | bytes 7339456 | tf_op jit(solution)/shard_map/sub | solution.py:48
  107.0 3.8 fusion.42
  110.8 0.5 copy-done.4
  111.4 1.1 fusion.5
  112.5 0.2 slice-done
  112.7 1.2 slice-done.2
  113.9 0.6 slice-done.1
  114.5 0.5 slice-done.3
  115.0 1.0 fusion.4
  116.0 0.7 fusion.49
  116.7 1.1 fusion.7
  117.8 1.6 copy-done.1
  119.4 0.7 fusion.48
  120.1 0.7 copy-done.10
  120.8 0.8 fusion.50
  121.6 2.1 copy.44
  123.7 0.0 reduce-scatter.9.cloned.1.call-start
  123.8 84.3 %reduce-scatter.7.cloned.1.call-done = bf16[16,512]{1,0:T(8,128)(2,1)} async-done(((bf16[512,512]{1,0:T(8,128)(2,1)}), bf16[16,512]{1,0:T(8,128)(2,1)}) %reduce-scatter.7.cloned.1.call-update) | async-done | bytes 16400
  208.0 3.7 fusion.8
  211.7 6.0 %copy.46 = bf16[3584,512]{1,0:T(8,128)(2,1)} copy(bf16[3584,512]{0,1:T(8,128)(2,1)} %fusion.8) | data formatting | bytes 7340032
  217.8 1.6 fusion.100
  219.4 1.8 copy.42
  221.2 3.9 fusion.37
  225.1 0.9 fusion.41
  226.1 3.7 fusion.34
  229.9 0.1 bitcast_dynamic-update-slice_fusion.2
  230.0 0.9 fusion.40
  230.9 0.1 bitcast_dynamic-update-slice_fusion
  231.0 0.6 slice_bitcast_fusion.3
  231.6 0.6 slice_bitcast_fusion.2
  232.2 1.0 slice_bitcast_fusion.1
  233.2 1.0 slice_bitcast_fusion
  234.2 71.8 %reduce-scatter.9.cloned.1.call-done = bf16[112,512]{1,0:T(8,128)(2,1)} async-done(((bf16[3584,512]{1,0:T(8,128)(2,1)}), bf16[112,512]{1,0:T(8,128)(2,1)}) %reduce-scatter.9.cloned.1.call-update) | async-done | bytes 114704
  306.0 1.7 copy.47
  307.7 3.8 fusion.11
  311.4 69.0 %all-reduce.2.cloned.1.call-done = bf16[112,512]{0,1:T(8,128)(2,1)} async-done(((bf16[112,512]{0,1:T(8,128)(2,1)}), bf16[112,512]{0,1:T(8,128)(2,1)}) %all-reduce.2.cloned.1.call-update) | async-done | bytes 114704 | tf_op jit(solution)/shard_map/psum | solution.py:112
  380.4 1.7 copy.43
  (52 shorter events, 0.4 us)
Async XLA Ops:
  7.2 56.6 %copy-start = (bf16[1,16,3584]{2,1,0:T(8,128)(2,1)S(1)}, bf16[1,16,3584]{2,1,0:T(8,128)(2,1)}, u32[]{:S(2)}) copy-start(bf16[1,16,3584]{2,1,0:T(8,128)(2,1)} %param.10) | copy-start | bytes 344068
  7.2 82.4 %copy-start.7 = (bf16[1,256,512]{2,1,0:T(8,128)(2,1)S(1)}, bf16[1,256,512]{2,1,0:T(8,128)(2,1)}, u32[]{:S(2)}) copy-start(bf16[1,256,512]{2,1,0:T(8,128)(2,1)} %param.8) | copy-start | bytes 786436
  7.2 56.6 %all-gather.2.cloned.1.call-start = ((), (), s32[]{:S(2)}) async-start(), calls=%async_computation.2 | async-start | bytes 3784704 | tf_op jit(solution)/shard_map/all_gather | solution.py:89
  7.9 200.1 %reduce-scatter.7.cloned.1.call-start = ((), (), s32[]{:S(2)}) async-start(), calls=%async_computation.4 | async-start | bytes 540672
  9.3 85.1 %copy-start.15 = (bf16[34,7,8,128]{3,2,1,0:T(8,128)(2,1)}, bf16[34,7,8,128]{3,2,1,0:T(8,128)(2,1)S(1)}, u32[]{:S(2)}) copy-start(bf16[34,7,8,128]{3,2,1,0:T(8,128)(2,1)S(1)} %get-tuple-element.30) | copy-start | bytes 1462276
  9.3 93.0 %copy-start.13 = (bf16[34,7,8,128]{3,2,1,0:T(8,128)(2,1)}, bf16[34,7,8,128]{3,2,1,0:T(8,128)(2,1)S(1)}, u32[]{:S(2)}) copy-start(bf16[34,7,8,128]{3,2,1,0:T(8,128)(2,1)S(1)} %get-tuple-element.31) | copy-start | bytes 1462276
  89.6 21.2 %copy-start.5 = (bf16[512,512]{1,0:T(8,128)(2,1)}, bf16[512,512]{1,0:T(8,128)(2,1)S(1)}, u32[]{:S(2)}) copy-start(bf16[512,512]{1,0:T(8,128)(2,1)S(1)} %all_gather.7) | copy-start | bytes 1572868
  89.7 8.5 %copy-start.11 = (bf16[768,128,1]{1,0,2:T(8,128)(2,1)}, bf16[768,128,1]{1,0,2:T(8,128)(2,1)S(1)}, u32[]{:S(2)}) copy-start(bf16[768,128,1]{1,0,2:T(8,128)(2,1)S(1)} %fusion.107) | copy-start | bytes 589828
  94.4 4.4 %copy-start.3 = (f32[7,272,768]{2,1,0:T(8,128)S(1)}, f32[7,272,768]{2,1,0:T(8,128)}, u32[]{:S(2)}) copy-start(f32[7,272,768]{2,1,0:T(8,128)} %get-tuple-element.35) | copy-start | bytes 17547268
  107.0 4.4 %copy-start.4 = (f32[7,272,768]{2,1,0:T(8,128)S(1)}, f32[7,272,768]{2,1,0:T(8,128)}, u32[]{:S(2)}) copy-start(f32[7,272,768]{2,1,0:T(8,128)} %get-tuple-element.33) | copy-start | bytes 17547268
  107.0 5.7 %slice-start = ((s8[5849088]{0:T(1024)(128)(4,1)}), s8[4194304]{0:T(1024)(128)(4,1)S(1)}, s32[]{:S(2)}) async-start(s8[5849088]{0:T(1024)(128)(4,1)} %bitcast.186), calls=%async_computation.6 | async-start | bytes 8388608
  107.0 6.9 %slice-start.2 = ((s8[5849088]{0:T(1024)(128)(4,1)}), s8[4194304]{0:T(1024)(128)(4,1)S(1)}, s32[]{:S(2)}) async-start(s8[5849088]{0:T(1024)(128)(4,1)} %bitcast.188), calls=%async_computation.8 | async-start | bytes 8388608
  111.4 8.7 %copy-start.8 = (bf16[768,128]{0,1:T(8,128)(2,1)}, bf16[768,128]{0,1:T(8,128)(2,1)S(1)}, u32[]{:S(2)}) copy-start(bf16[768,128]{0,1:T(8,128)(2,1)S(1)} %fusion.42) | copy-start | bytes 589828
  111.4 3.1 slice-start.1
  111.4 3.6 slice-start.3
  115.0 1.0 copy-start.16
  116.7 3.4 copy-start.9
  116.7 2.7 copy-start.14
  117.8 1.6 copy-start.1
  120.1 0.7 copy-start.10
  123.7 182.3 %reduce-scatter.9.cloned.1.call-start = ((), (), s32[]{:S(2)}) async-start(), calls=%async_computation.5 | async-start | bytes 3784704
  217.7 162.7 %all-reduce.2.cloned.1.call-start = ((), (), s32[]{:S(2)}) async-start(), calls=%async_computation.3 | async-start | bytes 262144 | tf_op jit(solution)/shard_map/psum | solution.py:112
  221.2 3.9 %copy-start.2 = (bf16[7,272,768]{2,1,0:T(8,128)(2,1)S(1)}, bf16[7,272,768]{2,1,0:T(8,128)(2,1)}, u32[]{:S(2)}) copy-start(bf16[7,272,768]{2,1,0:T(8,128)(2,1)} %copy-done.1) | copy-start | bytes 8773636
  221.2 3.9 %copy-start.6 = (bf16[512,512]{1,0:T(8,128)(2,1)S(1)}, bf16[512,512]{1,0:T(8,128)(2,1)}, u32[]{:S(2)}) copy-start(bf16[512,512]{1,0:T(8,128)(2,1)} %copy-done.5) | copy-start | bytes 1572868
  226.1 3.8 copy-start.12
  229.9 77.8 %copy-start.17 = (bf16[16,512]{1,0:T(8,128)(2,1)S(1)}, bf16[16,512]{1,0:T(8,128)(2,1)}, u32[]{:S(2)}) copy-start(bf16[16,512]{1,0:T(8,128)(2,1)} %reduce-scatter.7.cloned.1.call-done) | copy-start | bytes 49156
Sparse Core Ops, SparseCore 0:
  10.6 53.1 all-gather.1
  123.8 84.1 reduce-scatter.6
  217.9 88.0 reduce-scatter.8
  308.8 71.5 all-reduce.1
where the time goes:
time: 389 us
  waiting for transfers between devices  278 us (71%)
  matrix products  42.6 us (11%)
  blocking collectives  23.3 us (6%)
  local copies, waits for them, and re-layouts  22.5 us (6%)
  between operations  14.1 us (4%)
  other arithmetic  7.95 us (2%)
    unnamed x6, waiting for transfers between devices  157 us
    psum x1, waiting for transfers between devices, shards(): grad_weight = lax.psum(weight_part, 'dp').astype(jnp.float32)  69 us
    all_gather x1, waiting for transfers between devices, shards(): full_weight = lax.all_gather(beacon_weight, 'ctx', axis=0, tiled=True)  52.3 us
    all_gather x1, blocking collectives, shards(): all_kv = lax.all_gather(own_kv, 'ctx', axis=0, tiled=True)  23.3 us
    unnamed x51, local copies, waits for them, and re-layouts  19.2 us
    sub x2, matrix products, interval_pass(): expo_terms = jnp.exp(scores - highest)  9.42 us
  transfers between devices with their start and end apart: 4, of which 4 were waited for; matrix products, arithmetic and copies ran while one was open for 6% of the time, Pallas kernels for 0%

commit v1 on v0

--- a/solution.py
+++ b/solution.py
@@ -81,35 +81,55 @@
     )
 
 
+def exchange(blocks):
+    return lax.all_to_all(blocks, "ctx", 0, 0, tiled=True)
+
+
+def reduce_blocks(blocks):
+    return jnp.sum(exchange(blocks).astype(jnp.float32), 0).astype(jnp.bfloat16)
+
+
+def gather_rows(rows, count):
+    return exchange(jnp.broadcast_to(rows[None], (count,) + rows.shape)).reshape(-1, rows.shape[-1])
+
+
+def sum_dp(part):
+    size = lax.axis_size("dp")
+    step = 1
+    while step < size:
+        sent = part.astype(jnp.bfloat16)
+        pairs = [(i, i // (2 * step) * 2 * step + 2 * step - 1 - i % (2 * step)) for i in range(size)]
+        part = sent.astype(jnp.float32) + lax.ppermute(sent, "dp", pairs).astype(jnp.float32)
+        step *= 2
+    return part
+
+
 def shards(
     query, keys_values, beacon_query, beacon_hidden, beacon_weight, grad_tokens, grad_beacons
 ):
     position = lax.axis_index("ctx")
+    count = lax.axis_size("ctx")
+    rows = beacon_hidden.shape[1]
     hidden_rows = beacon_hidden[0]
     full_weight = lax.all_gather(beacon_weight, "ctx", axis=0, tiled=True)
-    own_kv = jnp.dot(hidden_rows, full_weight, preferred_element_type=jnp.float32).astype(
-        jnp.bfloat16
-    )
-    all_kv = lax.all_gather(own_kv, "ctx", axis=0, tiled=True)
+    hidden_cols = exchange(hidden_rows.reshape(rows, count, -1).transpose(1, 0, 2))
+    hidden_cols = hidden_cols.reshape(rows * count, -1)
+    part_kv = jnp.dot(hidden_cols, beacon_weight, preferred_element_type=jnp.float32)
+    own_kv = reduce_blocks(part_kv.astype(jnp.bfloat16).reshape(count, rows, -1))
+    all_kv = gather_rows(own_kv, count)
     result = interval_pass(
         query[0], keys_values[0], beacon_query[0], all_kv, grad_tokens[0], grad_beacons[0], position
     )
     tokens_out, beacons_out, query_grad, beacon_qgrad, token_kvgrad, contrib = result
-    own_grad = lax.psum_scatter(
-        contrib.astype(jnp.bfloat16), "ctx", scatter_dimension=0, tiled=True
-    )
+    own_grad = reduce_blocks(contrib.astype(jnp.bfloat16).reshape(count, rows, -1))
+    all_grad = gather_rows(own_grad, count)
     hidden_grad = lax.dot_general(
         own_grad, full_weight, (((1,), (1,)), ((), ())), preferred_element_type=jnp.float32
     ).astype(jnp.bfloat16)
-    weight_part = lax.psum_scatter(
-        lax.dot_general(
-            hidden_rows, own_grad, (((0,), (0,)), ((), ())), preferred_element_type=jnp.float32
-        ).astype(jnp.bfloat16),
-        "ctx",
-        scatter_dimension=0,
-        tiled=True,
+    weight_part = lax.dot_general(
+        hidden_cols, all_grad, (((0,), (0,)), ((), ())), preferred_element_type=jnp.float32
     )
-    grad_weight = lax.psum(weight_part, "dp").astype(jnp.float32)
+    grad_weight = sum_dp(weight_part)
     return (
         tokens_out[None],
         beacons_out[None],

time: 389 us -> 163 us (0.42)
  waiting for transfers between devices: 278 us -> 37 us
  starting transfers between devices: 0.16 us -> 34.8 us
  blocking collectives: 23.3 us -> 14 us
  local copies, waits for them, and re-layouts: 22.5 us -> 14 us
    unnamed x6 -> x1, waiting for transfers between devices: 157 us -> 0.68 us
    psum x1 -> x0, waiting for transfers between devices: 69 us -> none  [shards(): grad_weight = lax.psum(weight_part, 'dp').astype(jnp.float32)]
    all_gather x1, waiting for transfers between devices: 52.3 us -> 0.01 us  [shards(): full_weight = lax.all_gather(beacon_weight, 'ctx', axis=0, tiled=True)]
    all_to_all x0 -> x4, waiting for transfers between devices: none -> 27.5 us  [exchange(): return lax.all_to_all(blocks, 'ctx', 0, 0, tiled=True)]
    all_gather x1 -> x0, blocking collectives: 23.3 us -> none  [shards(): all_kv = lax.all_gather(own_kv, 'ctx', axis=0, tiled=True)]
    all_to_all x0 -> x4, starting transfers between devices: none -> 22.9 us  [exchange(): return lax.all_to_all(blocks, 'ctx', 0, 0, tiled=True)]
    unnamed x51 -> x59, local copies, waits for them, and re-layouts: 19.2 us -> 4.84 us
    all_to_all x0 -> x1, blocking collectives: none -> 14 us  [exchange(): return lax.all_to_all(blocks, 'ctx', 0, 0, tiled=True)]
  transfers between devices with their start and end apart: 4 -> 8, of which waited for: 4 -> 6; matrix products, arithmetic and copies ran while one was open for 6% -> 32% of each run, Pallas kernels for 0% -> 0%
where the time goes in v1:
time: 163 us; the launch traced here: 162 us
  matrix products  39.2 us (24%)
  waiting for transfers between devices  37 us (23%)
  starting transfers between devices  34.8 us (21%)
  between operations  14.5 us (9%)
  local copies, waits for them, and re-layouts  14 us (9%)
  blocking collectives  14 us (9%)
  other arithmetic  8.46 us (5%)
    all_to_all x4, waiting for transfers between devices, exchange(): return lax.all_to_all(blocks, 'ctx', 0, 0, tiled=True)  27.5 us
    all_to_all x4, starting transfers between devices, exchange(): return lax.all_to_all(blocks, 'ctx', 0, 0, tiled=True)  22.9 us
    all_to_all x1, blocking collectives, exchange(): return lax.all_to_all(blocks, 'ctx', 0, 0, tiled=True)  14 us
    ppermute x3, starting transfers between devices, sum_dp(): lax.ppermute(sent, 'dp', pairs).astype(jnp.float32)  11.9 us
    sub x2, matrix products, interval_pass(): expo_terms = jnp.exp(scores - highest)  10.4 us
    ppermute x3, waiting for transfers between devices, sum_dp(): lax.ppermute(sent, 'dp', pairs).astype(jnp.float32)  8.8 us
    dot_general x2, matrix products, interval_pass(): jnp.einsum('jrc,cd->rjd', weights, v_group, preferred_element_type=jnp.fl...  7.55 us
    dot_general x2, matrix products, interval_pass(): jnp.einsum('jrc,rjd->cd', weights, c_group, preferred_element_type=jnp.fl...  5.39 us
  transfers between devices with their start and end apart: 8, of which 6 were waited for; matrix products, arithmetic and copies ran while one was open for 32% of the time, Pallas kernels for 0%

profile of v1, /device:TPU:2, one launch (start us, length us, event | category | flops | bytes accessed | tf_op | source)
XLA Modules:
  0.0 161.9 jit_solution(1621835680159877740)
XLA Ops:
  7.2 1.2 reshape_squeeze.3
  8.5 14.0 %all_to_all.25 = bf16[32,16,112]{2,1,0:T(8,128)(2,1)S(1)} all-to-all(bf16[32,16,112]{2,1,0:T(8,128)(2,1)S(1)} %copy.46), channel_id=1, replica_groups=mesh['dp'=8,'ctx'=32] {'ctx'}, dimensions={0} | all-to-all | bytes 229376 | tf_op jit(solution)/shard_map/all_to_all | solution.py:85
  23.2 2.0 %convolution_convert_fusion.1 = bf16[512,512]{1,0:T(8,128)(2,1)} fusion(bf16[512,112]{1,0:T(8,128)(2,1)S(1)} %bitcast.200, bf16[112,512]{1,0:T(8,128)(2,1)} %param.11), kind=kOutput, calls=%fused_computation.38 | convolution fusion | flops 58982400 | bytes 753664 | tf_op jit(solution)/shard_map/dot_general | solution.py:117
  25.1 5.0 %all-to-all-start.1 = ((bf16[32,16,512]{2,1,0:T(8,128)(2,1)}), bf16[32,16,512]{2,1,0:T(8,128)(2,1)S(1)}, u32[]{:S(2)}, u32[]{:S(2)}) async-start(bf16[32,16,512]{2,1,0:T(8,128)(2,1)} %bitcast.2), calls=%async_computation.1 | async-start | bytes 1048576 | tf_op jit(solution)/shard_map/all_to_all | solution.py:85
  30.1 0.7 all-gather.2.cloned.1.call-update
  30.9 9.8 %all-to-all-done.1 = bf16[32,16,512]{2,1,0:T(8,128)(2,1)S(1)} async-done(((bf16[32,16,512]{2,1,0:T(8,128)(2,1)}), bf16[32,16,512]{2,1,0:T(8,128)(2,1)S(1)}, u32[]{:S(2)}, u32[]{:S(2)}) %all-to-all-start.1) | async-done | bytes 524320 | tf_op jit(solution)/shard_map/all_to_all | solution.py:85
  40.8 0.9 broadcast_in_dim.56
  41.6 5.1 %all-to-all-start.2 = ((bf16[32,16,512]{2,1,0:T(8,128)(2,1)}), bf16[32,16,512]{2,1,0:T(8,128)(2,1)S(1)}, u32[]{:S(2)}, u32[]{:S(2)}) async-start(bf16[32,16,512]{2,1,0:T(8,128)(2,1)} %broadcast_in_dim.56), calls=%async_computation.2 | async-start | bytes 1048576 | tf_op jit(solution)/shard_map/all_to_all | solution.py:85
  46.7 2.1 %fusion.86 = (bf16[34,7,8,128]{3,2,1,0:T(8,128)(2,1)S(1)}, bf16[34,7,8,128]{3,2,1,0:T(8,128)(2,1)}) fusion(bf16[16,1792]{1,0:T(8,128)(2,1)} %bitcast.211, bf16[256,1792]{1,0:T(8,128)(2,1)} %bitcast.208), kind=kLoop, calls=%fused_computation.104 | loop fusion | flops 1949696 | bytes 1949696
  48.8 1.0 fusion.85
  50.2 8.3 %all-to-all-done.2 = bf16[32,16,512]{2,1,0:T(8,128)(2,1)S(1)} async-done(((bf16[32,16,512]{2,1,0:T(8,128)(2,1)}), bf16[32,16,512]{2,1,0:T(8,128)(2,1)S(1)}, u32[]{:S(2)}, u32[]{:S(2)}) %all-to-all-start.2) | async-done | bytes 524320 | tf_op jit(solution)/shard_map/all_to_all | solution.py:85
  58.5 4.7 %fusion.135 = (f32[7,272]{1,0:T(8,128)S(1)}, f32[7,272,768]{2,1,0:T(8,128)}) fusion(pred[272,768]{1,0:T(8,128)(4,1)S(1)} %fusion.54, bf16[768,128,1]{1,0,2:T(8,128)(2,1)S(1)} %fusion.108, bf16[34,7,8,128]{3,2,1,0:T(8,128)(2,1)S(1)} %get-tuple-element.37), kind=kOutput, calls=%fused_computation.146 | convolution fusion | flops 380191488 | bytes 6749632 | tf_op jit(solution)/shard_map/sub | solution.py:48
  63.2 4.4 %fusion.44 = bf16[768,128]{0,1:T(8,128)(2,1)} fusion(bf16[34,7,8,128]{3,2,1,0:T(8,128)(2,1)S(1)} %get-tuple-element.35, f32[7,272,768]{2,1,0:T(8,128)} %get-tuple-element.42, f32[7,272]{1,0:T(8,128)S(1)} %get-tuple-element.41), kind=kOutput, calls=%fused_computation.48 | convolution fusion | flops 377266176 | bytes 6540736 | tf_op jit(solution)/shard_map/jrc,rjd->cd/dot_general | solution.py:57
  67.6 1.1 fusion.2
  68.7 1.1 fusion.4
  69.8 1.3 fusion.48
  71.1 5.7 %fusion.126 = (f32[7,272]{1,0:T(8,128)S(1)}, f32[7,272,768]{2,1,0:T(8,128)}) fusion(pred[272,768]{1,0:T(8,128)(4,1)} %copy-done.26, bf16[34,7,8,128]{3,2,1,0:T(8,128)(2,1)} %get-tuple-element.38, bf16[512,512]{1,0:T(8,128)(2,1)S(1)} %bitcast.194, bf16[256,512]{1,0:T(8,128)(2,1)} %bitcast.201), kind=kOutput, calls=%fused_computation.145 | convolution fusion | flops 380584704 | bytes 7339456 | tf_op jit(solution)/shard_map/sub | solution.py:48
  76.8 4.1 %fusion.5 = (f32[7,272]{1,0:T(8,128)S(1)}, f32[768,272,7]{0,1,2:T(8,128)S(1)}) fusion(f32[7,272,768]{2,1,0:T(8,128)} %get-tuple-element.40, f32[7,272]{1,0:T(8,128)S(1)} %get-tuple-element.39, bf16[34,7,8,128]{3,2,1,0:T(8,128)(2,1)} %get-tuple-element.36, bf16[512,512]{1,0:T(8,128)(2,1)S(1)} %bitcast.195, bf16[256,512]{1,0:T(8,128)(2,1)} %bitcast.202), kind=kOutput, calls=%fused_computation.9 | convolution fusion | flops 379119744 | bytes 12987264 | tf_op jit(solution)/shard_map/rjd,cd->jrc/dot_general | solution.py:59
  81.0 0.7 copy-done.3
  81.7 1.0 fusion.7
  82.7 0.7 fusion.47
  83.4 1.0 fusion.41
  84.4 0.7 copy-done.18
  85.1 0.8 fusion.51
  86.0 2.0 %copy.59 = bf16[512,512]{1,0:T(8,128)(2,1)} copy(bf16[512,512]{0,1:T(8,128)(2,1)} %fusion.51) | data formatting | bytes 1048576 | tf_op jit(solution)/shard_map/slice | solution.py:80
  88.0 5.4 %all-to-all-start.3 = ((bf16[32,16,512]{2,1,0:T(8,128)(2,1)}), bf16[32,16,512]{2,1,0:T(8,128)(2,1)}, u32[]{:S(2)}, u32[]{:S(2)}) async-start(bf16[32,16,512]{2,1,0:T(8,128)(2,1)} %bitcast.199), calls=%async_computation.3 | async-start | bytes 1048576 | tf_op jit(solution)/shard_map/all_to_all | solution.py:85
  93.4 3.8 %fusion.36 = bf16[7,34,8,128]{3,2,1,0:T(8,128)(2,1)S(1)} fusion(bf16[512,512]{1,0:T(8,128)(2,1)S(1)} %bitcast.196, bf16[256,512]{1,0:T(8,128)(2,1)} %bitcast.203, f32[7,272,768]{2,1,0:T(8,128)} %get-tuple-element.40, f32[7,272]{1,0:T(8,128)S(1)} %get-tuple-element.39), kind=kOutput, calls=%fused_computation.44 | convolution fusion | flops 377903104 | bytes 7130560 | tf_op jit(solution)/shard_map/jrc,cd->rjd/dot_general | solution.py:52
  97.3 0.9 fusion.40
  98.3 0.8 bitcast_dynamic-update-slice_fusion.1
  99.1 1.7 %fusion.39 = bf16[7,34,8,128]{3,2,1,0:T(8,128)(2,1)} fusion(bf16[768,128,1]{1,0,2:T(8,128)(2,1)S(1)} %copy-done.21, bf16[7,272,768]{2,1,0:T(8,128)(2,1)S(1)} %fusion.4), kind=kOutput, calls=%fused_computation.45 | convolution fusion | flops 374829056 | bytes 3608576 | tf_op jit(solution)/shard_map/jrc,cd->rjd/dot_general | solution.py:63
  100.8 3.7 %fusion.33 = bf16[7,34,8,128]{3,2,1,0:T(8,128)(2,1)S(1)} fusion(bf16[512,512]{1,0:T(8,128)(2,1)S(1)} %bitcast.198, bf16[256,512]{1,0:T(8,128)(2,1)S(1)} %bitcast.207, f32[7,272,768]{2,1,0:T(8,128)} %get-tuple-element.42, f32[7,272]{1,0:T(8,128)S(1)} %get-tuple-element.41), kind=kOutput, calls=%fused_computation.43 | convolution fusion | flops 377903104 | bytes 7130560 | tf_op jit(solution)/shard_map/jrc,cd->rjd/dot_general | solution.py:52
  104.7 1.0 copy-done.5
  105.7 1.0 slice_bitcast_fusion.1
  106.7 1.1 reduce_sum.65
  107.8 0.8 broadcast_in_dim.65
  108.6 7.5 %all-to-all-start.4 = ((bf16[32,16,512]{2,1,0:T(8,128)(2,1)}), bf16[32,16,512]{2,1,0:T(8,128)(2,1)S(1)}, u32[]{:S(2)}, u32[]{:S(2)}) async-start(bf16[32,16,512]{2,1,0:T(8,128)(2,1)} %broadcast_in_dim.65), calls=%async_computation.4 | async-start | bytes 1048576 | tf_op jit(solution)/shard_map/all_to_all | solution.py:85
  116.2 1.0 slice_bitcast_fusion
  117.2 9.4 %all-to-all-done.4 = bf16[32,16,512]{2,1,0:T(8,128)(2,1)S(1)} async-done(((bf16[32,16,512]{2,1,0:T(8,128)(2,1)}), bf16[32,16,512]{2,1,0:T(8,128)(2,1)S(1)}, u32[]{:S(2)}, u32[]{:S(2)}) %all-to-all-start.4) | async-done | bytes 524320 | tf_op jit(solution)/shard_map/all_to_all | solution.py:85
  126.9 2.1 %collective-permute-start = (bf16[112,512]{1,0:T(8,128)(2,1)S(1)}, bf16[112,512]{1,0:T(8,128)(2,1)S(1)}, u32[]{:S(2)}, u32[]{:S(2)}) collective-permute-start(bf16[112,512]{1,0:T(8,128)(2,1)S(1)} %fusion.50), channel_id=1, source_target_pairs={{0,32},{32,0},{64,96},{96,64},{128,160},{160,128},{192,224},{224,1... | collective-permute-start | bytes 344072 | tf_op jit(solution)/shard_map/ppermute | solution.py:102
  129.0 1.4 slice_bitcast_fusion.3
  130.4 2.2 %collective-permute-done = bf16[112,512]{1,0:T(8,128)(2,1)S(1)} collective-permute-done((bf16[112,512]{1,0:T(8,128)(2,1)S(1)}, bf16[112,512]{1,0:T(8,128)(2,1)S(1)}, u32[]{:S(2)}, u32[]{:S(2)}) %collective-permute-start) | collective-permute-done | bytes 114720 | tf_op jit(solution)/shard_map/ppermute | solution.py:102
  132.7 4.6 %collective-permute-start.1 = (bf16[112,512]{1,0:T(8,128)(2,1)S(1)}, bf16[112,512]{1,0:T(8,128)(2,1)S(1)}, u32[]{:S(2)}, u32[]{:S(2)}) collective-permute-start(bf16[112,512]{1,0:T(8,128)(2,1)S(1)} %add_convert_fusion.1), channel_id=1, source_target_pairs={{0,96},{32,64},{64,32},{96,0},{128,224},{160,192},{192,160},{224,1... | collective-permute-start | bytes 344072 | tf_op jit(solution)/shard_map/ppermute | solution.py:102
  137.9 2.3 %collective-permute-done.1 = bf16[112,512]{1,0:T(8,128)(2,1)S(1)} collective-permute-done((bf16[112,512]{1,0:T(8,128)(2,1)S(1)}, bf16[112,512]{1,0:T(8,128)(2,1)S(1)}, u32[]{:S(2)}, u32[]{:S(2)}) %collective-permute-start.1) | collective-permute-done | bytes 114720 | tf_op jit(solution)/shard_map/ppermute | solution.py:102
  140.3 5.2 %collective-permute-start.2 = (bf16[112,512]{1,0:T(8,128)(2,1)S(1)}, bf16[112,512]{1,0:T(8,128)(2,1)S(1)}, u32[]{:S(2)}, u32[]{:S(2)}) collective-permute-start(bf16[112,512]{1,0:T(8,128)(2,1)S(1)} %add_convert_fusion), channel_id=1, source_target_pairs={{0,224},{32,192},{64,160},{96,128},{128,96},{160,64},{192,32},{224... | collective-permute-start | bytes 344072 | tf_op jit(solution)/shard_map/ppermute | solution.py:102
  145.5 0.8 copy.60
  146.3 4.3 %collective-permute-done.2 = bf16[112,512]{1,0:T(8,128)(2,1)S(1)} collective-permute-done((bf16[112,512]{1,0:T(8,128)(2,1)S(1)}, bf16[112,512]{1,0:T(8,128)(2,1)S(1)}, u32[]{:S(2)}, u32[]{:S(2)}) %collective-permute-start.2) | collective-permute-done | bytes 114720 | tf_op jit(solution)/shard_map/ppermute | solution.py:102
  150.6 0.7 convert_add_fusion
  151.3 3.8 %fusion.10 = bf16[1,16,3584]{2,1,0:T(8,128)(2,1)} fusion(bf16[16,512]{1,0:T(8,128)(2,1)S(1)} %reduce_sum.65, bf16[3584,512]{1,0:T(8,128)(2,1)} %all-gather.2.cloned.1.call-done), kind=kOutput, calls=%fused_computation.19 | convolution fusion | flops 58777600 | bytes 3801088 | tf_op jit(solution)/shard_map/dot_general | solution.py:126
  (73 shorter events, 2.6 us)
Async XLA Ops:
  7.2 41.6 %copy-start.27 = (bf16[1,16,1792]{2,1,0:T(8,128)(2,1)S(1)}, bf16[1,16,1792]{2,1,0:T(8,128)(2,1)}, u32[]{:S(2)}) copy-start(bf16[1,16,1792]{2,1,0:T(8,128)(2,1)} %param.13) | copy-start | bytes 172036
  7.2 41.6 %copy-start.11 = (bf16[1,256,1792]{2,1,0:T(8,128)(2,1)S(1)}, bf16[1,256,1792]{2,1,0:T(8,128)(2,1)}, u32[]{:S(2)}) copy-start(bf16[1,256,1792]{2,1,0:T(8,128)(2,1)} %param.12) | copy-start | bytes 2752516
  7.2 51.3 %copy-start.9 = (bf16[1,256,512]{2,1,0:T(8,128)(2,1)S(1)}, bf16[1,256,512]{2,1,0:T(8,128)(2,1)}, u32[]{:S(2)}) copy-start(bf16[1,256,512]{2,1,0:T(8,128)(2,1)} %param.8) | copy-start | bytes 786436
  22.5 0.7 copy-start.7
  25.1 15.6 %all-to-all-start.1 = ((bf16[32,16,512]{2,1,0:T(8,128)(2,1)}), bf16[32,16,512]{2,1,0:T(8,128)(2,1)S(1)}, u32[]{:S(2)}, u32[]{:S(2)}) async-start(bf16[32,16,512]{2,1,0:T(8,128)(2,1)} %bitcast.2), calls=%async_computation.1 | async-start | bytes 1048576 | tf_op jit(solution)/shard_map/all_to_all | solution.py:85
  30.1 121.2 %all-gather.2.cloned.1.call-start = ((), (), s32[]{:S(2)}) async-start(), calls=%async_computation.5 | async-start | bytes 3784704 | tf_op jit(solution)/shard_map/all_gather | solution.py:114
  41.6 16.8 %all-to-all-start.2 = ((bf16[32,16,512]{2,1,0:T(8,128)(2,1)}), bf16[32,16,512]{2,1,0:T(8,128)(2,1)S(1)}, u32[]{:S(2)}, u32[]{:S(2)}) async-start(bf16[32,16,512]{2,1,0:T(8,128)(2,1)} %broadcast_in_dim.56), calls=%async_computation.2 | async-start | bytes 1048576 | tf_op jit(solution)/shard_map/all_to_all | solution.py:85
  48.8 14.4 %copy-start.24 = (bf16[34,7,8,128]{3,2,1,0:T(8,128)(2,1)}, bf16[34,7,8,128]{3,2,1,0:T(8,128)(2,1)S(1)}, u32[]{:S(2)}) copy-start(bf16[34,7,8,128]{3,2,1,0:T(8,128)(2,1)S(1)} %get-tuple-element.37) | copy-start | bytes 1462276
  50.2 17.4 %copy-start.26 = (pred[272,768]{1,0:T(8,128)(4,1)}, pred[272,768]{1,0:T(8,128)(4,1)S(1)}, u32[]{:S(2)}) copy-start(pred[272,768]{1,0:T(8,128)(4,1)S(1)} %fusion.54) | copy-start | bytes 626692
  58.5 9.1 %copy-start.20 = (bf16[768,128,1]{1,0,2:T(8,128)(2,1)}, bf16[768,128,1]{1,0,2:T(8,128)(2,1)S(1)}, u32[]{:S(2)}) copy-start(bf16[768,128,1]{1,0,2:T(8,128)(2,1)S(1)} %fusion.108) | copy-start | bytes 589828
  63.2 4.4 %copy-start.2 = (f32[7,272,768]{2,1,0:T(8,128)S(1)}, f32[7,272,768]{2,1,0:T(8,128)}, u32[]{:S(2)}) copy-start(f32[7,272,768]{2,1,0:T(8,128)} %get-tuple-element.42) | copy-start | bytes 17547268
  68.7 1.1 copy-start.25
  76.8 4.8 %copy-start.3 = (f32[7,272,768]{2,1,0:T(8,128)S(1)}, f32[7,272,768]{2,1,0:T(8,128)}, u32[]{:S(2)}) copy-start(f32[7,272,768]{2,1,0:T(8,128)} %get-tuple-element.40) | copy-start | bytes 17547268
  81.7 1.0 copy-start.22
  81.7 1.7 %copy-start.23 = (bf16[34,7,8,128]{3,2,1,0:T(8,128)(2,1)S(1)}, bf16[34,7,8,128]{3,2,1,0:T(8,128)(2,1)}, u32[]{:S(2)}) copy-start(bf16[34,7,8,128]{3,2,1,0:T(8,128)(2,1)} %get-tuple-element.36) | copy-start | bytes 1462276
  82.7 1.7 %copy-start = (bf16[7,272,768]{2,1,0:T(8,128)(2,1)}, bf16[7,272,768]{2,1,0:T(8,128)(2,1)S(1)}, u32[]{:S(2)}) copy-start(bf16[7,272,768]{2,1,0:T(8,128)(2,1)S(1)} %fusion.7) | copy-start | bytes 8773636
  83.4 1.0 copy-start.16
  83.4 1.7 %copy-start.12 = (bf16[768,128]{0,1:T(8,128)(2,1)S(1)}, bf16[768,128]{0,1:T(8,128)(2,1)}, u32[]{:S(2)}) copy-start(bf16[768,128]{0,1:T(8,128)(2,1)} %fusion.44) | copy-start | bytes 589828
  83.4 1.7 %copy-start.14 = (bf16[768,128]{0,1:T(8,128)(2,1)S(1)}, bf16[768,128]{0,1:T(8,128)(2,1)}, u32[]{:S(2)}) copy-start(bf16[768,128]{0,1:T(8,128)(2,1)} %fusion.48) | copy-start | bytes 589828
  84.4 0.7 copy-start.18
  88.0 18.7 %all-to-all-start.3 = ((bf16[32,16,512]{2,1,0:T(8,128)(2,1)}), bf16[32,16,512]{2,1,0:T(8,128)(2,1)}, u32[]{:S(2)}, u32[]{:S(2)}) async-start(bf16[32,16,512]{2,1,0:T(8,128)(2,1)} %bitcast.199), calls=%async_computation.3 | async-start | bytes 1048576 | tf_op jit(solution)/shard_map/all_to_all | solution.py:85
  93.4 3.9 %copy-start.1 = (bf16[7,272,768]{2,1,0:T(8,128)(2,1)S(1)}, bf16[7,272,768]{2,1,0:T(8,128)(2,1)}, u32[]{:S(2)}) copy-start(bf16[7,272,768]{2,1,0:T(8,128)(2,1)} %copy-done) | copy-start | bytes 8773636
  93.4 3.9 %copy-start.10 = (bf16[1,256,512]{2,1,0:T(8,128)(2,1)S(1)}, bf16[1,256,512]{2,1,0:T(8,128)(2,1)}, u32[]{:S(2)}) copy-start(bf16[1,256,512]{2,1,0:T(8,128)(2,1)} %param.8) | copy-start | bytes 786436
  97.3 1.9 %copy-start.21 = (bf16[768,128,1]{1,0,2:T(8,128)(2,1)S(1)}, bf16[768,128,1]{1,0,2:T(8,128)(2,1)}, u32[]{:S(2)}) copy-start(bf16[768,128,1]{1,0,2:T(8,128)(2,1)} %copy-done.20) | copy-start | bytes 589828
  100.8 15.3 %copy-start.4 = (bf16[272,1792]{1,0:T(8,128)(2,1)S(1)}, bf16[272,1792]{1,0:T(8,128)(2,1)}, u32[]{:S(2)}) copy-start(bf16[272,1792]{1,0:T(8,128)(2,1)} %bitcast_dynamic-update-slice_fusion.1) | copy-start | bytes 2924548
  100.8 15.3 %copy-start.6 = (bf16[7,34,8,128]{3,2,1,0:T(8,128)(2,1)S(1)}, bf16[7,34,8,128]{3,2,1,0:T(8,128)(2,1)}, u32[]{:S(2)}) copy-start(bf16[7,34,8,128]{3,2,1,0:T(8,128)(2,1)} %fusion.39) | copy-start | bytes 1462276
  104.6 22.1 %copy-start.8 = (bf16[32,16,112]{2,1,0:T(8,128)(2,1)S(1)}, bf16[32,16,112]{2,1,0:T(8,128)(2,1)}, u32[]{:S(2)}) copy-start(bf16[32,16,112]{2,1,0:T(8,128)(2,1)} %copy-done.7) | copy-start | bytes 344068
  104.6 40.9 %copy-start.13 = (bf16[768,128]{0,1:T(8,128)(2,1)S(1)}, bf16[768,128]{0,1:T(8,128)(2,1)}, u32[]{:S(2)}) copy-start(bf16[768,128]{0,1:T(8,128)(2,1)} %fusion.44) | copy-start | bytes 589828
  104.6 40.9 %copy-start.15 = (bf16[768,128]{0,1:T(8,128)(2,1)S(1)}, bf16[768,128]{0,1:T(8,128)(2,1)}, u32[]{:S(2)}) copy-start(bf16[768,128]{0,1:T(8,128)(2,1)} %fusion.48) | copy-start | bytes 589828
  104.6 40.9 %copy-start.17 = (bf16[768,128]{0,1:T(8,128)(2,1)S(1)}, bf16[768,128]{0,1:T(8,128)(2,1)}, u32[]{:S(2)}) copy-start(bf16[768,128]{0,1:T(8,128)(2,1)} %copy-done.16) | copy-start | bytes 589828
  104.6 40.9 %copy-start.19 = (bf16[768,128]{0,1:T(8,128)(2,1)S(1)}, bf16[768,128]{0,1:T(8,128)(2,1)}, u32[]{:S(2)}) copy-start(bf16[768,128]{0,1:T(8,128)(2,1)} %copy-done.18) | copy-start | bytes 589828
  104.7 1.0 copy-start.5
  108.6 18.0 %all-to-all-start.4 = ((bf16[32,16,512]{2,1,0:T(8,128)(2,1)}), bf16[32,16,512]{2,1,0:T(8,128)(2,1)S(1)}, u32[]{:S(2)}, u32[]{:S(2)}) async-start(bf16[32,16,512]{2,1,0:T(8,128)(2,1)} %broadcast_in_dim.65), calls=%async_computation.4 | async-start | bytes 1048576 | tf_op jit(solution)/shard_map/all_to_all | solution.py:85
  126.9 5.7 %collective-permute-start = (bf16[112,512]{1,0:T(8,128)(2,1)S(1)}, bf16[112,512]{1,0:T(8,128)(2,1)S(1)}, u32[]{:S(2)}, u32[]{:S(2)}) collective-permute-start(bf16[112,512]{1,0:T(8,128)(2,1)S(1)} %fusion.50), channel_id=1, source_target_pairs={{0,32},{32,0},{64,96},{96,64},{128,160},{160,128},{192,224},{224,1... | collective-permute-start | bytes 344072 | tf_op jit(solution)/shard_map/ppermute | solution.py:102
  132.7 7.6 %collective-permute-start.1 = (bf16[112,512]{1,0:T(8,128)(2,1)S(1)}, bf16[112,512]{1,0:T(8,128)(2,1)S(1)}, u32[]{:S(2)}, u32[]{:S(2)}) collective-permute-start(bf16[112,512]{1,0:T(8,128)(2,1)S(1)} %add_convert_fusion.1), channel_id=1, source_target_pairs={{0,96},{32,64},{64,32},{96,0},{128,224},{160,192},{192,160},{224,1... | collective-permute-start | bytes 344072 | tf_op jit(solution)/shard_map/ppermute | solution.py:102
  140.3 10.3 %collective-permute-start.2 = (bf16[112,512]{1,0:T(8,128)(2,1)S(1)}, bf16[112,512]{1,0:T(8,128)(2,1)S(1)}, u32[]{:S(2)}, u32[]{:S(2)}) collective-permute-start(bf16[112,512]{1,0:T(8,128)(2,1)S(1)} %add_convert_fusion), channel_id=1, source_target_pairs={{0,224},{32,192},{64,160},{96,128},{128,96},{160,64},{192,32},{224... | collective-permute-start | bytes 344072 | tf_op jit(solution)/shard_map/ppermute | solution.py:102
Sparse Core Ops, SparseCore 0:
  33.5 55.4 all-gather.1

commit v2 on v1

v2 whole, which is shorter than its diff:
```python
import jax
import jax.numpy as jnp
from jax import lax
from jax.experimental import pallas as pl
from jax.experimental.pallas import tpu as pltpu
from jax.sharding import PartitionSpec as P

KVH = 2
HD = 128
GROUP = 7
MASKED = -1e30
LOG2E = 1.4426950408889634
FACTOR = HD ** (-0.5)


def dot_nt(left, right):
    return lax.dot_general(
        left, right, (((1,), (1,)), ((), ())), preferred_element_type=jnp.float32
    )


def dot_nn(left, right):
    return jnp.dot(left, right, preferred_element_type=jnp.float32)


def head_rows(tokens_ref, beacons_ref, group, head):
    if head < GROUP:
        start = (group * GROUP + head) * HD
        return tokens_ref[:, start : start + HD]
    parts = []
    for each in range(GROUP):
        start = (group * GROUP + each) * HD
        parts.append(beacons_ref[:, start : start + HD])
    rows = beacons_ref.shape[0]
    parts.append(jnp.zeros((HD - GROUP * rows, HD), beacons_ref.dtype))
    return jnp.concatenate(parts, 0)


def token_bias(span):
    col = lax.broadcasted_iota(jnp.int32, (span, span), 0)
    row = lax.broadcasted_iota(jnp.int32, (span, span), 1)
    return jnp.where(col <= row, 0.0, MASKED).astype(jnp.float32)


def prefix_bias(total, width, start, rank_rows):
    col = lax.broadcasted_iota(jnp.int32, (total, width), 0)
    limit = start
    if rank_rows is not None:
        lane = lax.broadcasted_iota(jnp.int32, (total, width), 1)
        limit = start + 1 + (lane & (rank_rows - 1))
    return jnp.where(col < limit, 0.0, MASKED).astype(jnp.float32)


def token_stats_kernel(q_ref, bq_ref, kv_ref, c_ref, bc_ref, stats_ref, bias_ref):
    span = q_ref.shape[0]
    bias_ref[...] = token_bias(span)
    for group in range(KVH):
        keys = kv_ref[:, group * HD : (group + 1) * HD]
        vals = kv_ref[:, (KVH + group) * HD : (KVH + group + 1) * HD]
        for head in range(GROUP + 1):
            query = head_rows(q_ref, bq_ref, group, head)
            cot = head_rows(c_ref, bc_ref, group, head)
            width = query.shape[0]
            scores = dot_nt(keys, query) * (FACTOR * LOG2E)
            if head < GROUP:
                scores = scores + bias_ref[...]
            top = jnp.max(scores, 0, keepdims=True)
            expo = jnp.exp2(scores - top)
            dweights = dot_nt(vals, cot)
            stats_ref[0, group, head : head + 1, :width] = top
            stats_ref[1, group, head : head + 1, :width] = jnp.sum(expo, 0, keepdims=True)
            stats_ref[2, group, head : head + 1, :width] = jnp.sum(
                expo * dweights, 0, keepdims=True
            )


def beacon_grad_kernel(
    pos_ref, q_ref, bq_ref, kv_ref, c_ref, bc_ref, stats_ref, contrib_ref, rows_ref, bias_ref, bbias_ref
):
    total = kv_ref.shape[0]
    span = q_ref.shape[0]
    count = bq_ref.shape[0]
    start = pos_ref[0] * count
    bias_ref[...] = prefix_bias(total, span, start, None)
    bbias_ref[...] = prefix_bias(total, HD, start, count)
    for group in range(KVH):
        keys = kv_ref[:, group * HD : (group + 1) * HD]
        vals = kv_ref[:, (KVH + group) * HD : (KVH + group + 1) * HD]
        key_grad = jnp.zeros((total, HD), jnp.float32)
        val_grad = jnp.zeros((total, HD), jnp.float32)
        for head in range(GROUP + 1):
            query = head_rows(q_ref, bq_ref, group, head)
            cot = head_rows(c_ref, bc_ref, group, head)
            width = query.shape[0]
            bias = bias_ref if head < GROUP else bbias_ref
            scores = dot_nt(keys, query) * (FACTOR * LOG2E) + bias[...]
            top_tok = stats_ref[0, group, head : head + 1, :width]
            sum_tok = stats_ref[1, group, head : head + 1, :width]
            cen_tok = stats_ref[2, group, head : head + 1, :width]
            top = jnp.maximum(jnp.max(scores, 0, keepdims=True), top_tok)
            shift = jnp.exp2(top_tok - top)
            expo = jnp.exp2(scores - top)
            dweights = dot_nt(vals, cot)
            total_sum = shift * sum_tok + jnp.sum(expo, 0, keepdims=True)
            inverse = 1.0 / total_sum
            centre = inverse * (
                shift * cen_tok + jnp.sum(expo * dweights, 0, keepdims=True)
            )
            probs = expo * inverse
            dscores = (probs * (dweights - centre)).astype(jnp.bfloat16)
            key_grad = key_grad + dot_nn(dscores, query)
            val_grad = val_grad + dot_nn(probs.astype(jnp.bfloat16), cot)
            rows_ref[0, group, head : head + 1, :width] = top + jnp.log(total_sum) * LOG2E
            rows_ref[1, group, head : head + 1, :width] = centre
        contrib_ref[:, group * HD : (group + 1) * HD] = (key_grad * FACTOR).astype(jnp.bfloat16)
        contrib_ref[:, (KVH + group) * HD : (KVH + group + 1) * HD] = val_grad.astype(jnp.bfloat16)


def rest_kernel(
    pos_ref, q_ref, bq_ref, bkv_ref, kv_ref, c_ref, bc_ref, rows_ref,
    out_ref, bout_ref, dq_ref, bdq_ref, dkv_ref, bias_ref, bbias_ref, tbias_ref,
):
    total = bkv_ref.shape[0]
    span = q_ref.shape[0]
    count = bq_ref.shape[0]
    start = pos_ref[0] * count
    bias_ref[...] = prefix_bias(total, span, start, None)
    bbias_ref[...] = prefix_bias(total, HD, start, count)
    tbias_ref[...] = token_bias(span)
    for group in range(KVH):
        key_cols = slice(group * HD, (group + 1) * HD)
        val_cols = slice((KVH + group) * HD, (KVH + group + 1) * HD)
        sides = []
        for ref in (bkv_ref, kv_ref):
            keys = ref[:, key_cols]
            vals = ref[:, val_cols]
            sides.append((keys, vals, keys.T, vals.T))
        key_grad = jnp.zeros((span, HD), jnp.float32)
        val_grad = jnp.zeros((span, HD), jnp.float32)
        for head in range(GROUP + 1):
            query = head_rows(q_ref, bq_ref, group, head)
            cot = head_rows(c_ref, bc_ref, group, head)
            width = query.shape[0]
            lse = rows_ref[0, group, head : head + 1, :width]
            centre = rows_ref[1, group, head : head + 1, :width]
            out = None
            dquery = None
            for side in range(2):
                keys, vals, keys_t, vals_t = sides[side]
                scores = dot_nt(keys, query) * (FACTOR * LOG2E) - lse
                if side == 0:
                    scores = scores + (bias_ref if head < GROUP else bbias_ref)[...]
                elif head < GROUP:
                    scores = scores + tbias_ref[...]
                probs = jnp.exp2(scores)
                dscores = (probs * (dot_nt(vals, cot) - centre)).astype(jnp.bfloat16)
                weights = probs.astype(jnp.bfloat16)
                out_part = dot_nn(vals_t, weights)
                dq_part = dot_nn(keys_t, dscores)
                out = out_part if out is None else out + out_part
                dquery = dq_part if dquery is None else dquery + dq_part
                if side == 1:
                    key_grad = key_grad + dot_nn(dscores, query)
                    val_grad = val_grad + dot_nn(weights, cot)
            out = out.T.astype(jnp.bfloat16)
            dquery = (dquery * FACTOR).T.astype(jnp.bfloat16)
            if head < GROUP:
                at = (group * GROUP + head) * HD
                out_ref[:, at : at + HD] = out
                dq_ref[:, at : at + HD] = dquery
            else:
                for each in range(GROUP):
                    at = (group * GROUP + each) * HD
                    bout_ref[:, at : at + HD] = out[each * count : (each + 1) * count]
                    bdq_ref[:, at : at + HD] = dquery[each * count : (each + 1) * count]
        dkv_ref[:, key_cols] = (key_grad * FACTOR).astype(jnp.bfloat16)
        dkv_ref[:, val_cols] = val_grad.astype(jnp.bfloat16)


VM = pl.BlockSpec(memory_space=pltpu.VMEM)
SM = pl.BlockSpec(memory_space=pltpu.SMEM)


def call(kernel, outs, scratch, specs, args, flops):
    return pl.pallas_call(
        kernel,
        out_shape=outs,
        in_specs=specs,
        out_specs=tuple(VM for _ in outs),
        scratch_shapes=scratch,
        compiler_params=pltpu.CompilerParams(vmem_limit_bytes=40 * 1024 * 1024),
        cost_estimate=pl.CostEstimate(
            flops=flops, bytes_accessed=4 * 1024 * 1024, transcendentals=0
        ),
    )(*args)


def token_stats(query, beacon_query, kv, cot, beacon_cot):
    span = query.shape[0]
    return call(
        token_stats_kernel,
        (jax.ShapeDtypeStruct((3, KVH, GROUP + 1, span), jnp.float32),),
        [pltpu.VMEM((span, span), jnp.float32)],
        [VM] * 5,
        (query, beacon_query, kv, cot, beacon_cot),
        4 * span * span * HD * KVH * (GROUP + 1),
    )[0]


def beacon_grads(pos, query, beacon_query, all_kv, cot, beacon_cot, stats):
    span = query.shape[0]
    total = all_kv.shape[0]
    return call(
        beacon_grad_kernel,
        (
            jax.ShapeDtypeStruct(all_kv.shape, jnp.bfloat16),
            jax.ShapeDtypeStruct((2, KVH, GROUP + 1, span), jnp.float32),
        ),
        [pltpu.VMEM((total, span), jnp.float32), pltpu.VMEM((total, HD), jnp.float32)],
        [SM] + [VM] * 6,
        (pos, query, beacon_query, all_kv, cot, beacon_cot, stats),
        8 * span * total * HD * KVH * (GROUP + 1),
    )


def rest(pos, query, beacon_query, all_kv, kv, cot, beacon_cot, rows):
    span = query.shape[0]
    total = all_kv.shape[0]
    like = lambda x: jax.ShapeDtypeStruct(x.shape, jnp.bfloat16)
    return call(
        rest_kernel,
        (like(query), like(beacon_query), like(query), like(beacon_query), like(kv)),
        [
            pltpu.VMEM((total, span), jnp.float32),
            pltpu.VMEM((total, HD), jnp.float32),
            pltpu.VMEM((span, span), jnp.float32),
        ],
        [SM] + [VM] * 7,
        (pos, query, beacon_query, all_kv, kv, cot, beacon_cot, rows),
        10 * span * (total + span) * HD * KVH * (GROUP + 1),
    )


def exchange(blocks):
    return lax.all_to_all(blocks, "ctx", 0, 0, tiled=True)


def reduce_blocks(blocks):
    return jnp.sum(exchange(blocks).astype(jnp.float32), 0).astype(jnp.bfloat16)


def gather_rows(rows, count):
    return exchange(jnp.broadcast_to(rows[None], (count,) + rows.shape)).reshape(-1, rows.shape[-1])


def sum_dp(part):
    size = lax.axis_size("dp")
    step = 1
    while step < size:
        sent = part.astype(jnp.bfloat16)
        pairs = [(i, i // (2 * step) * 2 * step + 2 * step - 1 - i % (2 * step)) for i in range(size)]
        part = sent.astype(jnp.float32) + lax.ppermute(sent, "dp", pairs).astype(jnp.float32)
        step *= 2
    return part


def shards(
    query, keys_values, beacon_query, beacon_hidden, beacon_weight, grad_tokens, grad_beacons
):
    pos = lax.axis_index("ctx").astype(jnp.int32).reshape(1)
    count = lax.axis_size("ctx")
    rows = beacon_hidden.shape[1]
    hidden_rows = beacon_hidden[0]
    full_weight = lax.all_gather(beacon_weight, "ctx", axis=0, tiled=True)
    stats = token_stats(
        query[0], beacon_query[0], keys_values[0], grad_tokens[0], grad_beacons[0]
    )
    hidden_cols = exchange(hidden_rows.reshape(rows, count, -1).transpose(1, 0, 2))
    hidden_cols = hidden_cols.reshape(rows * count, -1)
    part_kv = jnp.dot(hidden_cols, beacon_weight, preferred_element_type=jnp.float32)
    own_kv = reduce_blocks(part_kv.astype(jnp.bfloat16).reshape(count, rows, -1))
    all_kv = gather_rows(own_kv, count)
    contrib, row_stats = beacon_grads(
        pos, query[0], beacon_query[0], all_kv, grad_tokens[0], grad_beacons[0], stats
    )
    tokens_out, beacons_out, query_grad, beacon_qgrad, token_kvgrad = rest(
        pos, query[0], beacon_query[0], all_kv, keys_values[0], grad_tokens[0], grad_beacons[0], row_stats
    )
    own_grad = reduce_blocks(contrib.reshape(count, rows, -1))
    all_grad = gather_rows(own_grad, count)
    hidden_grad = lax.dot_general(
        own_grad, full_weight, (((1,), (1,)), ((), ())), preferred_element_type=jnp.float32
    ).astype(jnp.bfloat16)
    weight_part = lax.dot_general(
        hidden_cols, all_grad, (((0,), (0,)), ((), ())), preferred_element_type=jnp.float32
    )
    grad_weight = sum_dp(weight_part)
    return (
        tokens_out[None],
        beacons_out[None],
        query_grad[None],
        token_kvgrad[None],
        beacon_qgrad[None],
        hidden_grad[None],
        grad_weight,
    )


def solution(mesh):
    placed = (
        P("dp", "ctx", None),
        P("dp", "ctx", None),
        P("dp", "ctx", None),
        P("dp", "ctx", None),
        P("ctx", None),
        P("dp", "ctx", None),
        P("dp", "ctx", None),
    )
    return jax.shard_map(
        shards,
        mesh=mesh,
        in_specs=placed,
        out_specs=(
            P("dp", "ctx", None),
            P("dp", "ctx", None),
            P("dp", "ctx", None),
            P("dp", "ctx", None),
            P("dp", "ctx", None),
            P("dp", "ctx", None),
            P("ctx", None),
        ),
        check_vma=False,
    )
```

time: 163 us -> 140 us (0.86)
  blocking collectives: 14 us -> 61.2 us
  matrix products: 39.2 us -> 5.18 us
  Pallas kernels: 0 us -> 20.1 us
  waiting for transfers between devices: 37 us -> 17.4 us
  starting transfers between devices: 34.8 us -> 18.2 us
  local copies, waits for them, and re-layouts: 14 us -> 2.08 us
  other arithmetic: 8.46 us -> 0.95 us
    all_to_all x1 -> x4, blocking collectives: 14 us -> 61.2 us  [exchange(): return lax.all_to_all(blocks, 'ctx', 0, 0, tiled=True)]
    dot_general x10 -> x0, matrix products: 22.8 us -> none  [the longest x2 7.55 us: interval_pass(): jnp.einsum('jrc,cd->rjd', weights, v_group, preferred_element_type=jnp.fl...]
    pallas_call x0 -> x3, Pallas kernels: none -> 20.1 us  [call(): pl.pallas_call(kernel, out_shape=outs, in_specs=specs, out_specs=tuple((V...]
    all_to_all x4 -> x1, starting transfers between devices: 22.9 us -> 4.98 us  [exchange(): return lax.all_to_all(blocks, 'ctx', 0, 0, tiled=True)]
    all_to_all x4 -> x1, waiting for transfers between devices: 27.5 us -> 10.1 us  [exchange(): return lax.all_to_all(blocks, 'ctx', 0, 0, tiled=True)]
    sub x2 -> x0, matrix products: 10.4 us -> none  [interval_pass(): expo_terms = jnp.exp(scores - highest)]
    unnamed x59 -> x10, local copies, waits for them, and re-layouts: 4.84 us -> 0.02 us
    broadcast_in_dim x4 -> x0, local copies, waits for them, and re-layouts: 4.03 us -> none  [the longest x1 1.44 us: shards(): beacons_out[None]]
  transfers between devices with their start and end apart: 8 -> 5, of which waited for: 6 -> 3; matrix products, arithmetic and copies ran while one was open for 32% -> 3% of each run, Pallas kernels for 0% -> 14%
where the time goes in v2:
time: 140 us; the launch traced here: 139 us
  blocking collectives  61.2 us (44%)
  Pallas kernels  20.1 us (14%)
  starting transfers between devices  18.2 us (13%)
  waiting for transfers between devices  17.4 us (12%)
  between operations  14.2 us (10%)
  matrix products  5.18 us (4%)
  local copies, waits for them, and re-layouts  2.08 us (1%)
    all_to_all x4, blocking collectives, exchange(): return lax.all_to_all(blocks, 'ctx', 0, 0, tiled=True)  61.2 us
    pallas_call x3, Pallas kernels, call(): pl.pallas_call(kernel, out_shape=outs, in_specs=specs, out_specs=tuple((V...  20.1 us
    ppermute x3, starting transfers between devices, sum_dp(): lax.ppermute(sent, 'dp', pairs).astype(jnp.float32)  13.2 us
    all_to_all x1, waiting for transfers between devices, exchange(): return lax.all_to_all(blocks, 'ctx', 0, 0, tiled=True)  10.1 us
    ppermute x3, waiting for transfers between devices, sum_dp(): lax.ppermute(sent, 'dp', pairs).astype(jnp.float32)  6.62 us
    all_to_all x1, starting transfers between devices, exchange(): return lax.all_to_all(blocks, 'ctx', 0, 0, tiled=True)  4.98 us
    dot_general x1, matrix products, shards(): lax.dot_general(own_grad, full_weight, (((1,), (1,)), ((), ())), preferre...  3.75 us
  transfers between devices with their start and end apart: 5, of which 3 were waited for; matrix products, arithmetic and copies ran while one was open for 3% of the time, Pallas kernels for 14%

profile of v2, /device:TPU:2, one launch (start us, length us, event | category | flops | bytes accessed | tf_op | source)
XLA Modules:
  0.0 139.3 jit_solution(2425006860131337204)
XLA Ops:
  7.2 0.0 copy-start.4
  7.2 0.0 copy-start.1
  7.2 0.0 copy-start.3
  7.2 0.0 copy-start.2
  7.2 0.0 copy-start
  7.2 0.0 all-gather.2.cloned.1.call-start
  7.3 0.7 all-gather.2.cloned.1.call-update
  8.0 1.1 reshape_squeeze.3
  9.1 0.1 copy.17
  9.1 14.0 %all_to_all.25 = bf16[32,16,112]{2,1,0:T(8,128)(2,1)S(1)} all-to-all(bf16[32,16,112]{2,1,0:T(8,128)(2,1)S(1)} %copy.17), channel_id=1, replica_groups=mesh['dp'=8,'ctx'=32] {'ctx'}, dimensions={0} | all-to-all | bytes 229376 | tf_op jit(solution)/shard_map/all_to_all | solution.py:245
  23.2 1.2 convolution_convert_fusion.1
  24.3 16.1 %all_to_all.26 = bf16[32,16,512]{2,1,0:T(8,128)(2,1)S(1)} all-to-all(bf16[32,16,512]{2,1,0:T(8,128)(2,1)S(1)} %bitcast.49), channel_id=1, replica_groups=mesh['dp'=8,'ctx'=32] {'ctx'}, dimensions={0} | all-to-all | bytes 1048576 | tf_op jit(solution)/shard_map/all_to_all | solution.py:245
  40.4 0.1 reduce_sum.24
  40.5 0.9 broadcast_in_dim.30
  41.3 5.0 %all-to-all-start.2 = ((bf16[32,16,512]{2,1,0:T(8,128)(2,1)}), bf16[32,16,512]{2,1,0:T(8,128)(2,1)S(1)}, u32[]{:S(2)}, u32[]{:S(2)}) async-start(bf16[32,16,512]{2,1,0:T(8,128)(2,1)} %broadcast_in_dim.30), calls=%async_computation.2 | async-start | bytes 1048576 | tf_op jit(solution)/shard_map/all_to_all | solution.py:245
  46.3 0.0 copy-done.4
  46.3 0.0 copy-done.1
  46.3 0.0 copy-done.3
  46.4 0.0 copy-done.2
  46.4 0.0 copy-done
  46.4 1.6 %shard_map.126.stats_ref = f32[3,2,8,256]{3,2,1,0:T(8,128)S(1)} custom-call(bf16[256,1792]{1,0:T(8,128)(2,1)S(1)} %bitcast.32, bf16[16,1792]{1,0:T(8,128)(2,1)S(1)} %bitcast.43, bf16[256,512]{1,0:T(8,128)(2,1)S(1)} %bitcast.41, bf16[256,1792]{1,0:T(8,128)(2,1)S(1)} %bitcast.35, bf16[16,1792]{1,0:T(8,128)(2,1)S(1)} %bitcast.46), custom_call_target="tpu_custom_call" | custom-call | flops 536870912 | bytes 4194304 | tf_op jit(solution)/shard_map/pallas_call | solution.py:185
  47.9 10.1 %all-to-all-done.2 = bf16[32,16,512]{2,1,0:T(8,128)(2,1)S(1)} async-done(((bf16[32,16,512]{2,1,0:T(8,128)(2,1)}), bf16[32,16,512]{2,1,0:T(8,128)(2,1)S(1)}, u32[]{:S(2)}, u32[]{:S(2)}) %all-to-all-start.2) | async-done | bytes 524320 | tf_op jit(solution)/shard_map/all_to_all | solution.py:245
  58.0 8.9 %shard_map.127 = (bf16[512,512]{1,0:T(8,128)(2,1)S(1)}, f32[2,2,8,256]{3,2,1,0:T(8,128)S(1)}) custom-call(s32[1]{0:T(128)} %bitcast.pos_ref, bf16[256,1792]{1,0:T(8,128)(2,1)S(1)} %bitcast.33, bf16[16,1792]{1,0:T(8,128)(2,1)S(1)} %bitcast.44, bf16[512,512]{1,0:T(8,128)(2,1)S(1)} %bitcast.38, bf16[256,1792]{1,0:T(8,128)(2,1)S(1)} %bitcast.36, ...), custom_call_target="tpu_custom_call" | custom-call | flops 2147483648 | bytes 4194304 | tf_op jit(solution)/shard_map/pallas_call | solution.py:185
  66.9 15.9 %all_to_all.27 = bf16[32,16,512]{2,1,0:T(8,128)(2,1)S(1)} all-to-all(bf16[32,16,512]{2,1,0:T(8,128)(2,1)S(1)} %bitcast.40), channel_id=1, replica_groups=mesh['dp'=8,'ctx'=32] {'ctx'}, dimensions={0} | all-to-all | bytes 1048576 | tf_op jit(solution)/shard_map/all_to_all | solution.py:245
  82.7 0.1 reduce_sum.25
  82.8 0.1 broadcast_in_dim.37
  82.9 15.2 %all_to_all.28 = bf16[32,16,512]{2,1,0:T(8,128)(2,1)S(1)} all-to-all(bf16[32,16,512]{2,1,0:T(8,128)(2,1)S(1)} %broadcast_in_dim.37), channel_id=1, replica_groups=mesh['dp'=8,'ctx'=32] {'ctx'}, dimensions={0} | all-to-all | bytes 1048576 | tf_op jit(solution)/shard_map/all_to_all | solution.py:245
  98.1 0.3 fusion.2
  98.4 2.8 %collective-permute-start = (bf16[112,512]{1,0:T(8,128)(2,1)S(1)}, bf16[112,512]{1,0:T(8,128)(2,1)S(1)}, u32[]{:S(2)}, u32[]{:S(2)}) collective-permute-start(bf16[112,512]{1,0:T(8,128)(2,1)S(1)} %fusion.2), channel_id=1, source_target_pairs={{0,32},{32,0},{64,96},{96,64},{128,160},{160,128},{192,224},{224,1... | collective-permute-start | bytes 344072 | tf_op jit(solution)/shard_map/ppermute | solution.py:262
  101.2 3.7 %collective-permute-done = bf16[112,512]{1,0:T(8,128)(2,1)S(1)} collective-permute-done((bf16[112,512]{1,0:T(8,128)(2,1)S(1)}, bf16[112,512]{1,0:T(8,128)(2,1)S(1)}, u32[]{:S(2)}, u32[]{:S(2)}) %collective-permute-start) | collective-permute-done | bytes 114720 | tf_op jit(solution)/shard_map/ppermute | solution.py:262
  104.8 4.0 %collective-permute-start.1 = (bf16[112,512]{1,0:T(8,128)(2,1)S(1)}, bf16[112,512]{1,0:T(8,128)(2,1)S(1)}, u32[]{:S(2)}, u32[]{:S(2)}) collective-permute-start(bf16[112,512]{1,0:T(8,128)(2,1)S(1)} %add_convert_fusion.1), channel_id=1, source_target_pairs={{0,96},{32,64},{64,32},{96,0},{128,224},{160,192},{192,160},{224,1... | collective-permute-start | bytes 344072 | tf_op jit(solution)/shard_map/ppermute | solution.py:262
  108.9 3.0 %collective-permute-done.1 = bf16[112,512]{1,0:T(8,128)(2,1)S(1)} collective-permute-done((bf16[112,512]{1,0:T(8,128)(2,1)S(1)}, bf16[112,512]{1,0:T(8,128)(2,1)S(1)}, u32[]{:S(2)}, u32[]{:S(2)}) %collective-permute-start.1) | collective-permute-done | bytes 114720 | tf_op jit(solution)/shard_map/ppermute | solution.py:262
  111.9 6.4 %collective-permute-start.2 = (bf16[112,512]{1,0:T(8,128)(2,1)S(1)}, bf16[112,512]{1,0:T(8,128)(2,1)S(1)}, u32[]{:S(2)}, u32[]{:S(2)}) collective-permute-start(bf16[112,512]{1,0:T(8,128)(2,1)S(1)} %add_convert_fusion), channel_id=1, source_target_pairs={{0,224},{32,192},{64,160},{96,128},{128,96},{160,64},{192,32},{224... | collective-permute-start | bytes 344072 | tf_op jit(solution)/shard_map/ppermute | solution.py:262
  118.3 9.7 %shard_map.128 = (bf16[256,1792]{1,0:T(8,128)(2,1)}, bf16[16,1792]{1,0:T(8,128)(2,1)}, bf16[256,1792]{1,0:T(8,128)(2,1)}, bf16[16,1792]{1,0:T(8,128)(2,1)}, bf16[256,512]{1,0:T(8,128)(2,1)}) custom-call(s32[1]{0:T(128)} %bitcast.pos_ref, bf16[256,1792]{1,0:T(8,128)(2,1)S(1)} %bitcast.34, bf16[16,1792]{1,0:T(8,128)(2,1)S(1)} %bitcast.45, ...), custom_call_target="tpu_custom_call" | custom-call | flops 4026531840 | bytes 4194304 | tf_op jit(solution)/shard_map/pallas_call | solution.py:185
  128.0 0.0 collective-permute-done.2
  128.0 0.7 convert_add_fusion
  128.7 0.0 all-gather.2.cloned.1.call-done
  128.7 3.8 %fusion = bf16[1,16,3584]{2,1,0:T(8,128)(2,1)} fusion(bf16[16,512]{1,0:T(8,128)(2,1)S(1)} %reduce_sum.25, bf16[3584,512]{1,0:T(8,128)(2,1)} %all-gather.2.cloned.1.call-done), kind=kOutput, calls=%fused_computation.1 | convolution fusion | flops 58777600 | bytes 3801088 | tf_op jit(solution)/shard_map/dot_general | solution.py:291
  (2 shorter events, 0.1 us)
Async XLA Ops:
  7.2 39.2 %copy-start.4 = (bf16[1,16,1792]{2,1,0:T(8,128)(2,1)S(1)}, bf16[1,16,1792]{2,1,0:T(8,128)(2,1)}, u32[]{:S(2)}) copy-start(bf16[1,16,1792]{2,1,0:T(8,128)(2,1)} %param.13) | copy-start | bytes 172036
  7.2 39.2 %copy-start.1 = (bf16[1,256,1792]{2,1,0:T(8,128)(2,1)S(1)}, bf16[1,256,1792]{2,1,0:T(8,128)(2,1)}, u32[]{:S(2)}) copy-start(bf16[1,256,1792]{2,1,0:T(8,128)(2,1)} %param.12) | copy-start | bytes 2752516
  7.2 39.2 %copy-start.3 = (bf16[1,16,1792]{2,1,0:T(8,128)(2,1)S(1)}, bf16[1,16,1792]{2,1,0:T(8,128)(2,1)}, u32[]{:S(2)}) copy-start(bf16[1,16,1792]{2,1,0:T(8,128)(2,1)} %param.9) | copy-start | bytes 172036
  7.2 39.2 %copy-start.2 = (bf16[1,256,512]{2,1,0:T(8,128)(2,1)S(1)}, bf16[1,256,512]{2,1,0:T(8,128)(2,1)}, u32[]{:S(2)}) copy-start(bf16[1,256,512]{2,1,0:T(8,128)(2,1)} %param.8) | copy-start | bytes 786436
  7.2 39.2 %copy-start = (bf16[1,256,1792]{2,1,0:T(8,128)(2,1)S(1)}, bf16[1,256,1792]{2,1,0:T(8,128)(2,1)}, u32[]{:S(2)}) copy-start(bf16[1,256,1792]{2,1,0:T(8,128)(2,1)} %param.7) | copy-start | bytes 2752516
  7.2 121.5 %all-gather.2.cloned.1.call-start = ((), (), s32[]{:S(2)}) async-start(), calls=%async_computation.5 | async-start | bytes 3784704 | tf_op jit(solution)/shard_map/all_gather | solution.py:274
  41.3 16.7 %all-to-all-start.2 = ((bf16[32,16,512]{2,1,0:T(8,128)(2,1)}), bf16[32,16,512]{2,1,0:T(8,128)(2,1)S(1)}, u32[]{:S(2)}, u32[]{:S(2)}) async-start(bf16[32,16,512]{2,1,0:T(8,128)(2,1)} %broadcast_in_dim.30), calls=%async_computation.2 | async-start | bytes 1048576 | tf_op jit(solution)/shard_map/all_to_all | solution.py:245
  98.4 6.4 %collective-permute-start = (bf16[112,512]{1,0:T(8,128)(2,1)S(1)}, bf16[112,512]{1,0:T(8,128)(2,1)S(1)}, u32[]{:S(2)}, u32[]{:S(2)}) collective-permute-start(bf16[112,512]{1,0:T(8,128)(2,1)S(1)} %fusion.2), channel_id=1, source_target_pairs={{0,32},{32,0},{64,96},{96,64},{128,160},{160,128},{192,224},{224,1... | collective-permute-start | bytes 344072 | tf_op jit(solution)/shard_map/ppermute | solution.py:262
  104.8 7.0 %collective-permute-start.1 = (bf16[112,512]{1,0:T(8,128)(2,1)S(1)}, bf16[112,512]{1,0:T(8,128)(2,1)S(1)}, u32[]{:S(2)}, u32[]{:S(2)}) collective-permute-start(bf16[112,512]{1,0:T(8,128)(2,1)S(1)} %add_convert_fusion.1), channel_id=1, source_target_pairs={{0,96},{32,64},{64,32},{96,0},{128,224},{160,192},{192,160},{224,1... | collective-permute-start | bytes 344072 | tf_op jit(solution)/shard_map/ppermute | solution.py:262
  111.9 16.1 %collective-permute-start.2 = (bf16[112,512]{1,0:T(8,128)(2,1)S(1)}, bf16[112,512]{1,0:T(8,128)(2,1)S(1)}, u32[]{:S(2)}, u32[]{:S(2)}) collective-permute-start(bf16[112,512]{1,0:T(8,128)(2,1)S(1)} %add_convert_fusion), channel_id=1, source_target_pairs={{0,224},{32,192},{64,160},{96,128},{128,96},{160,64},{192,32},{224... | collective-permute-start | bytes 344072 | tf_op jit(solution)/shard_map/ppermute | solution.py:262
Sparse Core Ops, SparseCore 0:
  10.6 57.1 all-gather.1

commit v3 on v2

--- a/solution.py
+++ b/solution.py
@@ -283,14 +283,18 @@
     contrib, row_stats = beacon_grads(
         pos, query[0], beacon_query[0], all_kv, grad_tokens[0], grad_beacons[0], stats
     )
-    tokens_out, beacons_out, query_grad, beacon_qgrad, token_kvgrad = rest(
+    others = rest(
         pos, query[0], beacon_query[0], all_kv, keys_values[0], grad_tokens[0], grad_beacons[0], row_stats
     )
-    own_grad = reduce_blocks(contrib.reshape(count, rows, -1))
+    arrived = exchange(contrib.reshape(count, rows, -1))
+    arrived, others = lax.optimization_barrier((arrived, others))
+    tokens_out, beacons_out, query_grad, beacon_qgrad, token_kvgrad = others
+    own_grad = jnp.sum(arrived.astype(jnp.float32), 0).astype(jnp.bfloat16)
     all_grad = gather_rows(own_grad, count)
     hidden_grad = lax.dot_general(
         own_grad, full_weight, (((1,), (1,)), ((), ())), preferred_element_type=jnp.float32
     ).astype(jnp.bfloat16)
+    all_grad, hidden_grad = lax.optimization_barrier((all_grad, hidden_grad))
     weight_part = lax.dot_general(
         hidden_cols, all_grad, (((0,), (0,)), ((), ())), preferred_element_type=jnp.float32
     )

time: 140 us -> 134 us (0.957)
  blocking collectives: 61.2 us -> 30.1 us
  starting transfers between devices: 18.2 us -> 30.4 us
  waiting for transfers between devices: 17.4 us -> 29 us
    all_to_all x4 -> x2, blocking collectives: 61.2 us -> 30.1 us  [exchange(): return lax.all_to_all(blocks, 'ctx', 0, 0, tiled=True)]
    all_to_all x1 -> x3, starting transfers between devices: 4.98 us -> 17.1 us  [exchange(): return lax.all_to_all(blocks, 'ctx', 0, 0, tiled=True)]
    all_to_all x1 -> x3, waiting for transfers between devices: 10.1 us -> 17.6 us  [exchange(): return lax.all_to_all(blocks, 'ctx', 0, 0, tiled=True)]
    ppermute x3, waiting for transfers between devices: 6.62 us -> 10.7 us  [sum_dp(): lax.ppermute(sent, 'dp', pairs).astype(jnp.float32)]
  transfers between devices with their start and end apart: 5 -> 7, of which waited for: 3 -> 6; matrix products, arithmetic and copies ran while one was open for 3% -> 6% of each run, Pallas kernels for 14% -> 16%
where the time goes in v3:
time: 134 us
  starting transfers between devices  30.4 us (23%)
  blocking collectives  30.1 us (22%)
  waiting for transfers between devices  29 us (22%)
  Pallas kernels  20.9 us (16%)
  between operations  14.2 us (11%)
  matrix products  5.17 us (4%)
  local copies, waits for them, and re-layouts  2.88 us (2%)
    all_to_all x2, blocking collectives, exchange(): return lax.all_to_all(blocks, 'ctx', 0, 0, tiled=True)  30.1 us
    pallas_call x3, Pallas kernels, call(): pl.pallas_call(kernel, out_shape=outs, in_specs=specs, out_specs=tuple((V...  20.9 us
    all_to_all x3, waiting for transfers between devices, exchange(): return lax.all_to_all(blocks, 'ctx', 0, 0, tiled=True)  17.6 us
    all_to_all x3, starting transfers between devices, exchange(): return lax.all_to_all(blocks, 'ctx', 0, 0, tiled=True)  17.1 us
    ppermute x3, starting transfers between devices, sum_dp(): lax.ppermute(sent, 'dp', pairs).astype(jnp.float32)  13.2 us
    ppermute x3, waiting for transfers between devices, sum_dp(): lax.ppermute(sent, 'dp', pairs).astype(jnp.float32)  10.7 us
    dot_general x1, matrix products, shards(): lax.dot_general(own_grad, full_weight, (((1,), (1,)), ((), ())), preferre...  3.75 us
  transfers between devices with their start and end apart: 7, of which 6 were waited for; matrix products, arithmetic and copies ran while one was open for 6% of the time, Pallas kernels for 16%

profile of v3, /device:TPU:2, one launch (start us, length us, event | category | flops | bytes accessed | tf_op | source)
XLA Modules:
  0.0 133.6 jit_solution(13675055815616434589)
XLA Ops:
  7.2 0.0 copy-start
  7.2 0.0 copy-start.3
  7.2 0.0 copy-start.1
  7.2 0.0 copy-start.4
  7.2 0.0 copy-start.2
  7.2 0.0 all-gather.2.cloned.1.call-start
  7.3 0.7 all-gather.2.cloned.1.call-update
  8.0 1.1 reshape_squeeze.3
  9.1 0.1 copy.16
  9.1 14.0 %all_to_all.25 = bf16[32,16,112]{2,1,0:T(8,128)(2,1)S(1)} all-to-all(bf16[32,16,112]{2,1,0:T(8,128)(2,1)S(1)} %bitcast.48), channel_id=1, replica_groups=mesh['dp'=8,'ctx'=32] {'ctx'}, dimensions={0} | all-to-all | bytes 229376 | tf_op jit(solution)/shard_map/all_to_all | solution.py:245
  23.2 1.2 convolution_convert_fusion.1
  24.3 16.1 %all_to_all.26 = bf16[32,16,512]{2,1,0:T(8,128)(2,1)S(1)} all-to-all(bf16[32,16,512]{2,1,0:T(8,128)(2,1)S(1)} %bitcast.45), channel_id=1, replica_groups=mesh['dp'=8,'ctx'=32] {'ctx'}, dimensions={0} | all-to-all | bytes 1048576 | tf_op jit(solution)/shard_map/all_to_all | solution.py:245
  40.4 0.1 reduce_sum.24
  40.5 0.9 broadcast_in_dim.30
  41.3 5.0 %all-to-all-start.2 = ((bf16[32,16,512]{2,1,0:T(8,128)(2,1)}), bf16[32,16,512]{2,1,0:T(8,128)(2,1)S(1)}, u32[]{:S(2)}, u32[]{:S(2)}) async-start(bf16[32,16,512]{2,1,0:T(8,128)(2,1)} %broadcast_in_dim.30), calls=%async_computation.2 | async-start | bytes 1048576 | tf_op jit(solution)/shard_map/all_to_all | solution.py:245
  46.3 0.0 copy-done
  46.3 0.0 copy-done.3
  46.3 0.0 copy-done.1
  46.4 0.0 copy-done.4
  46.4 0.0 copy-done.2
  46.4 1.6 %shard_map.126.stats_ref = f32[3,2,8,256]{3,2,1,0:T(8,128)S(1)} custom-call(bf16[256,1792]{1,0:T(8,128)(2,1)S(1)} %bitcast.28, bf16[16,1792]{1,0:T(8,128)(2,1)S(1)} %bitcast.38, bf16[256,512]{1,0:T(8,128)(2,1)S(1)} %bitcast.36, bf16[256,1792]{1,0:T(8,128)(2,1)S(1)} %bitcast.31, bf16[16,1792]{1,0:T(8,128)(2,1)S(1)} %bitcast.41), custom_call_target="tpu_custom_call" | custom-call | flops 536870912 | bytes 4194304 | tf_op jit(solution)/shard_map/pallas_call | solution.py:185
  47.9 10.1 %all-to-all-done.2 = bf16[32,16,512]{2,1,0:T(8,128)(2,1)S(1)} async-done(((bf16[32,16,512]{2,1,0:T(8,128)(2,1)}), bf16[32,16,512]{2,1,0:T(8,128)(2,1)S(1)}, u32[]{:S(2)}, u32[]{:S(2)}) %all-to-all-start.2) | async-done | bytes 524320 | tf_op jit(solution)/shard_map/all_to_all | solution.py:245
  58.0 9.6 %shard_map.127 = (bf16[512,512]{1,0:T(8,128)(2,1)}, f32[2,2,8,256]{3,2,1,0:T(8,128)S(1)}) custom-call(s32[1]{0:T(128)} %bitcast.pos_ref, bf16[256,1792]{1,0:T(8,128)(2,1)S(1)} %bitcast.29, bf16[16,1792]{1,0:T(8,128)(2,1)S(1)} %bitcast.39, bf16[512,512]{1,0:T(8,128)(2,1)S(1)} %bitcast.34, bf16[256,1792]{1,0:T(8,128)(2,1)S(1)} %bitcast.32, ...), custom_call_target="tpu_custom_call" | custom-call | flops 2147483648 | bytes 4194304 | tf_op jit(solution)/shard_map/pallas_call | solution.py:185
  67.6 5.6 %all-to-all-start.3 = ((bf16[32,16,512]{2,1,0:T(8,128)(2,1)}), bf16[32,16,512]{2,1,0:T(8,128)(2,1)S(1)}, u32[]{:S(2)}, u32[]{:S(2)}) async-start(bf16[32,16,512]{2,1,0:T(8,128)(2,1)} %bitcast.10), calls=%async_computation.3 | async-start | bytes 1048576 | tf_op jit(solution)/shard_map/all_to_all | solution.py:245
  73.2 9.7 %shard_map.128 = (bf16[256,1792]{1,0:T(8,128)(2,1)}, bf16[16,1792]{1,0:T(8,128)(2,1)}, bf16[256,1792]{1,0:T(8,128)(2,1)}, bf16[16,1792]{1,0:T(8,128)(2,1)}, bf16[256,512]{1,0:T(8,128)(2,1)}) custom-call(s32[1]{0:T(128)} %bitcast.pos_ref, bf16[256,1792]{1,0:T(8,128)(2,1)S(1)} %bitcast.30, bf16[16,1792]{1,0:T(8,128)(2,1)S(1)} %bitcast.40, ...), custom_call_target="tpu_custom_call" | custom-call | flops 4026531840 | bytes 4194304 | tf_op jit(solution)/shard_map/pallas_call | solution.py:185
  82.9 0.8 all-to-all-done.3
  83.7 0.1 reduce_sum.25
  83.8 0.8 broadcast_in_dim.36
  84.7 6.6 %all-to-all-start.4 = ((bf16[32,16,512]{2,1,0:T(8,128)(2,1)}), bf16[32,16,512]{2,1,0:T(8,128)(2,1)S(1)}, u32[]{:S(2)}, u32[]{:S(2)}) async-start(bf16[32,16,512]{2,1,0:T(8,128)(2,1)} %broadcast_in_dim.36), calls=%async_computation.4 | async-start | bytes 1048576 | tf_op jit(solution)/shard_map/all_to_all | solution.py:245
  91.2 0.0 all-gather.2.cloned.1.call-done
  91.3 3.8 %convolution_convert_fusion = bf16[16,3584]{1,0:T(8,128)(2,1)} fusion(bf16[16,512]{1,0:T(8,128)(2,1)S(1)} %reduce_sum.25, bf16[3584,512]{1,0:T(8,128)(2,1)} %all-gather.2.cloned.1.call-done), kind=kOutput, calls=%fused_computation | convolution fusion | flops 58777600 | bytes 3801088 | tf_op jit(solution)/shard_map/dot_general | solution.py:294
  95.0 6.7 %all-to-all-done.4 = bf16[32,16,512]{2,1,0:T(8,128)(2,1)S(1)} async-done(((bf16[32,16,512]{2,1,0:T(8,128)(2,1)}), bf16[32,16,512]{2,1,0:T(8,128)(2,1)S(1)}, u32[]{:S(2)}, u32[]{:S(2)}) %all-to-all-start.4) | async-done | bytes 524320 | tf_op jit(solution)/shard_map/all_to_all | solution.py:245
  101.7 0.3 fusion
  102.0 2.8 %collective-permute-start = (bf16[112,512]{1,0:T(8,128)(2,1)S(1)}, bf16[112,512]{1,0:T(8,128)(2,1)S(1)}, u32[]{:S(2)}, u32[]{:S(2)}) collective-permute-start(bf16[112,512]{1,0:T(8,128)(2,1)S(1)} %fusion), channel_id=1, source_target_pairs={{0,32},{32,0},{64,96},{96,64},{128,160},{160,128},{192,224},{224,1... | collective-permute-start | bytes 344072 | tf_op jit(solution)/shard_map/ppermute | solution.py:262
  104.8 3.7 %collective-permute-done = bf16[112,512]{1,0:T(8,128)(2,1)S(1)} collective-permute-done((bf16[112,512]{1,0:T(8,128)(2,1)S(1)}, bf16[112,512]{1,0:T(8,128)(2,1)S(1)}, u32[]{:S(2)}, u32[]{:S(2)}) %collective-permute-start) | collective-permute-done | bytes 114720 | tf_op jit(solution)/shard_map/ppermute | solution.py:262
  108.5 4.0 %collective-permute-start.1 = (bf16[112,512]{1,0:T(8,128)(2,1)S(1)}, bf16[112,512]{1,0:T(8,128)(2,1)S(1)}, u32[]{:S(2)}, u32[]{:S(2)}) collective-permute-start(bf16[112,512]{1,0:T(8,128)(2,1)S(1)} %add_convert_fusion.1), channel_id=1, source_target_pairs={{0,96},{32,64},{64,32},{96,0},{128,224},{160,192},{192,160},{224,1... | collective-permute-start | bytes 344072 | tf_op jit(solution)/shard_map/ppermute | solution.py:262
  112.5 3.0 %collective-permute-done.1 = bf16[112,512]{1,0:T(8,128)(2,1)S(1)} collective-permute-done((bf16[112,512]{1,0:T(8,128)(2,1)S(1)}, bf16[112,512]{1,0:T(8,128)(2,1)S(1)}, u32[]{:S(2)}, u32[]{:S(2)}) %collective-permute-start.1) | collective-permute-done | bytes 114720 | tf_op jit(solution)/shard_map/ppermute | solution.py:262
  115.5 6.4 %collective-permute-start.2 = (bf16[112,512]{1,0:T(8,128)(2,1)S(1)}, bf16[112,512]{1,0:T(8,128)(2,1)S(1)}, u32[]{:S(2)}, u32[]{:S(2)}) collective-permute-start(bf16[112,512]{1,0:T(8,128)(2,1)S(1)} %add_convert_fusion), channel_id=1, source_target_pairs={{0,224},{32,192},{64,160},{96,128},{128,96},{160,64},{192,32},{224... | collective-permute-start | bytes 344072 | tf_op jit(solution)/shard_map/ppermute | solution.py:262
  121.9 4.1 %collective-permute-done.2 = bf16[112,512]{1,0:T(8,128)(2,1)S(1)} collective-permute-done((bf16[112,512]{1,0:T(8,128)(2,1)S(1)}, bf16[112,512]{1,0:T(8,128)(2,1)S(1)}, u32[]{:S(2)}, u32[]{:S(2)}) %collective-permute-start.2) | collective-permute-done | bytes 114720 | tf_op jit(solution)/shard_map/ppermute | solution.py:262
  126.0 0.7 convert_add_fusion
  (2 shorter events, 0.1 us)
Async XLA Ops:
  7.2 39.2 %copy-start = (bf16[1,256,1792]{2,1,0:T(8,128)(2,1)S(1)}, bf16[1,256,1792]{2,1,0:T(8,128)(2,1)}, u32[]{:S(2)}) copy-start(bf16[1,256,1792]{2,1,0:T(8,128)(2,1)} %param.7) | copy-start | bytes 2752516
  7.2 39.2 %copy-start.3 = (bf16[1,16,1792]{2,1,0:T(8,128)(2,1)S(1)}, bf16[1,16,1792]{2,1,0:T(8,128)(2,1)}, u32[]{:S(2)}) copy-start(bf16[1,16,1792]{2,1,0:T(8,128)(2,1)} %param.9) | copy-start | bytes 172036
  7.2 39.2 %copy-start.1 = (bf16[1,256,1792]{2,1,0:T(8,128)(2,1)S(1)}, bf16[1,256,1792]{2,1,0:T(8,128)(2,1)}, u32[]{:S(2)}) copy-start(bf16[1,256,1792]{2,1,0:T(8,128)(2,1)} %param.12) | copy-start | bytes 2752516
  7.2 39.2 %copy-start.4 = (bf16[1,16,1792]{2,1,0:T(8,128)(2,1)S(1)}, bf16[1,16,1792]{2,1,0:T(8,128)(2,1)}, u32[]{:S(2)}) copy-start(bf16[1,16,1792]{2,1,0:T(8,128)(2,1)} %param.13) | copy-start | bytes 172036
  7.2 39.2 %copy-start.2 = (bf16[1,256,512]{2,1,0:T(8,128)(2,1)S(1)}, bf16[1,256,512]{2,1,0:T(8,128)(2,1)}, u32[]{:S(2)}) copy-start(bf16[1,256,512]{2,1,0:T(8,128)(2,1)} %param.8) | copy-start | bytes 786436
  7.2 84.0 %all-gather.2.cloned.1.call-start = ((), (), s32[]{:S(2)}) async-start(), calls=%async_computation.5 | async-start | bytes 3784704 | tf_op jit(solution)/shard_map/all_gather | solution.py:274
  41.3 16.7 %all-to-all-start.2 = ((bf16[32,16,512]{2,1,0:T(8,128)(2,1)}), bf16[32,16,512]{2,1,0:T(8,128)(2,1)S(1)}, u32[]{:S(2)}, u32[]{:S(2)}) async-start(bf16[32,16,512]{2,1,0:T(8,128)(2,1)} %broadcast_in_dim.30), calls=%async_computation.2 | async-start | bytes 1048576 | tf_op jit(solution)/shard_map/all_to_all | solution.py:245
  67.6 16.1 %all-to-all-start.3 = ((bf16[32,16,512]{2,1,0:T(8,128)(2,1)}), bf16[32,16,512]{2,1,0:T(8,128)(2,1)S(1)}, u32[]{:S(2)}, u32[]{:S(2)}) async-start(bf16[32,16,512]{2,1,0:T(8,128)(2,1)} %bitcast.10), calls=%async_computation.3 | async-start | bytes 1048576 | tf_op jit(solution)/shard_map/all_to_all | solution.py:245
  84.7 17.1 %all-to-all-start.4 = ((bf16[32,16,512]{2,1,0:T(8,128)(2,1)}), bf16[32,16,512]{2,1,0:T(8,128)(2,1)S(1)}, u32[]{:S(2)}, u32[]{:S(2)}) async-start(bf16[32,16,512]{2,1,0:T(8,128)(2,1)} %broadcast_in_dim.36), calls=%async_computation.4 | async-start | bytes 1048576 | tf_op jit(solution)/shard_map/all_to_all | solution.py:245
  102.0 6.4 %collective-permute-start = (bf16[112,512]{1,0:T(8,128)(2,1)S(1)}, bf16[112,512]{1,0:T(8,128)(2,1)S(1)}, u32[]{:S(2)}, u32[]{:S(2)}) collective-permute-start(bf16[112,512]{1,0:T(8,128)(2,1)S(1)} %fusion), channel_id=1, source_target_pairs={{0,32},{32,0},{64,96},{96,64},{128,160},{160,128},{192,224},{224,1... | collective-permute-start | bytes 344072 | tf_op jit(solution)/shard_map/ppermute | solution.py:262
  108.5 7.0 %collective-permute-start.1 = (bf16[112,512]{1,0:T(8,128)(2,1)S(1)}, bf16[112,512]{1,0:T(8,128)(2,1)S(1)}, u32[]{:S(2)}, u32[]{:S(2)}) collective-permute-start(bf16[112,512]{1,0:T(8,128)(2,1)S(1)} %add_convert_fusion.1), channel_id=1, source_target_pairs={{0,96},{32,64},{64,32},{96,0},{128,224},{160,192},{192,160},{224,1... | collective-permute-start | bytes 344072 | tf_op jit(solution)/shard_map/ppermute | solution.py:262
  115.5 10.5 %collective-permute-start.2 = (bf16[112,512]{1,0:T(8,128)(2,1)S(1)}, bf16[112,512]{1,0:T(8,128)(2,1)S(1)}, u32[]{:S(2)}, u32[]{:S(2)}) collective-permute-start(bf16[112,512]{1,0:T(8,128)(2,1)S(1)} %add_convert_fusion), channel_id=1, source_target_pairs={{0,224},{32,192},{64,160},{96,128},{128,96},{160,64},{192,32},{224... | collective-permute-start | bytes 344072 | tf_op jit(solution)/shard_map/ppermute | solution.py:262
Sparse Core Ops, SparseCore 0:
  10.6 57.1 all-gather.1

commit v4 on v3

--- a/solution.py
+++ b/solution.py
@@ -271,7 +271,6 @@
     count = lax.axis_size("ctx")
     rows = beacon_hidden.shape[1]
     hidden_rows = beacon_hidden[0]
-    full_weight = lax.all_gather(beacon_weight, "ctx", axis=0, tiled=True)
     stats = token_stats(
         query[0], beacon_query[0], keys_values[0], grad_tokens[0], grad_beacons[0]
     )
@@ -291,14 +290,14 @@
     tokens_out, beacons_out, query_grad, beacon_qgrad, token_kvgrad = others
     own_grad = jnp.sum(arrived.astype(jnp.float32), 0).astype(jnp.bfloat16)
     all_grad = gather_rows(own_grad, count)
-    hidden_grad = lax.dot_general(
-        own_grad, full_weight, (((1,), (1,)), ((), ())), preferred_element_type=jnp.float32
-    ).astype(jnp.bfloat16)
-    all_grad, hidden_grad = lax.optimization_barrier((all_grad, hidden_grad))
     weight_part = lax.dot_general(
         hidden_cols, all_grad, (((0,), (0,)), ((), ())), preferred_element_type=jnp.float32
     )
     grad_weight = sum_dp(weight_part)
+    hidden_part = lax.dot_general(
+        all_grad, beacon_weight, (((1,), (1,)), ((), ())), preferred_element_type=jnp.float32
+    ).astype(jnp.bfloat16)
+    hidden_grad = exchange(hidden_part.reshape(count, rows, -1)).transpose(1, 0, 2).reshape(rows, -1)
     return (
         tokens_out[None],
         beacons_out[None],

time: 134 us -> 125 us (0.933); the launches traced: 134 us -> 123 us
  blocking collectives: 30.1 us -> 57.7 us
  between operations: 14.2 us -> 0.79 us
  waiting for transfers between devices: 29 us -> 16.7 us
  starting transfers between devices: 30.4 us -> 21.8 us
  matrix products: 5.17 us -> 0.82 us
    all_to_all x2 -> x4, blocking collectives: 30.1 us -> 57.7 us  [exchange(): return lax.all_to_all(blocks, 'ctx', 0, 0, tiled=True)]
    all_to_all x3 -> x2, waiting for transfers between devices: 17.6 us -> 10 us  [exchange(): return lax.all_to_all(blocks, 'ctx', 0, 0, tiled=True)]
    all_to_all x3 -> x2, starting transfers between devices: 17.1 us -> 10.2 us  [exchange(): return lax.all_to_all(blocks, 'ctx', 0, 0, tiled=True)]
    ppermute x3, waiting for transfers between devices: 10.7 us -> 6.62 us  [sum_dp(): lax.ppermute(sent, 'dp', pairs).astype(jnp.float32)]
    dot_general x1, matrix products: 3.75 us -> 0.29 us  [shards(): lax.dot_general(all_grad, beacon_weight, (((1,), (1,)), ((), ())), prefer...]
    ppermute x3, starting transfers between devices: 13.2 us -> 11.5 us  [sum_dp(): lax.ppermute(sent, 'dp', pairs).astype(jnp.float32)]
  transfers between devices with their start and end apart: 7 -> 5, of which waited for: 6 -> 4; matrix products, arithmetic and copies ran while one was open for 6% -> 1% of each run, Pallas kernels for 16% -> 9%
where the time goes in v4:
time: 125 us; the launch traced here: 123 us
  blocking collectives  57.7 us (46%)
  starting transfers between devices  21.8 us (17%)
  Pallas kernels  20.7 us (17%)
  waiting for transfers between devices  16.7 us (13%)
  local copies, waits for them, and re-layouts  3.49 us (3%)
    all_to_all x4, blocking collectives, exchange(): return lax.all_to_all(blocks, 'ctx', 0, 0, tiled=True)  57.7 us
    pallas_call x3, Pallas kernels, call(): pl.pallas_call(kernel, out_shape=outs, in_specs=specs, out_specs=tuple((V...  20.7 us
    ppermute x3, starting transfers between devices, sum_dp(): lax.ppermute(sent, 'dp', pairs).astype(jnp.float32)  11.5 us
    all_to_all x2, starting transfers between devices, exchange(): return lax.all_to_all(blocks, 'ctx', 0, 0, tiled=True)  10.2 us
    all_to_all x2, waiting for transfers between devices, exchange(): return lax.all_to_all(blocks, 'ctx', 0, 0, tiled=True)  10 us
    ppermute x3, waiting for transfers between devices, sum_dp(): lax.ppermute(sent, 'dp', pairs).astype(jnp.float32)  6.62 us
  transfers between devices with their start and end apart: 5, of which 4 were waited for; matrix products, arithmetic and copies ran while one was open for 1% of the time, Pallas kernels for 9%

profile of v4, /device:TPU:2, one launch (start us, length us, event | category | flops | bytes accessed | tf_op | source)
XLA Modules:
  0.0 122.9 jit_solution(5264345985899933916)
XLA Ops:
  0.6 0.0 copy-start
  0.6 1.1 reshape_squeeze.3
  1.8 0.1 copy.26
  1.8 14.0 %all_to_all.30 = bf16[32,16,112]{2,1,0:T(8,128)(2,1)S(1)} all-to-all(bf16[32,16,112]{2,1,0:T(8,128)(2,1)S(1)} %copy.26), channel_id=1, replica_groups=mesh['dp'=8,'ctx'=32] {'ctx'}, dimensions={0} | all-to-all | bytes 229376 | tf_op jit(solution)/shard_map/all_to_all | solution.py:245
  15.9 0.0 copy-start.6
  15.9 0.0 copy-done
  15.9 0.3 convolution_convert_fusion
  16.2 0.4 copy-done.6
  16.5 0.0 copy-start.4
  16.5 0.0 copy-start.5
  16.5 15.3 %all_to_all.31 = bf16[32,16,512]{2,1,0:T(8,128)(2,1)S(1)} all-to-all(bf16[32,16,512]{2,1,0:T(8,128)(2,1)S(1)} %bitcast.50), channel_id=1, replica_groups=mesh['dp'=8,'ctx'=32] {'ctx'}, dimensions={0} | all-to-all | bytes 1048576 | tf_op jit(solution)/shard_map/all_to_all | solution.py:245
  31.8 0.0 copy-start.2
  31.8 0.1 reduce_sum.24
  31.9 0.0 copy-start.1
  31.9 0.9 broadcast_in_dim.27
  32.8 0.0 copy-start.3
  32.8 5.2 %all-to-all-start.2 = ((bf16[32,16,512]{2,1,0:T(8,128)(2,1)}), bf16[32,16,512]{2,1,0:T(8,128)(2,1)S(1)}, u32[]{:S(2)}, u32[]{:S(2)}) async-start(bf16[32,16,512]{2,1,0:T(8,128)(2,1)} %broadcast_in_dim.27), calls=%async_computation.2 | async-start | bytes 1048576 | tf_op jit(solution)/shard_map/all_to_all | solution.py:245
  38.0 0.0 copy-done.4
  38.0 0.0 copy-done.5
  38.0 0.0 copy-done.2
  38.0 0.0 copy-done.1
  38.0 0.0 copy-done.3
  38.0 1.5 %shard_map.126.stats_ref = f32[3,2,8,256]{3,2,1,0:T(8,128)S(1)} custom-call(bf16[256,1792]{1,0:T(8,128)(2,1)S(1)} %bitcast.33, bf16[16,1792]{1,0:T(8,128)(2,1)S(1)} %bitcast.43, bf16[256,512]{1,0:T(8,128)(2,1)S(1)} %bitcast.41, bf16[256,1792]{1,0:T(8,128)(2,1)S(1)} %bitcast.36, bf16[16,1792]{1,0:T(8,128)(2,1)S(1)} %bitcast.46), custom_call_target="tpu_custom_call" | custom-call | flops 536870912 | bytes 4194304 | tf_op jit(solution)/shard_map/pallas_call | solution.py:185
  39.5 9.0 %all-to-all-done.2 = bf16[32,16,512]{2,1,0:T(8,128)(2,1)S(1)} async-done(((bf16[32,16,512]{2,1,0:T(8,128)(2,1)}), bf16[32,16,512]{2,1,0:T(8,128)(2,1)S(1)}, u32[]{:S(2)}, u32[]{:S(2)}) %all-to-all-start.2) | async-done | bytes 524320 | tf_op jit(solution)/shard_map/all_to_all | solution.py:245
  48.6 9.6 %shard_map.127 = (bf16[512,512]{1,0:T(8,128)(2,1)}, f32[2,2,8,256]{3,2,1,0:T(8,128)S(1)}) custom-call(s32[1]{0:T(128)} %bitcast.pos_ref, bf16[256,1792]{1,0:T(8,128)(2,1)S(1)} %bitcast.34, bf16[16,1792]{1,0:T(8,128)(2,1)S(1)} %bitcast.44, bf16[512,512]{1,0:T(8,128)(2,1)S(1)} %bitcast.39, bf16[256,1792]{1,0:T(8,128)(2,1)S(1)} %bitcast.37, ...), custom_call_target="tpu_custom_call" | custom-call | flops 2147483648 | bytes 4194304 | tf_op jit(solution)/shard_map/pallas_call | solution.py:185
  58.2 5.1 %all-to-all-start.3 = ((bf16[32,16,512]{2,1,0:T(8,128)(2,1)}), bf16[32,16,512]{2,1,0:T(8,128)(2,1)S(1)}, u32[]{:S(2)}, u32[]{:S(2)}) async-start(bf16[32,16,512]{2,1,0:T(8,128)(2,1)} %bitcast.10), calls=%async_computation.3 | async-start | bytes 1048576 | tf_op jit(solution)/shard_map/all_to_all | solution.py:245
  63.2 9.6 %shard_map.128 = (bf16[256,1792]{1,0:T(8,128)(2,1)}, bf16[16,1792]{1,0:T(8,128)(2,1)}, bf16[256,1792]{1,0:T(8,128)(2,1)}, bf16[16,1792]{1,0:T(8,128)(2,1)}, bf16[256,512]{1,0:T(8,128)(2,1)}) custom-call(s32[1]{0:T(128)} %bitcast.pos_ref, bf16[256,1792]{1,0:T(8,128)(2,1)S(1)} %bitcast.35, bf16[16,1792]{1,0:T(8,128)(2,1)S(1)} %bitcast.45, ...), custom_call_target="tpu_custom_call" | custom-call | flops 4026531840 | bytes 4194304 | tf_op jit(solution)/shard_map/pallas_call | solution.py:185
  72.8 1.0 all-to-all-done.3
  73.8 0.1 reduce_sum.25
  73.9 0.1 broadcast_in_dim.33
  74.0 0.0 copy-start.7
  74.0 16.9 %all_to_all.32 = bf16[32,16,512]{2,1,0:T(8,128)(2,1)S(1)} all-to-all(bf16[32,16,512]{2,1,0:T(8,128)(2,1)S(1)} %broadcast_in_dim.33), channel_id=1, replica_groups=mesh['dp'=8,'ctx'=32] {'ctx'}, dimensions={0} | all-to-all | bytes 1048576 | tf_op jit(solution)/shard_map/all_to_all | solution.py:245
  90.9 0.0 copy-done.7
  91.0 0.3 fusion.1
  91.2 2.0 %collective-permute-start = (bf16[112,512]{1,0:T(8,128)(2,1)S(1)}, bf16[112,512]{1,0:T(8,128)(2,1)S(1)}, u32[]{:S(2)}, u32[]{:S(2)}) collective-permute-start(bf16[112,512]{1,0:T(8,128)(2,1)S(1)} %fusion.1), channel_id=1, source_target_pairs={{0,32},{32,0},{64,96},{96,64},{128,160},{160,128},{192,224},{224,1... | collective-permute-start | bytes 344072 | tf_op jit(solution)/shard_map/ppermute | solution.py:262
  93.2 3.7 %collective-permute-done = bf16[112,512]{1,0:T(8,128)(2,1)S(1)} collective-permute-done((bf16[112,512]{1,0:T(8,128)(2,1)S(1)}, bf16[112,512]{1,0:T(8,128)(2,1)S(1)}, u32[]{:S(2)}, u32[]{:S(2)}) %collective-permute-start) | collective-permute-done | bytes 114720 | tf_op jit(solution)/shard_map/ppermute | solution.py:262
  96.9 4.5 %collective-permute-start.1 = (bf16[112,512]{1,0:T(8,128)(2,1)S(1)}, bf16[112,512]{1,0:T(8,128)(2,1)S(1)}, u32[]{:S(2)}, u32[]{:S(2)}) collective-permute-start(bf16[112,512]{1,0:T(8,128)(2,1)S(1)} %add_convert_fusion.1), channel_id=1, source_target_pairs={{0,96},{32,64},{64,32},{96,0},{128,224},{160,192},{192,160},{224,1... | collective-permute-start | bytes 344072 | tf_op jit(solution)/shard_map/ppermute | solution.py:262
  101.4 3.0 %collective-permute-done.1 = bf16[112,512]{1,0:T(8,128)(2,1)S(1)} collective-permute-done((bf16[112,512]{1,0:T(8,128)(2,1)S(1)}, bf16[112,512]{1,0:T(8,128)(2,1)S(1)}, u32[]{:S(2)}, u32[]{:S(2)}) %collective-permute-start.1) | collective-permute-done | bytes 114720 | tf_op jit(solution)/shard_map/ppermute | solution.py:262
  104.4 5.0 %collective-permute-start.2 = (bf16[112,512]{1,0:T(8,128)(2,1)S(1)}, bf16[112,512]{1,0:T(8,128)(2,1)S(1)}, u32[]{:S(2)}, u32[]{:S(2)}) collective-permute-start(bf16[112,512]{1,0:T(8,128)(2,1)S(1)} %add_convert_fusion), channel_id=1, source_target_pairs={{0,224},{32,192},{64,160},{96,128},{128,96},{160,64},{192,32},{224... | collective-permute-start | bytes 344072 | tf_op jit(solution)/shard_map/ppermute | solution.py:262
  109.4 0.3 convolution_convert_fusion.1
  109.7 0.1 copy.27
  109.9 11.4 %all_to_all.33 = bf16[32,16,112]{2,1,0:T(8,128)(2,1)S(1)} all-to-all(bf16[32,16,112]{2,1,0:T(8,128)(2,1)S(1)} %bitcast.52), channel_id=1, replica_groups=mesh['dp'=8,'ctx'=32] {'ctx'}, dimensions={0} | all-to-all | bytes 229376 | tf_op jit(solution)/shard_map/all_to_all | solution.py:245
  121.3 0.8 broadcast_in_dim_reshape.3
  122.2 0.0 collective-permute-done.2
  122.2 0.7 convert_add_fusion
  (3 shorter events, 0.1 us)
Async XLA Ops:
  0.6 15.3 %copy-start = (bf16[112,512]{1,0:T(8,128)(2,1)S(1)}, bf16[112,512]{1,0:T(8,128)(2,1)}, u32[]{:S(2)}) copy-start(bf16[112,512]{1,0:T(8,128)(2,1)} %param.11) | copy-start | bytes 344068
  15.9 0.7 copy-start.6
  16.5 21.4 %copy-start.4 = (bf16[1,16,1792]{2,1,0:T(8,128)(2,1)S(1)}, bf16[1,16,1792]{2,1,0:T(8,128)(2,1)}, u32[]{:S(2)}) copy-start(bf16[1,16,1792]{2,1,0:T(8,128)(2,1)} %param.9) | copy-start | bytes 172036
  16.5 21.4 %copy-start.5 = (bf16[1,16,1792]{2,1,0:T(8,128)(2,1)S(1)}, bf16[1,16,1792]{2,1,0:T(8,128)(2,1)}, u32[]{:S(2)}) copy-start(bf16[1,16,1792]{2,1,0:T(8,128)(2,1)} %param.13) | copy-start | bytes 172036
  31.8 6.2 %copy-start.2 = (bf16[1,256,1792]{2,1,0:T(8,128)(2,1)S(1)}, bf16[1,256,1792]{2,1,0:T(8,128)(2,1)}, u32[]{:S(2)}) copy-start(bf16[1,256,1792]{2,1,0:T(8,128)(2,1)} %param.12) | copy-start | bytes 2752516
  31.9 6.1 %copy-start.1 = (bf16[1,256,1792]{2,1,0:T(8,128)(2,1)S(1)}, bf16[1,256,1792]{2,1,0:T(8,128)(2,1)}, u32[]{:S(2)}) copy-start(bf16[1,256,1792]{2,1,0:T(8,128)(2,1)} %param.7) | copy-start | bytes 2752516
  32.8 5.2 %copy-start.3 = (bf16[1,256,512]{2,1,0:T(8,128)(2,1)S(1)}, bf16[1,256,512]{2,1,0:T(8,128)(2,1)}, u32[]{:S(2)}) copy-start(bf16[1,256,512]{2,1,0:T(8,128)(2,1)} %param.8) | copy-start | bytes 786436
  32.8 15.8 %all-to-all-start.2 = ((bf16[32,16,512]{2,1,0:T(8,128)(2,1)}), bf16[32,16,512]{2,1,0:T(8,128)(2,1)S(1)}, u32[]{:S(2)}, u32[]{:S(2)}) async-start(bf16[32,16,512]{2,1,0:T(8,128)(2,1)} %broadcast_in_dim.27), calls=%async_computation.2 | async-start | bytes 1048576 | tf_op jit(solution)/shard_map/all_to_all | solution.py:245
  58.2 15.7 %all-to-all-start.3 = ((bf16[32,16,512]{2,1,0:T(8,128)(2,1)}), bf16[32,16,512]{2,1,0:T(8,128)(2,1)S(1)}, u32[]{:S(2)}, u32[]{:S(2)}) async-start(bf16[32,16,512]{2,1,0:T(8,128)(2,1)} %bitcast.10), calls=%async_computation.3 | async-start | bytes 1048576 | tf_op jit(solution)/shard_map/all_to_all | solution.py:245
  74.0 17.0 %copy-start.7 = (bf16[32,16,112]{2,1,0:T(8,128)(2,1)S(1)}, bf16[32,16,112]{2,1,0:T(8,128)(2,1)}, u32[]{:S(2)}) copy-start(bf16[32,16,112]{2,1,0:T(8,128)(2,1)} %copy-done.6) | copy-start | bytes 344068
  91.2 5.7 %collective-permute-start = (bf16[112,512]{1,0:T(8,128)(2,1)S(1)}, bf16[112,512]{1,0:T(8,128)(2,1)S(1)}, u32[]{:S(2)}, u32[]{:S(2)}) collective-permute-start(bf16[112,512]{1,0:T(8,128)(2,1)S(1)} %fusion.1), channel_id=1, source_target_pairs={{0,32},{32,0},{64,96},{96,64},{128,160},{160,128},{192,224},{224,1... | collective-permute-start | bytes 344072 | tf_op jit(solution)/shard_map/ppermute | solution.py:262
  96.9 7.5 %collective-permute-start.1 = (bf16[112,512]{1,0:T(8,128)(2,1)S(1)}, bf16[112,512]{1,0:T(8,128)(2,1)S(1)}, u32[]{:S(2)}, u32[]{:S(2)}) collective-permute-start(bf16[112,512]{1,0:T(8,128)(2,1)S(1)} %add_convert_fusion.1), channel_id=1, source_target_pairs={{0,96},{32,64},{64,32},{96,0},{128,224},{160,192},{192,160},{224,1... | collective-permute-start | bytes 344072 | tf_op jit(solution)/shard_map/ppermute | solution.py:262
  104.4 17.7 %collective-permute-start.2 = (bf16[112,512]{1,0:T(8,128)(2,1)S(1)}, bf16[112,512]{1,0:T(8,128)(2,1)S(1)}, u32[]{:S(2)}, u32[]{:S(2)}) collective-permute-start(bf16[112,512]{1,0:T(8,128)(2,1)S(1)} %add_convert_fusion), channel_id=1, source_target_pairs={{0,224},{32,192},{64,160},{96,128},{128,96},{160,64},{192,32},{224... | collective-permute-start | bytes 344072 | tf_op jit(solution)/shard_map/ppermute | solution.py:262

commit v5 on v4

--- a/solution.py
+++ b/solution.py
@@ -253,15 +253,18 @@
     return exchange(jnp.broadcast_to(rows[None], (count,) + rows.shape)).reshape(-1, rows.shape[-1])
 
 
-def sum_dp(part):
-    size = lax.axis_size("dp")
-    step = 1
-    while step < size:
-        sent = part.astype(jnp.bfloat16)
-        pairs = [(i, i // (2 * step) * 2 * step + 2 * step - 1 - i % (2 * step)) for i in range(size)]
-        part = sent.astype(jnp.float32) + lax.ppermute(sent, "dp", pairs).astype(jnp.float32)
-        step *= 2
-    return part
+def swap_dp(sent, mask):
+    pairs = [(i, i ^ mask) for i in range(lax.axis_size("dp"))]
+    return lax.ppermute(sent, "dp", pairs).astype(jnp.float32)
+
+
+def sum_dp(part, beside):
+    sent = part.astype(jnp.bfloat16)
+    near, far, wide = [swap_dp(sent, mask) for mask in (2, 4, 6)]
+    near, far, wide, beside = lax.optimization_barrier((near, far, wide, beside))
+    part = (sent.astype(jnp.float32) + near) + (far + wide)
+    sent = part.astype(jnp.bfloat16)
+    return sent.astype(jnp.float32) + swap_dp(sent, 1), beside
 
 
 def shards(
@@ -293,11 +296,12 @@
     weight_part = lax.dot_general(
         hidden_cols, all_grad, (((0,), (0,)), ((), ())), preferred_element_type=jnp.float32
     )
-    grad_weight = sum_dp(weight_part)
     hidden_part = lax.dot_general(
         all_grad, beacon_weight, (((1,), (1,)), ((), ())), preferred_element_type=jnp.float32
     ).astype(jnp.bfloat16)
-    hidden_grad = exchange(hidden_part.reshape(count, rows, -1)).transpose(1, 0, 2).reshape(rows, -1)
+    hidden_blocks = exchange(hidden_part.reshape(count, rows, -1))
+    grad_weight, hidden_blocks = sum_dp(weight_part, hidden_blocks)
+    hidden_grad = hidden_blocks.transpose(1, 0, 2).reshape(rows, -1)
     return (
         tokens_out[None],
         beacons_out[None],

time: 125 us -> 121 us (0.968)
  blocking collectives: 57.7 us -> 46.2 us
  starting transfers between devices: 21.8 us -> 25.2 us
  waiting for transfers between devices: 16.7 us -> 20 us
    all_to_all x4 -> x3, blocking collectives: 57.7 us -> 46.2 us  [exchange(): return lax.all_to_all(blocks, 'ctx', 0, 0, tiled=True)]
    all_to_all x2 -> x3, starting transfers between devices: 10.2 us -> 15.3 us  [exchange(): return lax.all_to_all(blocks, 'ctx', 0, 0, tiled=True)]
    all_to_all x2 -> x3, waiting for transfers between devices: 10 us -> 11.8 us  [exchange(): return lax.all_to_all(blocks, 'ctx', 0, 0, tiled=True)]
    ppermute x3 -> x4, waiting for transfers between devices: 6.62 us -> 8.24 us  [swap_dp(): return lax.ppermute(sent, 'dp', pairs).astype(jnp.float32)]
    ppermute x3 -> x4, starting transfers between devices: 11.5 us -> 9.97 us  [swap_dp(): return lax.ppermute(sent, 'dp', pairs).astype(jnp.float32)]
  transfers between devices with their start and end apart: 5 -> 7, of which waited for: 4 -> 7; matrix products, arithmetic and copies ran while one was open for 1% -> 2% of each run, Pallas kernels for 9% -> 9%
where the time goes in v5:
time: 121 us; the launch traced here: 119 us
  blocking collectives  46.2 us (38%)
  starting transfers between devices  25.2 us (21%)
  Pallas kernels  20.7 us (17%)
  waiting for transfers between devices  20 us (17%)
  local copies, waits for them, and re-layouts  4.14 us (3%)
    all_to_all x3, blocking collectives, exchange(): return lax.all_to_all(blocks, 'ctx', 0, 0, tiled=True)  46.2 us
    pallas_call x3, Pallas kernels, call(): pl.pallas_call(kernel, out_shape=outs, in_specs=specs, out_specs=tuple((V...  20.7 us
    all_to_all x3, starting transfers between devices, exchange(): return lax.all_to_all(blocks, 'ctx', 0, 0, tiled=True)  15.3 us
    all_to_all x3, waiting for transfers between devices, exchange(): return lax.all_to_all(blocks, 'ctx', 0, 0, tiled=True)  11.8 us
    ppermute x4, starting transfers between devices, swap_dp(): return lax.ppermute(sent, 'dp', pairs).astype(jnp.float32)  9.97 us
    ppermute x4, waiting for transfers between devices, swap_dp(): return lax.ppermute(sent, 'dp', pairs).astype(jnp.float32)  8.24 us
  transfers between devices with their start and end apart: 7, of which 7 were waited for; matrix products, arithmetic and copies ran while one was open for 2% of the time, Pallas kernels for 9%

profile of v5, /device:TPU:2, one launch (start us, length us, event | category | flops | bytes accessed | tf_op | source)
XLA Modules:
  0.0 118.9 jit_solution(752710998140639478)
XLA Ops:
  0.6 0.0 copy-start
  0.6 1.1 reshape_squeeze.3
  1.8 0.1 copy.26
  1.8 14.0 %all_to_all.30 = bf16[32,16,112]{2,1,0:T(8,128)(2,1)S(1)} all-to-all(bf16[32,16,112]{2,1,0:T(8,128)(2,1)S(1)} %copy.26), channel_id=1, replica_groups=mesh['dp'=8,'ctx'=32] {'ctx'}, dimensions={0} | all-to-all | bytes 229376 | tf_op jit(solution)/shard_map/all_to_all | solution.py:245
  15.9 0.0 copy-start.6
  15.9 0.0 copy-done
  15.9 0.3 convolution_convert_fusion
  16.2 0.4 copy-done.6
  16.5 0.0 copy-start.4
  16.5 0.0 copy-start.5
  16.5 15.3 %all_to_all.31 = bf16[32,16,512]{2,1,0:T(8,128)(2,1)S(1)} all-to-all(bf16[32,16,512]{2,1,0:T(8,128)(2,1)S(1)} %bitcast.50), channel_id=1, replica_groups=mesh['dp'=8,'ctx'=32] {'ctx'}, dimensions={0} | all-to-all | bytes 1048576 | tf_op jit(solution)/shard_map/all_to_all | solution.py:245
  31.8 0.0 copy-start.2
  31.8 0.1 reduce_sum.24
  31.9 0.0 copy-start.1
  31.9 0.9 broadcast_in_dim.27
  32.8 5.2 %all-to-all-start.2 = ((bf16[32,16,512]{2,1,0:T(8,128)(2,1)}), bf16[32,16,512]{2,1,0:T(8,128)(2,1)S(1)}, u32[]{:S(2)}, u32[]{:S(2)}) async-start(bf16[32,16,512]{2,1,0:T(8,128)(2,1)} %broadcast_in_dim.27), calls=%async_computation.2 | async-start | bytes 1048576 | tf_op jit(solution)/shard_map/all_to_all | solution.py:245
  38.0 0.0 copy-done.4
  38.0 0.0 copy-done.5
  38.0 0.0 copy-done.2
  38.0 0.0 copy-done.1
  38.0 0.0 copy-done.3
  38.0 1.5 %shard_map.126.stats_ref = f32[3,2,8,256]{3,2,1,0:T(8,128)S(1)} custom-call(bf16[256,1792]{1,0:T(8,128)(2,1)S(1)} %bitcast.33, bf16[16,1792]{1,0:T(8,128)(2,1)S(1)} %bitcast.43, bf16[256,512]{1,0:T(8,128)(2,1)S(1)} %bitcast.41, bf16[256,1792]{1,0:T(8,128)(2,1)S(1)} %bitcast.36, bf16[16,1792]{1,0:T(8,128)(2,1)S(1)} %bitcast.46), custom_call_target="tpu_custom_call" | custom-call | flops 536870912 | bytes 4194304 | tf_op jit(solution)/shard_map/pallas_call | solution.py:185
  39.5 9.0 %all-to-all-done.2 = bf16[32,16,512]{2,1,0:T(8,128)(2,1)S(1)} async-done(((bf16[32,16,512]{2,1,0:T(8,128)(2,1)}), bf16[32,16,512]{2,1,0:T(8,128)(2,1)S(1)}, u32[]{:S(2)}, u32[]{:S(2)}) %all-to-all-start.2) | async-done | bytes 524320 | tf_op jit(solution)/shard_map/all_to_all | solution.py:245
  48.6 9.6 %shard_map.127 = (bf16[512,512]{1,0:T(8,128)(2,1)}, f32[2,2,8,256]{3,2,1,0:T(8,128)S(1)}) custom-call(s32[1]{0:T(128)} %bitcast.pos_ref, bf16[256,1792]{1,0:T(8,128)(2,1)S(1)} %bitcast.34, bf16[16,1792]{1,0:T(8,128)(2,1)S(1)} %bitcast.44, bf16[512,512]{1,0:T(8,128)(2,1)S(1)} %bitcast.39, bf16[256,1792]{1,0:T(8,128)(2,1)S(1)} %bitcast.37, ...), custom_call_target="tpu_custom_call" | custom-call | flops 2147483648 | bytes 4194304 | tf_op jit(solution)/shard_map/pallas_call | solution.py:185
  58.2 5.1 %all-to-all-start.3 = ((bf16[32,16,512]{2,1,0:T(8,128)(2,1)}), bf16[32,16,512]{2,1,0:T(8,128)(2,1)S(1)}, u32[]{:S(2)}, u32[]{:S(2)}) async-start(bf16[32,16,512]{2,1,0:T(8,128)(2,1)} %bitcast.10), calls=%async_computation.3 | async-start | bytes 1048576 | tf_op jit(solution)/shard_map/all_to_all | solution.py:245
  63.2 9.6 %shard_map.128 = (bf16[256,1792]{1,0:T(8,128)(2,1)}, bf16[16,1792]{1,0:T(8,128)(2,1)}, bf16[256,1792]{1,0:T(8,128)(2,1)}, bf16[16,1792]{1,0:T(8,128)(2,1)}, bf16[256,512]{1,0:T(8,128)(2,1)}) custom-call(s32[1]{0:T(128)} %bitcast.pos_ref, bf16[256,1792]{1,0:T(8,128)(2,1)S(1)} %bitcast.35, bf16[16,1792]{1,0:T(8,128)(2,1)S(1)} %bitcast.45, ...), custom_call_target="tpu_custom_call" | custom-call | flops 4026531840 | bytes 4194304 | tf_op jit(solution)/shard_map/pallas_call | solution.py:185
  72.8 1.0 all-to-all-done.3
  73.8 0.1 reduce_sum.25
  73.9 0.1 broadcast_in_dim.33
  74.0 0.0 copy-start.7
  74.0 16.9 %all_to_all.32 = bf16[32,16,512]{2,1,0:T(8,128)(2,1)S(1)} all-to-all(bf16[32,16,512]{2,1,0:T(8,128)(2,1)S(1)} %broadcast_in_dim.33), channel_id=1, replica_groups=mesh['dp'=8,'ctx'=32] {'ctx'}, dimensions={0} | all-to-all | bytes 1048576 | tf_op jit(solution)/shard_map/all_to_all | solution.py:245
  90.9 0.0 copy-done.7
  90.9 0.3 fusion.1
  91.2 6.4 %collective-permute-start.2 = (bf16[112,512]{1,0:T(8,128)(2,1)S(1)}, bf16[112,512]{1,0:T(8,128)(2,1)S(1)}, u32[]{:S(2)}, u32[]{:S(2)}) collective-permute-start(bf16[112,512]{1,0:T(8,128)(2,1)S(1)} %fusion.1), channel_id=1, source_target_pairs={{0,192},{32,224},{64,128},{96,160},{128,64},{160,96},{192,0},{224,... | collective-permute-start | bytes 344072 | tf_op jit(solution)/shard_map/ppermute | solution.py:258
  97.6 1.0 collective-permute-start.1
  98.6 1.5 %collective-permute-start = (bf16[112,512]{1,0:T(8,128)(2,1)S(1)}, bf16[112,512]{1,0:T(8,128)(2,1)S(1)}, u32[]{:S(2)}, u32[]{:S(2)}) collective-permute-start(bf16[112,512]{1,0:T(8,128)(2,1)S(1)} %fusion.1), channel_id=1, source_target_pairs={{0,64},{32,96},{64,0},{96,32},{128,192},{160,224},{192,128},{224,1... | collective-permute-start | bytes 344072 | tf_op jit(solution)/shard_map/ppermute | solution.py:258
  100.0 0.3 convolution_convert_fusion.1
  100.3 0.8 copy.27
  101.1 5.0 %all-to-all-start.5 = ((bf16[32,16,112]{2,1,0:T(8,128)(2,1)}), bf16[32,16,112]{2,1,0:T(8,128)(2,1)S(1)}, u32[]{:S(2)}, u32[]{:S(2)}) async-start(bf16[32,16,112]{2,1,0:T(8,128)(2,1)} %bitcast.19), calls=%async_computation.5 | async-start | bytes 262144 | tf_op jit(solution)/shard_map/all_to_all | solution.py:245
  106.1 1.8 %collective-permute-done.2 = bf16[112,512]{1,0:T(8,128)(2,1)S(1)} collective-permute-done((bf16[112,512]{1,0:T(8,128)(2,1)S(1)}, bf16[112,512]{1,0:T(8,128)(2,1)S(1)}, u32[]{:S(2)}, u32[]{:S(2)}) %collective-permute-start.2) | collective-permute-done | bytes 114720 | tf_op jit(solution)/shard_map/ppermute | solution.py:258
  107.9 2.1 %collective-permute-done.1 = bf16[112,512]{1,0:T(8,128)(2,1)S(1)} collective-permute-done((bf16[112,512]{1,0:T(8,128)(2,1)S(1)}, bf16[112,512]{1,0:T(8,128)(2,1)S(1)}, u32[]{:S(2)}, u32[]{:S(2)}) %collective-permute-start.1) | collective-permute-done | bytes 114720 | tf_op jit(solution)/shard_map/ppermute | solution.py:258
  110.1 1.0 collective-permute-done
  111.1 1.7 %all-to-all-done.5 = bf16[32,16,112]{2,1,0:T(8,128)(2,1)S(1)} async-done(((bf16[32,16,112]{2,1,0:T(8,128)(2,1)}), bf16[32,16,112]{2,1,0:T(8,128)(2,1)S(1)}, u32[]{:S(2)}, u32[]{:S(2)}) %all-to-all-start.5) | async-done | bytes 114720 | tf_op jit(solution)/shard_map/all_to_all | solution.py:245
  112.9 0.1 add_convert_fusion
  112.9 1.1 collective-permute-start.3
  114.1 0.8 broadcast_in_dim_reshape.3
  114.9 3.3 %collective-permute-done.3 = bf16[112,512]{1,0:T(8,128)(2,1)S(1)} collective-permute-done((bf16[112,512]{1,0:T(8,128)(2,1)S(1)}, bf16[112,512]{1,0:T(8,128)(2,1)S(1)}, u32[]{:S(2)}, u32[]{:S(2)}) %collective-permute-start.3) | collective-permute-done | bytes 114720 | tf_op jit(solution)/shard_map/ppermute | solution.py:258
  118.2 0.7 convert_add_fusion
  (5 shorter events, 0.1 us)
Async XLA Ops:
  0.6 15.3 %copy-start = (bf16[112,512]{1,0:T(8,128)(2,1)S(1)}, bf16[112,512]{1,0:T(8,128)(2,1)}, u32[]{:S(2)}) copy-start(bf16[112,512]{1,0:T(8,128)(2,1)} %param.11) | copy-start | bytes 344068
  15.9 0.7 copy-start.6
  16.5 21.4 %copy-start.4 = (bf16[1,16,1792]{2,1,0:T(8,128)(2,1)S(1)}, bf16[1,16,1792]{2,1,0:T(8,128)(2,1)}, u32[]{:S(2)}) copy-start(bf16[1,16,1792]{2,1,0:T(8,128)(2,1)} %param.9) | copy-start | bytes 172036
  16.5 21.4 %copy-start.5 = (bf16[1,16,1792]{2,1,0:T(8,128)(2,1)S(1)}, bf16[1,16,1792]{2,1,0:T(8,128)(2,1)}, u32[]{:S(2)}) copy-start(bf16[1,16,1792]{2,1,0:T(8,128)(2,1)} %param.13) | copy-start | bytes 172036
  31.8 6.2 %copy-start.2 = (bf16[1,256,1792]{2,1,0:T(8,128)(2,1)S(1)}, bf16[1,256,1792]{2,1,0:T(8,128)(2,1)}, u32[]{:S(2)}) copy-start(bf16[1,256,1792]{2,1,0:T(8,128)(2,1)} %param.12) | copy-start | bytes 2752516
  31.9 6.1 %copy-start.1 = (bf16[1,256,1792]{2,1,0:T(8,128)(2,1)S(1)}, bf16[1,256,1792]{2,1,0:T(8,128)(2,1)}, u32[]{:S(2)}) copy-start(bf16[1,256,1792]{2,1,0:T(8,128)(2,1)} %param.7) | copy-start | bytes 2752516
  32.8 5.2 %copy-start.3 = (bf16[1,256,512]{2,1,0:T(8,128)(2,1)S(1)}, bf16[1,256,512]{2,1,0:T(8,128)(2,1)}, u32[]{:S(2)}) copy-start(bf16[1,256,512]{2,1,0:T(8,128)(2,1)} %param.8) | copy-start | bytes 786436
  32.8 15.8 %all-to-all-start.2 = ((bf16[32,16,512]{2,1,0:T(8,128)(2,1)}), bf16[32,16,512]{2,1,0:T(8,128)(2,1)S(1)}, u32[]{:S(2)}, u32[]{:S(2)}) async-start(bf16[32,16,512]{2,1,0:T(8,128)(2,1)} %broadcast_in_dim.27), calls=%async_computation.2 | async-start | bytes 1048576 | tf_op jit(solution)/shard_map/all_to_all | solution.py:245
  58.2 15.7 %all-to-all-start.3 = ((bf16[32,16,512]{2,1,0:T(8,128)(2,1)}), bf16[32,16,512]{2,1,0:T(8,128)(2,1)S(1)}, u32[]{:S(2)}, u32[]{:S(2)}) async-start(bf16[32,16,512]{2,1,0:T(8,128)(2,1)} %bitcast.10), calls=%async_computation.3 | async-start | bytes 1048576 | tf_op jit(solution)/shard_map/all_to_all | solution.py:245
  74.0 16.9 %copy-start.7 = (bf16[32,16,112]{2,1,0:T(8,128)(2,1)S(1)}, bf16[32,16,112]{2,1,0:T(8,128)(2,1)}, u32[]{:S(2)}) copy-start(bf16[32,16,112]{2,1,0:T(8,128)(2,1)} %copy-done.6) | copy-start | bytes 344068
  91.2 16.7 %collective-permute-start.2 = (bf16[112,512]{1,0:T(8,128)(2,1)S(1)}, bf16[112,512]{1,0:T(8,128)(2,1)S(1)}, u32[]{:S(2)}, u32[]{:S(2)}) collective-permute-start(bf16[112,512]{1,0:T(8,128)(2,1)S(1)} %fusion.1), channel_id=1, source_target_pairs={{0,192},{32,224},{64,128},{96,160},{128,64},{160,96},{192,0},{224,... | collective-permute-start | bytes 344072 | tf_op jit(solution)/shard_map/ppermute | solution.py:258
  97.6 12.5 %collective-permute-start.1 = (bf16[112,512]{1,0:T(8,128)(2,1)S(1)}, bf16[112,512]{1,0:T(8,128)(2,1)S(1)}, u32[]{:S(2)}, u32[]{:S(2)}) collective-permute-start(bf16[112,512]{1,0:T(8,128)(2,1)S(1)} %fusion.1), channel_id=1, source_target_pairs={{0,128},{32,160},{64,192},{96,224},{128,0},{160,32},{192,64},{224,... | collective-permute-start | bytes 344072 | tf_op jit(solution)/shard_map/ppermute | solution.py:258
  98.6 12.5 %collective-permute-start = (bf16[112,512]{1,0:T(8,128)(2,1)S(1)}, bf16[112,512]{1,0:T(8,128)(2,1)S(1)}, u32[]{:S(2)}, u32[]{:S(2)}) collective-permute-start(bf16[112,512]{1,0:T(8,128)(2,1)S(1)} %fusion.1), channel_id=1, source_target_pairs={{0,64},{32,96},{64,0},{96,32},{128,192},{160,224},{192,128},{224,1... | collective-permute-start | bytes 344072 | tf_op jit(solution)/shard_map/ppermute | solution.py:258
  101.1 11.7 %all-to-all-start.5 = ((bf16[32,16,112]{2,1,0:T(8,128)(2,1)}), bf16[32,16,112]{2,1,0:T(8,128)(2,1)S(1)}, u32[]{:S(2)}, u32[]{:S(2)}) async-start(bf16[32,16,112]{2,1,0:T(8,128)(2,1)} %bitcast.19), calls=%async_computation.5 | async-start | bytes 262144 | tf_op jit(solution)/shard_map/all_to_all | solution.py:245
  112.9 5.3 %collective-permute-start.3 = (bf16[112,512]{1,0:T(8,128)(2,1)S(1)}, bf16[112,512]{1,0:T(8,128)(2,1)S(1)}, u32[]{:S(2)}, u32[]{:S(2)}) collective-permute-start(bf16[112,512]{1,0:T(8,128)(2,1)S(1)} %add_convert_fusion), channel_id=1, source_target_pairs={{0,32},{32,0},{64,96},{96,64},{128,160},{160,128},{192,224},{224,1... | collective-permute-start | bytes 344072 | tf_op jit(solution)/shard_map/ppermute | solution.py:258

commit v6 on v5

--- a/solution.py
+++ b/solution.py
@@ -83,37 +83,46 @@
     start = pos_ref[0] * count
     bias_ref[...] = prefix_bias(total, span, start, None)
     bbias_ref[...] = prefix_bias(total, HD, start, count)
-    for group in range(KVH):
+    jobs = [(group, head) for group in range(KVH) for head in range(GROUP + 1)]
+
+    def products(group, head):
+        query = head_rows(q_ref, bq_ref, group, head)
+        cot = head_rows(c_ref, bc_ref, group, head)
         keys = kv_ref[:, group * HD : (group + 1) * HD]
         vals = kv_ref[:, (KVH + group) * HD : (KVH + group + 1) * HD]
-        key_grad = jnp.zeros((total, HD), jnp.float32)
-        val_grad = jnp.zeros((total, HD), jnp.float32)
-        for head in range(GROUP + 1):
-            query = head_rows(q_ref, bq_ref, group, head)
-            cot = head_rows(c_ref, bc_ref, group, head)
-            width = query.shape[0]
-            bias = bias_ref if head < GROUP else bbias_ref
-            scores = dot_nt(keys, query) * (FACTOR * LOG2E) + bias[...]
-            top_tok = stats_ref[0, group, head : head + 1, :width]
-            sum_tok = stats_ref[1, group, head : head + 1, :width]
-            cen_tok = stats_ref[2, group, head : head + 1, :width]
-            top = jnp.maximum(jnp.max(scores, 0, keepdims=True), top_tok)
-            shift = jnp.exp2(top_tok - top)
-            expo = jnp.exp2(scores - top)
-            dweights = dot_nt(vals, cot)
-            total_sum = shift * sum_tok + jnp.sum(expo, 0, keepdims=True)
-            inverse = 1.0 / total_sum
-            centre = inverse * (
-                shift * cen_tok + jnp.sum(expo * dweights, 0, keepdims=True)
+        return query, cot, dot_nt(keys, query), dot_nt(vals, cot)
+
+    ahead = products(*jobs[0])
+    for at, (group, head) in enumerate(jobs):
+        query, cot, scores, dweights = ahead
+        if at + 1 < len(jobs):
+            ahead = products(*jobs[at + 1])
+        if head == 0:
+            key_grad = jnp.zeros((total, HD), jnp.float32)
+            val_grad = jnp.zeros((total, HD), jnp.float32)
+        width = query.shape[0]
+        bias = bias_ref if head < GROUP else bbias_ref
+        scores = scores * (FACTOR * LOG2E) + bias[...]
+        top_tok = stats_ref[0, group, head : head + 1, :width]
+        sum_tok = stats_ref[1, group, head : head + 1, :width]
+        cen_tok = stats_ref[2, group, head : head + 1, :width]
+        top = jnp.maximum(jnp.max(scores, 0, keepdims=True), top_tok)
+        shift = jnp.exp2(top_tok - top)
+        expo = jnp.exp2(scores - top)
+        total_sum = shift * sum_tok + jnp.sum(expo, 0, keepdims=True)
+        inverse = 1.0 / total_sum
+        centre = inverse * (shift * cen_tok + jnp.sum(expo * dweights, 0, keepdims=True))
+        probs = expo * inverse
+        dscores = (probs * (dweights - centre)).astype(jnp.bfloat16)
+        key_grad = key_grad + dot_nn(dscores, query)
+        val_grad = val_grad + dot_nn(probs.astype(jnp.bfloat16), cot)
+        rows_ref[0, group, head : head + 1, :width] = top + jnp.log(total_sum) * LOG2E
+        rows_ref[1, group, head : head + 1, :width] = centre
+        if head == GROUP:
+            contrib_ref[:, group * HD : (group + 1) * HD] = (key_grad * FACTOR).astype(jnp.bfloat16)
+            contrib_ref[:, (KVH + group) * HD : (KVH + group + 1) * HD] = val_grad.astype(
+                jnp.bfloat16
             )
-            probs = expo * inverse
-            dscores = (probs * (dweights - centre)).astype(jnp.bfloat16)
-            key_grad = key_grad + dot_nn(dscores, query)
-            val_grad = val_grad + dot_nn(probs.astype(jnp.bfloat16), cot)
-            rows_ref[0, group, head : head + 1, :width] = top + jnp.log(total_sum) * LOG2E
-            rows_ref[1, group, head : head + 1, :width] = centre
-        contrib_ref[:, group * HD : (group + 1) * HD] = (key_grad * FACTOR).astype(jnp.bfloat16)
-        contrib_ref[:, (KVH + group) * HD : (KVH + group + 1) * HD] = val_grad.astype(jnp.bfloat16)
 
 
 def rest_kernel(
@@ -241,6 +250,23 @@
     )
 
 
+def hidden_grad_kernel(grad_ref, weight_ref, out_ref):
+    part = dot_nt(grad_ref[...], weight_ref[...]).astype(jnp.bfloat16)
+    out_ref[...] = part.reshape(out_ref.shape)
+
+
+def hidden_grad_part(all_grad, weight, count):
+    total, width = all_grad.shape
+    return call(
+        hidden_grad_kernel,
+        (jax.ShapeDtypeStruct((count, total // count, weight.shape[0]), jnp.bfloat16),),
+        [],
+        [VM] * 2,
+        (all_grad, weight),
+        2 * total * width * weight.shape[0],
+    )[0]
+
+
 def exchange(blocks):
     return lax.all_to_all(blocks, "ctx", 0, 0, tiled=True)
 
@@ -260,7 +286,7 @@
 
 def sum_dp(part, beside):
     sent = part.astype(jnp.bfloat16)
-    near, far, wide = [swap_dp(sent, mask) for mask in (2, 4, 6)]
+    near, far, wide = [swap_dp(sent, mask) for mask in (2, 5, 7)]
     near, far, wide, beside = lax.optimization_barrier((near, far, wide, beside))
     part = (sent.astype(jnp.float32) + near) + (far + wide)
     sent = part.astype(jnp.bfloat16)
@@ -296,10 +322,7 @@
     weight_part = lax.dot_general(
         hidden_cols, all_grad, (((0,), (0,)), ((), ())), preferred_element_type=jnp.float32
     )
-    hidden_part = lax.dot_general(
-        all_grad, beacon_weight, (((1,), (1,)), ((), ())), preferred_element_type=jnp.float32
-    ).astype(jnp.bfloat16)
-    hidden_blocks = exchange(hidden_part.reshape(count, rows, -1))
+    hidden_blocks = exchange(hidden_grad_part(all_grad, beacon_weight, count))
     grad_weight, hidden_blocks = sum_dp(weight_part, hidden_blocks)
     hidden_grad = hidden_blocks.transpose(1, 0, 2).reshape(rows, -1)
     return (

time: 121 us -> 118 us (0.975)
  Pallas kernels: 20.7 us -> 19.2 us
    pallas_call x3 -> x4, Pallas kernels: 20.7 us -> 19.2 us  [call(): pl.pallas_call(kernel, out_shape=outs, in_specs=specs, out_specs=tuple((V...]
  transfers between devices with their start and end apart: 7 -> 7, of which waited for: 7 -> 6; matrix products, arithmetic and copies ran while one was open for 2% -> 1% of each run, Pallas kernels for 9% -> 10%
where the time goes in v6:
time: 118 us; the launch traced here: 116 us
  blocking collectives  46.4 us (39%)
  starting transfers between devices  24.8 us (21%)
  waiting for transfers between devices  20 us (17%)
  Pallas kernels  19.2 us (16%)
  local copies, waits for them, and re-layouts  3.34 us (3%)
    all_to_all x3, blocking collectives, exchange(): return lax.all_to_all(blocks, 'ctx', 0, 0, tiled=True)  46.4 us
    pallas_call x4, Pallas kernels, call(): pl.pallas_call(kernel, out_shape=outs, in_specs=specs, out_specs=tuple((V...  19.2 us
    all_to_all x3, starting transfers between devices, exchange(): return lax.all_to_all(blocks, 'ctx', 0, 0, tiled=True)  15.3 us
    all_to_all x3, waiting for transfers between devices, exchange(): return lax.all_to_all(blocks, 'ctx', 0, 0, tiled=True)  11.8 us
    ppermute x4, starting transfers between devices, swap_dp(): return lax.ppermute(sent, 'dp', pairs).astype(jnp.float32)  9.52 us
    ppermute x4, waiting for transfers between devices, swap_dp(): return lax.ppermute(sent, 'dp', pairs).astype(jnp.float32)  8.12 us
  transfers between devices with their start and end apart: 7, of which 6 were waited for; matrix products, arithmetic and copies ran while one was open for 1% of the time, Pallas kernels for 10%

profile of v6, /device:TPU:2, one launch (start us, length us, event | category | flops | bytes accessed | tf_op | source)
XLA Modules:
  0.0 116.0 jit_solution(8580835814159766858)
XLA Ops:
  0.6 1.1 reshape_squeeze.3
  1.7 0.1 copy.21
  1.8 0.0 copy-start.2
  1.8 14.2 %all_to_all.30 = bf16[32,16,112]{2,1,0:T(8,128)(2,1)S(1)} all-to-all(bf16[32,16,112]{2,1,0:T(8,128)(2,1)S(1)} %copy.21), channel_id=1, replica_groups=mesh['dp'=8,'ctx'=32] {'ctx'}, dimensions={0} | all-to-all | bytes 229376 | tf_op jit(solution)/shard_map/all_to_all | solution.py:271
  16.0 0.0 copy-start.6
  16.0 0.0 copy-done.2
  16.0 0.3 convolution_convert_fusion
  16.3 0.4 copy-done.6
  16.6 0.0 copy-start.4
  16.6 0.0 copy-start.5
  16.6 15.3 %all_to_all.31 = bf16[32,16,512]{2,1,0:T(8,128)(2,1)S(1)} all-to-all(bf16[32,16,512]{2,1,0:T(8,128)(2,1)S(1)} %bitcast.47), channel_id=1, replica_groups=mesh['dp'=8,'ctx'=32] {'ctx'}, dimensions={0} | all-to-all | bytes 1048576 | tf_op jit(solution)/shard_map/all_to_all | solution.py:271
  31.9 0.0 copy-start.1
  31.9 0.1 reduce_sum.24
  32.0 0.0 copy-start
  32.0 0.9 broadcast_in_dim.27
  32.9 0.0 copy-start.3
  32.9 5.2 %all-to-all-start.2 = ((bf16[32,16,512]{2,1,0:T(8,128)(2,1)}), bf16[32,16,512]{2,1,0:T(8,128)(2,1)S(1)}, u32[]{:S(2)}, u32[]{:S(2)}) async-start(bf16[32,16,512]{2,1,0:T(8,128)(2,1)} %broadcast_in_dim.27), calls=%async_computation.2 | async-start | bytes 1048576 | tf_op jit(solution)/shard_map/all_to_all | solution.py:271
  38.1 0.0 copy-done.4
  38.1 0.0 copy-done.5
  38.1 0.0 copy-done.1
  38.1 0.0 copy-done
  38.1 0.0 copy-done.3
  38.1 1.5 %shard_map.126.stats_ref = f32[3,2,8,256]{3,2,1,0:T(8,128)S(1)} custom-call(bf16[256,1792]{1,0:T(8,128)(2,1)S(1)} %bitcast.31, bf16[16,1792]{1,0:T(8,128)(2,1)S(1)} %bitcast.41, bf16[256,512]{1,0:T(8,128)(2,1)S(1)} %bitcast.39, bf16[256,1792]{1,0:T(8,128)(2,1)S(1)} %bitcast.34, bf16[16,1792]{1,0:T(8,128)(2,1)S(1)} %bitcast.44), custom_call_target="tpu_custom_call" | custom-call | flops 536870912 | bytes 4194304 | tf_op jit(solution)/shard_map/pallas_call | solution.py:194
  39.6 9.0 %all-to-all-done.2 = bf16[32,16,512]{2,1,0:T(8,128)(2,1)S(1)} async-done(((bf16[32,16,512]{2,1,0:T(8,128)(2,1)}), bf16[32,16,512]{2,1,0:T(8,128)(2,1)S(1)}, u32[]{:S(2)}, u32[]{:S(2)}) %all-to-all-start.2) | async-done | bytes 524320 | tf_op jit(solution)/shard_map/all_to_all | solution.py:271
  48.7 7.1 %shard_map.127 = (bf16[512,512]{1,0:T(8,128)(2,1)}, f32[2,2,8,256]{3,2,1,0:T(8,128)S(1)}) custom-call(s32[1]{0:T(128)} %bitcast.pos_ref, bf16[256,1792]{1,0:T(8,128)(2,1)S(1)} %bitcast.32, bf16[16,1792]{1,0:T(8,128)(2,1)S(1)} %bitcast.42, bf16[512,512]{1,0:T(8,128)(2,1)S(1)} %bitcast.37, bf16[256,1792]{1,0:T(8,128)(2,1)S(1)} %bitcast.35, ...), custom_call_target="tpu_custom_call" | custom-call | flops 2147483648 | bytes 4194304 | tf_op jit(solution)/shard_map/pallas_call | solution.py:194
  55.8 5.1 %all-to-all-start.3 = ((bf16[32,16,512]{2,1,0:T(8,128)(2,1)}), bf16[32,16,512]{2,1,0:T(8,128)(2,1)S(1)}, u32[]{:S(2)}, u32[]{:S(2)}) async-start(bf16[32,16,512]{2,1,0:T(8,128)(2,1)} %bitcast.10), calls=%async_computation.3 | async-start | bytes 1048576 | tf_op jit(solution)/shard_map/all_to_all | solution.py:271
  60.9 9.6 %shard_map.128 = (bf16[256,1792]{1,0:T(8,128)(2,1)}, bf16[16,1792]{1,0:T(8,128)(2,1)}, bf16[256,1792]{1,0:T(8,128)(2,1)}, bf16[16,1792]{1,0:T(8,128)(2,1)}, bf16[256,512]{1,0:T(8,128)(2,1)}) custom-call(s32[1]{0:T(128)} %bitcast.pos_ref, bf16[256,1792]{1,0:T(8,128)(2,1)S(1)} %bitcast.33, bf16[16,1792]{1,0:T(8,128)(2,1)S(1)} %bitcast.43, ...), custom_call_target="tpu_custom_call" | custom-call | flops 4026531840 | bytes 4194304 | tf_op jit(solution)/shard_map/pallas_call | solution.py:194
  70.5 1.0 all-to-all-done.3
  71.4 0.1 reduce_sum.25
  71.5 0.1 broadcast_in_dim.33
  71.6 0.0 copy-start.7
  71.6 16.9 %all_to_all.32 = bf16[32,16,512]{2,1,0:T(8,128)(2,1)S(1)} all-to-all(bf16[32,16,512]{2,1,0:T(8,128)(2,1)S(1)} %broadcast_in_dim.33), channel_id=1, replica_groups=mesh['dp'=8,'ctx'=32] {'ctx'}, dimensions={0} | all-to-all | bytes 1048576 | tf_op jit(solution)/shard_map/all_to_all | solution.py:271
  88.5 0.0 copy-done.7
  88.5 0.3 fusion.1
  88.8 6.0 %collective-permute-start.2 = (bf16[112,512]{1,0:T(8,128)(2,1)S(1)}, bf16[112,512]{1,0:T(8,128)(2,1)S(1)}, u32[]{:S(2)}, u32[]{:S(2)}) collective-permute-start(bf16[112,512]{1,0:T(8,128)(2,1)S(1)} %fusion.1), channel_id=1, source_target_pairs={{0,224},{32,192},{64,160},{96,128},{128,96},{160,64},{192,32},{224... | collective-permute-start | bytes 344072 | tf_op jit(solution)/shard_map/ppermute | solution.py:284
  94.8 1.0 collective-permute-start.1
  95.7 1.5 %collective-permute-start = (bf16[112,512]{1,0:T(8,128)(2,1)S(1)}, bf16[112,512]{1,0:T(8,128)(2,1)S(1)}, u32[]{:S(2)}, u32[]{:S(2)}) collective-permute-start(bf16[112,512]{1,0:T(8,128)(2,1)S(1)} %fusion.1), channel_id=1, source_target_pairs={{0,64},{32,96},{64,0},{96,32},{128,192},{160,224},{192,128},{224,1... | collective-permute-start | bytes 344072 | tf_op jit(solution)/shard_map/ppermute | solution.py:284
  97.2 0.9 shard_map.129
  98.2 5.0 %all-to-all-start.5 = ((bf16[32,16,112]{2,1,0:T(8,128)(2,1)}), bf16[32,16,112]{2,1,0:T(8,128)(2,1)S(1)}, u32[]{:S(2)}, u32[]{:S(2)}) async-start(bf16[32,16,112]{2,1,0:T(8,128)(2,1)} %shard_map.129), calls=%async_computation.5 | async-start | bytes 262144 | tf_op jit(solution)/shard_map/all_to_all | solution.py:271
  103.2 0.0 collective-permute-done.2
  103.2 2.3 %collective-permute-done.1 = bf16[112,512]{1,0:T(8,128)(2,1)S(1)} collective-permute-done((bf16[112,512]{1,0:T(8,128)(2,1)S(1)}, bf16[112,512]{1,0:T(8,128)(2,1)S(1)}, u32[]{:S(2)}, u32[]{:S(2)}) %collective-permute-start.1) | collective-permute-done | bytes 114720 | tf_op jit(solution)/shard_map/ppermute | solution.py:284
  105.5 2.6 %collective-permute-done = bf16[112,512]{1,0:T(8,128)(2,1)S(1)} collective-permute-done((bf16[112,512]{1,0:T(8,128)(2,1)S(1)}, bf16[112,512]{1,0:T(8,128)(2,1)S(1)}, u32[]{:S(2)}, u32[]{:S(2)}) %collective-permute-start) | collective-permute-done | bytes 114720 | tf_op jit(solution)/shard_map/ppermute | solution.py:284
  108.1 1.8 %all-to-all-done.5 = bf16[32,16,112]{2,1,0:T(8,128)(2,1)S(1)} async-done(((bf16[32,16,112]{2,1,0:T(8,128)(2,1)}), bf16[32,16,112]{2,1,0:T(8,128)(2,1)S(1)}, u32[]{:S(2)}, u32[]{:S(2)}) %all-to-all-start.5) | async-done | bytes 114720 | tf_op jit(solution)/shard_map/all_to_all | solution.py:271
  109.9 0.1 add_convert_fusion
  110.0 1.1 collective-permute-start.3
  111.1 0.8 broadcast_in_dim_reshape.3
  112.0 3.3 %collective-permute-done.3 = bf16[112,512]{1,0:T(8,128)(2,1)S(1)} collective-permute-done((bf16[112,512]{1,0:T(8,128)(2,1)S(1)}, bf16[112,512]{1,0:T(8,128)(2,1)S(1)}, u32[]{:S(2)}, u32[]{:S(2)}) %collective-permute-start.3) | collective-permute-done | bytes 114720 | tf_op jit(solution)/shard_map/ppermute | solution.py:284
  115.3 0.7 convert_add_fusion
  (4 shorter events, 0.1 us)
Async XLA Ops:
  1.8 14.2 %copy-start.2 = (bf16[112,512]{1,0:T(8,128)(2,1)S(1)}, bf16[112,512]{1,0:T(8,128)(2,1)}, u32[]{:S(2)}) copy-start(bf16[112,512]{1,0:T(8,128)(2,1)} %weight_ref.1) | copy-start | bytes 344068
  16.0 0.7 copy-start.6
  16.6 21.4 %copy-start.4 = (bf16[1,16,1792]{2,1,0:T(8,128)(2,1)S(1)}, bf16[1,16,1792]{2,1,0:T(8,128)(2,1)}, u32[]{:S(2)}) copy-start(bf16[1,16,1792]{2,1,0:T(8,128)(2,1)} %param.9) | copy-start | bytes 172036
  16.6 21.4 %copy-start.5 = (bf16[1,16,1792]{2,1,0:T(8,128)(2,1)S(1)}, bf16[1,16,1792]{2,1,0:T(8,128)(2,1)}, u32[]{:S(2)}) copy-start(bf16[1,16,1792]{2,1,0:T(8,128)(2,1)} %param.13) | copy-start | bytes 172036
  31.9 6.2 %copy-start.1 = (bf16[1,256,1792]{2,1,0:T(8,128)(2,1)S(1)}, bf16[1,256,1792]{2,1,0:T(8,128)(2,1)}, u32[]{:S(2)}) copy-start(bf16[1,256,1792]{2,1,0:T(8,128)(2,1)} %param.12) | copy-start | bytes 2752516
  32.0 6.1 %copy-start = (bf16[1,256,1792]{2,1,0:T(8,128)(2,1)S(1)}, bf16[1,256,1792]{2,1,0:T(8,128)(2,1)}, u32[]{:S(2)}) copy-start(bf16[1,256,1792]{2,1,0:T(8,128)(2,1)} %param.7) | copy-start | bytes 2752516
  32.9 5.2 %copy-start.3 = (bf16[1,256,512]{2,1,0:T(8,128)(2,1)S(1)}, bf16[1,256,512]{2,1,0:T(8,128)(2,1)}, u32[]{:S(2)}) copy-start(bf16[1,256,512]{2,1,0:T(8,128)(2,1)} %param.8) | copy-start | bytes 786436
  32.9 15.8 %all-to-all-start.2 = ((bf16[32,16,512]{2,1,0:T(8,128)(2,1)}), bf16[32,16,512]{2,1,0:T(8,128)(2,1)S(1)}, u32[]{:S(2)}, u32[]{:S(2)}) async-start(bf16[32,16,512]{2,1,0:T(8,128)(2,1)} %broadcast_in_dim.27), calls=%async_computation.2 | async-start | bytes 1048576 | tf_op jit(solution)/shard_map/all_to_all | solution.py:271
  55.8 15.7 %all-to-all-start.3 = ((bf16[32,16,512]{2,1,0:T(8,128)(2,1)}), bf16[32,16,512]{2,1,0:T(8,128)(2,1)S(1)}, u32[]{:S(2)}, u32[]{:S(2)}) async-start(bf16[32,16,512]{2,1,0:T(8,128)(2,1)} %bitcast.10), calls=%async_computation.3 | async-start | bytes 1048576 | tf_op jit(solution)/shard_map/all_to_all | solution.py:271
  71.6 16.9 %copy-start.7 = (bf16[32,16,112]{2,1,0:T(8,128)(2,1)S(1)}, bf16[32,16,112]{2,1,0:T(8,128)(2,1)}, u32[]{:S(2)}) copy-start(bf16[32,16,112]{2,1,0:T(8,128)(2,1)} %copy-done.6) | copy-start | bytes 344068
  88.8 14.4 %collective-permute-start.2 = (bf16[112,512]{1,0:T(8,128)(2,1)S(1)}, bf16[112,512]{1,0:T(8,128)(2,1)S(1)}, u32[]{:S(2)}, u32[]{:S(2)}) collective-permute-start(bf16[112,512]{1,0:T(8,128)(2,1)S(1)} %fusion.1), channel_id=1, source_target_pairs={{0,224},{32,192},{64,160},{96,128},{128,96},{160,64},{192,32},{224... | collective-permute-start | bytes 344072 | tf_op jit(solution)/shard_map/ppermute | solution.py:284
  94.8 10.7 %collective-permute-start.1 = (bf16[112,512]{1,0:T(8,128)(2,1)S(1)}, bf16[112,512]{1,0:T(8,128)(2,1)S(1)}, u32[]{:S(2)}, u32[]{:S(2)}) collective-permute-start(bf16[112,512]{1,0:T(8,128)(2,1)S(1)} %fusion.1), channel_id=1, source_target_pairs={{0,160},{32,128},{64,224},{96,192},{128,32},{160,0},{192,96},{224,... | collective-permute-start | bytes 344072 | tf_op jit(solution)/shard_map/ppermute | solution.py:284
  95.7 12.3 %collective-permute-start = (bf16[112,512]{1,0:T(8,128)(2,1)S(1)}, bf16[112,512]{1,0:T(8,128)(2,1)S(1)}, u32[]{:S(2)}, u32[]{:S(2)}) collective-permute-start(bf16[112,512]{1,0:T(8,128)(2,1)S(1)} %fusion.1), channel_id=1, source_target_pairs={{0,64},{32,96},{64,0},{96,32},{128,192},{160,224},{192,128},{224,1... | collective-permute-start | bytes 344072 | tf_op jit(solution)/shard_map/ppermute | solution.py:284
  98.2 11.7 %all-to-all-start.5 = ((bf16[32,16,112]{2,1,0:T(8,128)(2,1)}), bf16[32,16,112]{2,1,0:T(8,128)(2,1)S(1)}, u32[]{:S(2)}, u32[]{:S(2)}) async-start(bf16[32,16,112]{2,1,0:T(8,128)(2,1)} %shard_map.129), calls=%async_computation.5 | async-start | bytes 262144 | tf_op jit(solution)/shard_map/all_to_all | solution.py:271
  110.0 5.3 %collective-permute-start.3 = (bf16[112,512]{1,0:T(8,128)(2,1)S(1)}, bf16[112,512]{1,0:T(8,128)(2,1)S(1)}, u32[]{:S(2)}, u32[]{:S(2)}) collective-permute-start(bf16[112,512]{1,0:T(8,128)(2,1)S(1)} %add_convert_fusion), channel_id=1, source_target_pairs={{0,32},{32,0},{64,96},{96,64},{128,160},{160,128},{192,224},{224,1... | collective-permute-start | bytes 344072 | tf_op jit(solution)/shard_map/ppermute | solution.py:284

commit v7 on v6

--- a/solution.py
+++ b/solution.py
@@ -136,54 +136,61 @@
     bias_ref[...] = prefix_bias(total, span, start, None)
     bbias_ref[...] = prefix_bias(total, HD, start, count)
     tbias_ref[...] = token_bias(span)
+    jobs = [(group, head) for group in range(KVH) for head in range(GROUP + 1)]
+    sides = []
     for group in range(KVH):
         key_cols = slice(group * HD, (group + 1) * HD)
         val_cols = slice((KVH + group) * HD, (KVH + group + 1) * HD)
-        sides = []
-        for ref in (bkv_ref, kv_ref):
-            keys = ref[:, key_cols]
-            vals = ref[:, val_cols]
-            sides.append((keys, vals, keys.T, vals.T))
-        key_grad = jnp.zeros((span, HD), jnp.float32)
-        val_grad = jnp.zeros((span, HD), jnp.float32)
-        for head in range(GROUP + 1):
-            query = head_rows(q_ref, bq_ref, group, head)
-            cot = head_rows(c_ref, bc_ref, group, head)
-            width = query.shape[0]
-            lse = rows_ref[0, group, head : head + 1, :width]
-            centre = rows_ref[1, group, head : head + 1, :width]
-            out = None
-            dquery = None
-            for side in range(2):
-                keys, vals, keys_t, vals_t = sides[side]
-                scores = dot_nt(keys, query) * (FACTOR * LOG2E) - lse
-                if side == 0:
-                    scores = scores + (bias_ref if head < GROUP else bbias_ref)[...]
-                elif head < GROUP:
-                    scores = scores + tbias_ref[...]
-                probs = jnp.exp2(scores)
-                dscores = (probs * (dot_nt(vals, cot) - centre)).astype(jnp.bfloat16)
-                weights = probs.astype(jnp.bfloat16)
-                out_part = dot_nn(vals_t, weights)
-                dq_part = dot_nn(keys_t, dscores)
-                out = out_part if out is None else out + out_part
-                dquery = dq_part if dquery is None else dquery + dq_part
-                if side == 1:
-                    key_grad = key_grad + dot_nn(dscores, query)
-                    val_grad = val_grad + dot_nn(weights, cot)
-            out = out.T.astype(jnp.bfloat16)
-            dquery = (dquery * FACTOR).T.astype(jnp.bfloat16)
-            if head < GROUP:
-                at = (group * GROUP + head) * HD
-                out_ref[:, at : at + HD] = out
-                dq_ref[:, at : at + HD] = dquery
-            else:
-                for each in range(GROUP):
-                    at = (group * GROUP + each) * HD
-                    bout_ref[:, at : at + HD] = out[each * count : (each + 1) * count]
-                    bdq_ref[:, at : at + HD] = dquery[each * count : (each + 1) * count]
-        dkv_ref[:, key_cols] = (key_grad * FACTOR).astype(jnp.bfloat16)
-        dkv_ref[:, val_cols] = val_grad.astype(jnp.bfloat16)
+        both = [(ref[:, key_cols], ref[:, val_cols]) for ref in (bkv_ref, kv_ref)]
+        sides.append([(keys, vals, keys.T, vals.T) for keys, vals in both])
+
+    def products(group, head):
+        query = head_rows(q_ref, bq_ref, group, head)
+        cot = head_rows(c_ref, bc_ref, group, head)
+        pairs = [(dot_nt(side[0], query), dot_nt(side[1], cot)) for side in sides[group]]
+        return query, cot, pairs
+
+    ahead = products(*jobs[0])
+    for job, (group, head) in enumerate(jobs):
+        query, cot, pairs = ahead
+        if job + 1 < len(jobs):
+            ahead = products(*jobs[job + 1])
+        if head == 0:
+            key_grad = jnp.zeros((span, HD), jnp.float32)
+            val_grad = jnp.zeros((span, HD), jnp.float32)
+        width = query.shape[0]
+        lse = rows_ref[0, group, head : head + 1, :width]
+        centre = rows_ref[1, group, head : head + 1, :width]
+        out = jnp.zeros((HD, width), jnp.float32)
+        dquery = jnp.zeros((HD, width), jnp.float32)
+        for side in range(2):
+            _, _, keys_t, vals_t = sides[group][side]
+            scores = pairs[side][0] * (FACTOR * LOG2E) - lse
+            if side == 0:
+                scores = scores + (bias_ref if head < GROUP else bbias_ref)[...]
+            elif head < GROUP:
+                scores = scores + tbias_ref[...]
+            probs = jnp.exp2(scores)
+            dscores = (probs * (pairs[side][1] - centre)).astype(jnp.bfloat16)
+            weights = probs.astype(jnp.bfloat16)
+            out = out + dot_nn(vals_t, weights)
+            dquery = dquery + dot_nn(keys_t, dscores)
+            if side == 1:
+                key_grad = key_grad + dot_nn(dscores, query)
+                val_grad = val_grad + dot_nn(weights, cot)
+        out = out.T.astype(jnp.bfloat16)
+        dquery = (dquery * FACTOR).T.astype(jnp.bfloat16)
+        if head < GROUP:
+            at = (group * GROUP + head) * HD
+            out_ref[:, at : at + HD] = out
+            dq_ref[:, at : at + HD] = dquery
+            continue
+        for each in range(GROUP):
+            at = (group * GROUP + each) * HD
+            bout_ref[:, at : at + HD] = out[each * count : (each + 1) * count]
+            bdq_ref[:, at : at + HD] = dquery[each * count : (each + 1) * count]
+        dkv_ref[:, group * HD : (group + 1) * HD] = (key_grad * FACTOR).astype(jnp.bfloat16)
+        dkv_ref[:, (KVH + group) * HD : (KVH + group + 1) * HD] = val_grad.astype(jnp.bfloat16)
 
 
 VM = pl.BlockSpec(memory_space=pltpu.VMEM)
@@ -267,6 +274,27 @@
     )[0]
 
 
+def weight_grad_kernel(hidden_ref, grad_ref, out_ref):
+    rows = grad_ref.shape[0]
+    out_ref[...] = lax.dot_general(
+        hidden_ref[...].reshape(rows, -1),
+        grad_ref[...],
+        (((0,), (0,)), ((), ())),
+        preferred_element_type=jnp.float32,
+    ).astype(jnp.bfloat16)
+
+
+def weight_grad_part(hidden_blocks, all_grad):
+    return call(
+        weight_grad_kernel,
+        (jax.ShapeDtypeStruct((hidden_blocks.shape[-1], all_grad.shape[1]), jnp.bfloat16),),
+        [],
+        [VM] * 2,
+        (hidden_blocks, all_grad),
+        10**10,
+    )[0]
+
+
 def exchange(blocks):
     return lax.all_to_all(blocks, "ctx", 0, 0, tiled=True)
 
@@ -285,9 +313,9 @@
 
 
 def sum_dp(part, beside):
-    sent = part.astype(jnp.bfloat16)
+    sent = part
     near, far, wide = [swap_dp(sent, mask) for mask in (2, 5, 7)]
-    near, far, wide, beside = lax.optimization_barrier((near, far, wide, beside))
+    sent, beside = lax.optimization_barrier((sent, beside))
     part = (sent.astype(jnp.float32) + near) + (far + wide)
     sent = part.astype(jnp.bfloat16)
     return sent.astype(jnp.float32) + swap_dp(sent, 1), beside
@@ -319,10 +347,10 @@
     tokens_out, beacons_out, query_grad, beacon_qgrad, token_kvgrad = others
     own_grad = jnp.sum(arrived.astype(jnp.float32), 0).astype(jnp.bfloat16)
     all_grad = gather_rows(own_grad, count)
-    weight_part = lax.dot_general(
-        hidden_cols, all_grad, (((0,), (0,)), ((), ())), preferred_element_type=jnp.float32
-    )
-    hidden_blocks = exchange(hidden_grad_part(all_grad, beacon_weight, count))
+    hidden_part = hidden_grad_part(all_grad, beacon_weight, count)
+    hidden_part, late_grad = lax.optimization_barrier((hidden_part, all_grad))
+    weight_part = weight_grad_part(hidden_cols, late_grad)
+    hidden_blocks = exchange(hidden_part)
     grad_weight, hidden_blocks = sum_dp(weight_part, hidden_blocks)
     hidden_grad = hidden_blocks.transpose(1, 0, 2).reshape(rows, -1)
     return (

time: 118 us -> 116 us (0.983)
  blocking collectives: 46.4 us -> 56 us
  waiting for transfers between devices: 20 us -> 15.5 us
  starting transfers between devices: 24.8 us -> 20.4 us
  Pallas kernels: 19.2 us -> 16.7 us
    all_to_all x3 -> x4, blocking collectives: 46.4 us -> 56 us  [exchange(): return lax.all_to_all(blocks, 'ctx', 0, 0, tiled=True)]
    ppermute x4, waiting for transfers between devices: 8.12 us -> 3.32 us  [swap_dp(): return lax.ppermute(sent, 'dp', pairs).astype(jnp.float32)]
    all_to_all x3 -> x2, starting transfers between devices: 15.3 us -> 10.9 us  [exchange(): return lax.all_to_all(blocks, 'ctx', 0, 0, tiled=True)]
    pallas_call x4 -> x5, Pallas kernels: 19.2 us -> 16.7 us  [call(): pl.pallas_call(kernel, out_shape=outs, in_specs=specs, out_specs=tuple((V...]
    all_to_all x3 -> x2, waiting for transfers between devices: 11.8 us -> 12.2 us  [exchange(): return lax.all_to_all(blocks, 'ctx', 0, 0, tiled=True)]
  transfers between devices with their start and end apart: 7 -> 6, of which waited for: 6 -> 3; matrix products, arithmetic and copies ran while one was open for 1% -> 1% of each run, Pallas kernels for 10% -> 8%
where the time goes in v7:
time: 116 us; the launch traced here: 115 us
  blocking collectives  56 us (48%)
  starting transfers between devices  20.4 us (18%)
  Pallas kernels  16.7 us (14%)
  waiting for transfers between devices  15.5 us (13%)
  local copies, waits for them, and re-layouts  2.97 us (3%)
  other arithmetic  2 us (2%)
    all_to_all x4, blocking collectives, exchange(): return lax.all_to_all(blocks, 'ctx', 0, 0, tiled=True)  56 us
    pallas_call x5, Pallas kernels, call(): pl.pallas_call(kernel, out_shape=outs, in_specs=specs, out_specs=tuple((V...  16.7 us
    all_to_all x2, waiting for transfers between devices, exchange(): return lax.all_to_all(blocks, 'ctx', 0, 0, tiled=True)  12.2 us
    all_to_all x2, starting transfers between devices, exchange(): return lax.all_to_all(blocks, 'ctx', 0, 0, tiled=True)  10.9 us
    ppermute x4, starting transfers between devices, swap_dp(): return lax.ppermute(sent, 'dp', pairs).astype(jnp.float32)  9.53 us
    ppermute x4, waiting for transfers between devices, swap_dp(): return lax.ppermute(sent, 'dp', pairs).astype(jnp.float32)  3.32 us
  transfers between devices with their start and end apart: 6, of which 3 were waited for; matrix products, arithmetic and copies ran while one was open for 1% of the time, Pallas kernels for 8%

profile of v7, /device:TPU:2, one launch (start us, length us, event | category | flops | bytes accessed | tf_op | source)
XLA Modules:
  0.0 114.6 jit_solution(31419667916188168)
XLA Ops:
  0.6 1.1 reshape_squeeze.3
  1.7 0.1 copy.18
  1.8 0.0 copy-start.2
  1.8 14.2 %all_to_all.30 = bf16[32,16,112]{2,1,0:T(8,128)(2,1)S(1)} all-to-all(bf16[32,16,112]{2,1,0:T(8,128)(2,1)S(1)} %bitcast.44), channel_id=1, replica_groups=mesh['dp'=8,'ctx'=32] {'ctx'}, dimensions={0} | all-to-all | bytes 229376 | tf_op jit(solution)/shard_map/all_to_all | solution.py:299
  16.0 0.0 copy-done.2
  16.0 0.3 convolution_convert_fusion
  16.3 0.0 copy-start.4
  16.3 0.0 copy-start.5
  16.3 15.3 %all_to_all.31 = bf16[32,16,512]{2,1,0:T(8,128)(2,1)S(1)} all-to-all(bf16[32,16,512]{2,1,0:T(8,128)(2,1)S(1)} %bitcast.42), channel_id=1, replica_groups=mesh['dp'=8,'ctx'=32] {'ctx'}, dimensions={0} | all-to-all | bytes 1048576 | tf_op jit(solution)/shard_map/all_to_all | solution.py:299
  31.6 0.0 copy-start.1
  31.6 0.1 reduce_sum.24
  31.7 0.0 copy-start
  31.7 0.9 broadcast_in_dim.27
  32.5 0.0 copy-start.3
  32.5 5.2 %all-to-all-start.2 = ((bf16[32,16,512]{2,1,0:T(8,128)(2,1)}), bf16[32,16,512]{2,1,0:T(8,128)(2,1)S(1)}, u32[]{:S(2)}, u32[]{:S(2)}) async-start(bf16[32,16,512]{2,1,0:T(8,128)(2,1)} %broadcast_in_dim.27), calls=%async_computation.2 | async-start | bytes 1048576 | tf_op jit(solution)/shard_map/all_to_all | solution.py:299
  37.7 0.0 copy-done.4
  37.7 0.0 copy-done.5
  37.7 0.0 copy-done.1
  37.7 0.0 copy-done
  37.8 0.0 copy-done.3
  37.8 1.5 %shard_map.126.stats_ref = f32[3,2,8,256]{3,2,1,0:T(8,128)S(1)} custom-call(bf16[256,1792]{1,0:T(8,128)(2,1)S(1)} %bitcast.24, bf16[16,1792]{1,0:T(8,128)(2,1)S(1)} %bitcast.36, bf16[256,512]{1,0:T(8,128)(2,1)S(1)} %bitcast.34, bf16[256,1792]{1,0:T(8,128)(2,1)S(1)} %bitcast.27, bf16[16,1792]{1,0:T(8,128)(2,1)S(1)} %bitcast.39), custom_call_target="tpu_custom_call" | custom-call | flops 536870912 | bytes 4194304 | tf_op jit(solution)/shard_map/pallas_call | solution.py:201
  39.3 9.0 %all-to-all-done.2 = bf16[32,16,512]{2,1,0:T(8,128)(2,1)S(1)} async-done(((bf16[32,16,512]{2,1,0:T(8,128)(2,1)}), bf16[32,16,512]{2,1,0:T(8,128)(2,1)S(1)}, u32[]{:S(2)}, u32[]{:S(2)}) %all-to-all-start.2) | async-done | bytes 524320 | tf_op jit(solution)/shard_map/all_to_all | solution.py:299
  48.3 7.1 %shard_map.127 = (bf16[512,512]{1,0:T(8,128)(2,1)}, f32[2,2,8,256]{3,2,1,0:T(8,128)S(1)}) custom-call(s32[1]{0:T(128)} %bitcast.pos_ref, bf16[256,1792]{1,0:T(8,128)(2,1)S(1)} %bitcast.25, bf16[16,1792]{1,0:T(8,128)(2,1)S(1)} %bitcast.37, bf16[512,512]{1,0:T(8,128)(2,1)S(1)} %bitcast.30, bf16[256,1792]{1,0:T(8,128)(2,1)S(1)} %bitcast.28, ...), custom_call_target="tpu_custom_call" | custom-call | flops 2147483648 | bytes 4194304 | tf_op jit(solution)/shard_map/pallas_call | solution.py:201
  55.4 5.7 %all-to-all-start.3 = ((bf16[32,16,512]{2,1,0:T(8,128)(2,1)}), bf16[32,16,512]{2,1,0:T(8,128)(2,1)}, u32[]{:S(2)}, u32[]{:S(2)}) async-start(bf16[32,16,512]{2,1,0:T(8,128)(2,1)} %bitcast.10), calls=%async_computation.3 | async-start | bytes 1048576 | tf_op jit(solution)/shard_map/all_to_all | solution.py:299
  61.2 7.5 %shard_map.128 = (bf16[256,1792]{1,0:T(8,128)(2,1)}, bf16[16,1792]{1,0:T(8,128)(2,1)}, bf16[256,1792]{1,0:T(8,128)(2,1)}, bf16[16,1792]{1,0:T(8,128)(2,1)}, bf16[256,512]{1,0:T(8,128)(2,1)}) custom-call(s32[1]{0:T(128)} %bitcast.pos_ref, bf16[256,1792]{1,0:T(8,128)(2,1)S(1)} %bitcast.26, bf16[16,1792]{1,0:T(8,128)(2,1)S(1)} %bitcast.38, ...), custom_call_target="tpu_custom_call" | custom-call | flops 4026531840 | bytes 4194304 | tf_op jit(solution)/shard_map/pallas_call | solution.py:201
  68.7 3.1 %all-to-all-done.3 = bf16[32,16,512]{2,1,0:T(8,128)(2,1)} async-done(((bf16[32,16,512]{2,1,0:T(8,128)(2,1)}), bf16[32,16,512]{2,1,0:T(8,128)(2,1)}, u32[]{:S(2)}, u32[]{:S(2)}) %all-to-all-start.3) | async-done | bytes 524320 | tf_op jit(solution)/shard_map/all_to_all | solution.py:299
  71.8 1.1 reduce_sum.25
  72.9 0.1 broadcast_in_dim.33
  73.0 15.2 %all_to_all.32 = bf16[32,16,512]{2,1,0:T(8,128)(2,1)S(1)} all-to-all(bf16[32,16,512]{2,1,0:T(8,128)(2,1)S(1)} %broadcast_in_dim.33), channel_id=1, replica_groups=mesh['dp'=8,'ctx'=32] {'ctx'}, dimensions={0} | all-to-all | bytes 1048576 | tf_op jit(solution)/shard_map/all_to_all | solution.py:299
  88.2 0.3 shard_map.129
  88.5 0.2 shard_map.130
  88.7 6.0 %collective-permute-start.2 = (bf16[112,512]{1,0:T(8,128)(2,1)S(1)}, bf16[112,512]{1,0:T(8,128)(2,1)S(1)}, u32[]{:S(2)}, u32[]{:S(2)}) collective-permute-start(bf16[112,512]{1,0:T(8,128)(2,1)S(1)} %shard_map.130), channel_id=1, source_target_pairs={{0,224},{32,192},{64,160},{96,128},{128,96},{160,64},{192,32},{224... | collective-permute-start | bytes 344072 | tf_op jit(solution)/shard_map/ppermute | solution.py:312
  94.7 1.0 collective-permute-start.1
  95.7 1.5 %collective-permute-start = (bf16[112,512]{1,0:T(8,128)(2,1)S(1)}, bf16[112,512]{1,0:T(8,128)(2,1)S(1)}, u32[]{:S(2)}, u32[]{:S(2)}) collective-permute-start(bf16[112,512]{1,0:T(8,128)(2,1)S(1)} %shard_map.130), channel_id=1, source_target_pairs={{0,64},{32,96},{64,0},{96,32},{128,192},{160,224},{192,128},{224,1... | collective-permute-start | bytes 344072 | tf_op jit(solution)/shard_map/ppermute | solution.py:312
  97.2 11.3 %all_to_all.33 = bf16[32,16,112]{2,1,0:T(8,128)(2,1)S(1)} all-to-all(bf16[32,16,112]{2,1,0:T(8,128)(2,1)S(1)} %shard_map.129), channel_id=1, replica_groups=mesh['dp'=8,'ctx'=32] {'ctx'}, dimensions={0} | all-to-all | bytes 229376 | tf_op jit(solution)/shard_map/all_to_all | solution.py:299
  108.5 0.0 collective-permute-done.2
  108.5 0.0 collective-permute-done.1
  108.5 0.0 collective-permute-done
  108.5 0.1 add_convert_fusion
  108.6 1.1 collective-permute-start.3
  109.7 0.8 broadcast_in_dim_reshape.3
  110.6 3.3 %collective-permute-done.3 = bf16[112,512]{1,0:T(8,128)(2,1)S(1)} collective-permute-done((bf16[112,512]{1,0:T(8,128)(2,1)S(1)}, bf16[112,512]{1,0:T(8,128)(2,1)S(1)}, u32[]{:S(2)}, u32[]{:S(2)}) %collective-permute-start.3) | collective-permute-done | bytes 114720 | tf_op jit(solution)/shard_map/ppermute | solution.py:312
  113.9 0.7 convert_add_fusion
  (1 shorter events, 0.0 us)
Async XLA Ops:
  1.8 14.2 %copy-start.2 = (bf16[112,512]{1,0:T(8,128)(2,1)S(1)}, bf16[112,512]{1,0:T(8,128)(2,1)}, u32[]{:S(2)}) copy-start(bf16[112,512]{1,0:T(8,128)(2,1)} %weight_ref.1) | copy-start | bytes 344068
  16.3 21.4 %copy-start.4 = (bf16[1,16,1792]{2,1,0:T(8,128)(2,1)S(1)}, bf16[1,16,1792]{2,1,0:T(8,128)(2,1)}, u32[]{:S(2)}) copy-start(bf16[1,16,1792]{2,1,0:T(8,128)(2,1)} %param.9) | copy-start | bytes 172036
  16.3 21.4 %copy-start.5 = (bf16[1,16,1792]{2,1,0:T(8,128)(2,1)S(1)}, bf16[1,16,1792]{2,1,0:T(8,128)(2,1)}, u32[]{:S(2)}) copy-start(bf16[1,16,1792]{2,1,0:T(8,128)(2,1)} %param.13) | copy-start | bytes 172036
  31.6 6.2 %copy-start.1 = (bf16[1,256,1792]{2,1,0:T(8,128)(2,1)S(1)}, bf16[1,256,1792]{2,1,0:T(8,128)(2,1)}, u32[]{:S(2)}) copy-start(bf16[1,256,1792]{2,1,0:T(8,128)(2,1)} %param.12) | copy-start | bytes 2752516
  31.7 6.1 %copy-start = (bf16[1,256,1792]{2,1,0:T(8,128)(2,1)S(1)}, bf16[1,256,1792]{2,1,0:T(8,128)(2,1)}, u32[]{:S(2)}) copy-start(bf16[1,256,1792]{2,1,0:T(8,128)(2,1)} %param.7) | copy-start | bytes 2752516
  32.5 5.2 %copy-start.3 = (bf16[1,256,512]{2,1,0:T(8,128)(2,1)S(1)}, bf16[1,256,512]{2,1,0:T(8,128)(2,1)}, u32[]{:S(2)}) copy-start(bf16[1,256,512]{2,1,0:T(8,128)(2,1)} %param.8) | copy-start | bytes 786436
  32.5 15.8 %all-to-all-start.2 = ((bf16[32,16,512]{2,1,0:T(8,128)(2,1)}), bf16[32,16,512]{2,1,0:T(8,128)(2,1)S(1)}, u32[]{:S(2)}, u32[]{:S(2)}) async-start(bf16[32,16,512]{2,1,0:T(8,128)(2,1)} %broadcast_in_dim.27), calls=%async_computation.2 | async-start | bytes 1048576 | tf_op jit(solution)/shard_map/all_to_all | solution.py:299
  55.4 16.4 %all-to-all-start.3 = ((bf16[32,16,512]{2,1,0:T(8,128)(2,1)}), bf16[32,16,512]{2,1,0:T(8,128)(2,1)}, u32[]{:S(2)}, u32[]{:S(2)}) async-start(bf16[32,16,512]{2,1,0:T(8,128)(2,1)} %bitcast.10), calls=%async_computation.3 | async-start | bytes 1048576 | tf_op jit(solution)/shard_map/all_to_all | solution.py:299
  88.7 19.8 %collective-permute-start.2 = (bf16[112,512]{1,0:T(8,128)(2,1)S(1)}, bf16[112,512]{1,0:T(8,128)(2,1)S(1)}, u32[]{:S(2)}, u32[]{:S(2)}) collective-permute-start(bf16[112,512]{1,0:T(8,128)(2,1)S(1)} %shard_map.130), channel_id=1, source_target_pairs={{0,224},{32,192},{64,160},{96,128},{128,96},{160,64},{192,32},{224... | collective-permute-start | bytes 344072 | tf_op jit(solution)/shard_map/ppermute | solution.py:312
  94.7 13.8 %collective-permute-start.1 = (bf16[112,512]{1,0:T(8,128)(2,1)S(1)}, bf16[112,512]{1,0:T(8,128)(2,1)S(1)}, u32[]{:S(2)}, u32[]{:S(2)}) collective-permute-start(bf16[112,512]{1,0:T(8,128)(2,1)S(1)} %shard_map.130), channel_id=1, source_target_pairs={{0,160},{32,128},{64,224},{96,192},{128,32},{160,0},{192,96},{224,... | collective-permute-start | bytes 344072 | tf_op jit(solution)/shard_map/ppermute | solution.py:312
  95.7 12.8 %collective-permute-start = (bf16[112,512]{1,0:T(8,128)(2,1)S(1)}, bf16[112,512]{1,0:T(8,128)(2,1)S(1)}, u32[]{:S(2)}, u32[]{:S(2)}) collective-permute-start(bf16[112,512]{1,0:T(8,128)(2,1)S(1)} %shard_map.130), channel_id=1, source_target_pairs={{0,64},{32,96},{64,0},{96,32},{128,192},{160,224},{192,128},{224,1... | collective-permute-start | bytes 344072 | tf_op jit(solution)/shard_map/ppermute | solution.py:312
  108.6 5.3 %collective-permute-start.3 = (bf16[112,512]{1,0:T(8,128)(2,1)S(1)}, bf16[112,512]{1,0:T(8,128)(2,1)S(1)}, u32[]{:S(2)}, u32[]{:S(2)}) collective-permute-start(bf16[112,512]{1,0:T(8,128)(2,1)S(1)} %add_convert_fusion), channel_id=1, source_target_pairs={{0,32},{32,0},{64,96},{96,64},{128,160},{160,128},{192,224},{224,1... | collective-permute-start | bytes 344072 | tf_op jit(solution)/shard_map/ppermute | solution.py:312

commit v8 on v7

--- a/solution.py
+++ b/solution.py
@@ -8,6 +8,7 @@
 KVH = 2
 HD = 128
 GROUP = 7
+LINES = 4
 MASKED = -1e30
 LOG2E = 1.4426950408889634
 FACTOR = HD ** (-0.5)
@@ -204,7 +205,7 @@
         in_specs=specs,
         out_specs=tuple(VM for _ in outs),
         scratch_shapes=scratch,
-        compiler_params=pltpu.CompilerParams(vmem_limit_bytes=40 * 1024 * 1024),
+        compiler_params=pltpu.CompilerParams(vmem_limit_bytes=16 * 1024 * 1024),
         cost_estimate=pl.CostEstimate(
             flops=flops, bytes_accessed=4 * 1024 * 1024, transcendentals=0
         ),
@@ -257,85 +258,138 @@
     )
 
 
-def hidden_grad_kernel(grad_ref, weight_ref, out_ref):
-    part = dot_nt(grad_ref[...], weight_ref[...]).astype(jnp.bfloat16)
-    out_ref[...] = part.reshape(out_ref.shape)
-
-
-def hidden_grad_part(all_grad, weight, count):
+def partial_kernel(line_ref, hidden_ref, w0_ref, w1_ref, w2_ref, w3_ref, part_ref, *block_refs):
+    line = line_ref[0]
+    rows = hidden_ref.shape[0] * hidden_ref.shape[2]
+    total = jnp.zeros((rows, w0_ref.shape[1]), jnp.float32)
+    for step, w_ref in enumerate((w0_ref, w1_ref, w2_ref, w3_ref)):
+        block = hidden_ref[:, line ^ step].reshape(rows, w_ref.shape[0])
+        block_refs[step][...] = block
+        total = total + dot_nn(block, w_ref[...])
+    part_ref[...] = total.astype(jnp.bfloat16).reshape(part_ref.shape)
+
+
+def partial_kv(line, hidden, weights):
+    size, _, rows, depth = hidden.shape
+    block = jax.ShapeDtypeStruct((size * rows, depth), jnp.bfloat16)
+    part = jax.ShapeDtypeStruct((size, rows, weights[0].shape[1]), jnp.bfloat16)
+    return call(
+        partial_kernel,
+        (part,) + (block,) * LINES,
+        [],
+        [SM] + [VM] * (1 + LINES),
+        (line, hidden) + tuple(weights),
+        2 * LINES * size * rows * depth * weights[0].shape[1],
+    )
+
+
+def hidden_grad_kernel(line_ref, grad_ref, w0_ref, w1_ref, w2_ref, w3_ref, out_ref):
+    line = line_ref[0]
+    rows = grad_ref.shape[0] // LINES
+    grad = grad_ref[pl.ds(pl.multiple_of(line * rows, rows), rows), :]
+    for step, w_ref in enumerate((w0_ref, w1_ref, w2_ref, w3_ref)):
+        part = dot_nt(grad, w_ref[...]).astype(jnp.bfloat16)
+        out_ref[:, line ^ step] = part.reshape(out_ref.shape[0], out_ref.shape[2], -1)
+
+
+def hidden_grad_part(line, all_grad, weights, size):
     total, width = all_grad.shape
+    depth = weights[0].shape[0]
     return call(
         hidden_grad_kernel,
-        (jax.ShapeDtypeStruct((count, total // count, weight.shape[0]), jnp.bfloat16),),
+        (jax.ShapeDtypeStruct((size, LINES, total // (LINES * size), depth), jnp.bfloat16),),
         [],
-        [VM] * 2,
-        (all_grad, weight),
-        2 * total * width * weight.shape[0],
+        [SM] + [VM] * (1 + LINES),
+        (line, all_grad) + tuple(weights),
+        2 * total * width * depth,
     )[0]
 
 
-def weight_grad_kernel(hidden_ref, grad_ref, out_ref):
-    rows = grad_ref.shape[0]
-    out_ref[...] = lax.dot_general(
-        hidden_ref[...].reshape(rows, -1),
-        grad_ref[...],
-        (((0,), (0,)), ((), ())),
-        preferred_element_type=jnp.float32,
-    ).astype(jnp.bfloat16)
-
-
-def weight_grad_part(hidden_blocks, all_grad):
+def weight_grad_kernel(line_ref, grad_ref, h0_ref, h1_ref, h2_ref, h3_ref, out_ref):
+    line = line_ref[0]
+    rows = grad_ref.shape[0] // LINES
+    total = jnp.zeros(out_ref.shape, jnp.float32)
+    for step, h_ref in enumerate((h0_ref, h1_ref, h2_ref, h3_ref)):
+        at = pl.multiple_of((line ^ step) * rows, rows)
+        total = total + lax.dot_general(
+            h_ref[...],
+            grad_ref[pl.ds(at, rows), :],
+            (((0,), (0,)), ((), ())),
+            preferred_element_type=jnp.float32,
+        )
+    out_ref[...] = total.astype(jnp.bfloat16)
+
+
+def weight_grad_part(line, all_grad, hiddens):
     return call(
         weight_grad_kernel,
-        (jax.ShapeDtypeStruct((hidden_blocks.shape[-1], all_grad.shape[1]), jnp.bfloat16),),
+        (jax.ShapeDtypeStruct((hiddens[0].shape[1], all_grad.shape[1]), jnp.bfloat16),),
         [],
-        [VM] * 2,
-        (hidden_blocks, all_grad),
-        10**10,
+        [SM] + [VM] * (1 + LINES),
+        (line, all_grad) + tuple(hiddens),
+        10**9,
     )[0]
+
+
+def sum_kernel(arrived_ref, spread_ref):
+    own = jnp.sum(arrived_ref[...].astype(jnp.float32), 0).astype(jnp.bfloat16)
+    spread_ref[...] = jnp.broadcast_to(own[None], spread_ref.shape)
+
+
+def sum_and_spread(arrived):
+    shape = jax.ShapeDtypeStruct(arrived.shape, jnp.bfloat16)
+    return call(sum_kernel, (shape,), [], [VM], (arrived,), 1024)[0]
 
 
 def exchange(blocks):
     return lax.all_to_all(blocks, "ctx", 0, 0, tiled=True)
 
 
-def reduce_blocks(blocks):
-    return jnp.sum(exchange(blocks).astype(jnp.float32), 0).astype(jnp.bfloat16)
-
-
-def gather_rows(rows, count):
-    return exchange(jnp.broadcast_to(rows[None], (count,) + rows.shape)).reshape(-1, rows.shape[-1])
-
-
-def swap_dp(sent, mask):
-    pairs = [(i, i ^ mask) for i in range(lax.axis_size("dp"))]
-    return lax.ppermute(sent, "dp", pairs).astype(jnp.float32)
-
-
-def sum_dp(part, beside):
-    sent = part
-    near, far, wide = [swap_dp(sent, mask) for mask in (2, 5, 7)]
+def exchange_line(blocks):
+    size = blocks.shape[0]
+    groups = [[line * size + i for i in range(size)] for line in range(LINES)]
+    return lax.all_to_all(blocks, "ctx", 0, 0, axis_index_groups=groups, tiled=True)
+
+
+def swap(rows, axis, mask):
+    pairs = [(i, i ^ mask) for i in range(lax.axis_size(axis))]
+    return lax.ppermute(rows, axis, pairs)
+
+
+def sum_dp(sent, beside):
+    near, far, wide = [swap(sent, "dp", mask).astype(jnp.float32) for mask in (2, 5, 7)]
     sent, beside = lax.optimization_barrier((sent, beside))
-    part = (sent.astype(jnp.float32) + near) + (far + wide)
-    sent = part.astype(jnp.bfloat16)
-    return sent.astype(jnp.float32) + swap_dp(sent, 1), beside
+    sent = ((sent.astype(jnp.float32) + near) + (far + wide)).astype(jnp.bfloat16)
+    return sent.astype(jnp.float32) + swap(sent, "dp", 1).astype(jnp.float32), beside
 
 
 def shards(
     query, keys_values, beacon_query, beacon_hidden, beacon_weight, grad_tokens, grad_beacons
 ):
-    pos = lax.axis_index("ctx").astype(jnp.int32).reshape(1)
     count = lax.axis_size("ctx")
+    size = count // LINES
+    index = lax.axis_index("ctx").astype(jnp.int32)
+    pos = index.reshape(1)
+    line = (index // size).reshape(1)
     rows = beacon_hidden.shape[1]
-    hidden_rows = beacon_hidden[0]
     stats = token_stats(
         query[0], beacon_query[0], keys_values[0], grad_tokens[0], grad_beacons[0]
     )
-    hidden_cols = exchange(hidden_rows.reshape(rows, count, -1).transpose(1, 0, 2))
-    hidden_cols = hidden_cols.reshape(rows * count, -1)
-    part_kv = jnp.dot(hidden_cols, beacon_weight, preferred_element_type=jnp.float32)
-    own_kv = reduce_blocks(part_kv.astype(jnp.bfloat16).reshape(count, rows, -1))
-    all_kv = gather_rows(own_kv, count)
+
+    hidden = beacon_hidden[0].reshape(rows, LINES, size, -1).transpose(2, 1, 0, 3)
+    hidden, late_weight = lax.optimization_barrier((hidden, beacon_weight))
+    hidden = exchange_line(hidden)
+    weights = [beacon_weight] + [
+        swap(late_weight, "ctx", step * size) for step in range(1, LINES)
+    ]
+    part_kv, *blocks = partial_kv(line, hidden, weights)
+    own_kv = jnp.sum(exchange_line(part_kv).astype(jnp.float32), 0).astype(jnp.bfloat16)
+    all_kv = exchange(jnp.broadcast_to(own_kv[None], (count,) + own_kv.shape))
+    all_kv = all_kv.reshape(rows * count, -1)
+    columns = [blocks[0]] + [
+        swap(blocks[step], "ctx", step * size) for step in range(1, LINES)
+    ]
+
     contrib, row_stats = beacon_grads(
         pos, query[0], beacon_query[0], all_kv, grad_tokens[0], grad_beacons[0], stats
     )
@@ -345,14 +399,14 @@
     arrived = exchange(contrib.reshape(count, rows, -1))
     arrived, others = lax.optimization_barrier((arrived, others))
     tokens_out, beacons_out, query_grad, beacon_qgrad, token_kvgrad = others
-    own_grad = jnp.sum(arrived.astype(jnp.float32), 0).astype(jnp.bfloat16)
-    all_grad = gather_rows(own_grad, count)
-    hidden_part = hidden_grad_part(all_grad, beacon_weight, count)
+    all_grad = exchange(sum_and_spread(arrived)).reshape(rows * count, -1)
+
+    hidden_part = hidden_grad_part(line, all_grad, weights, size)
     hidden_part, late_grad = lax.optimization_barrier((hidden_part, all_grad))
-    weight_part = weight_grad_part(hidden_cols, late_grad)
-    hidden_blocks = exchange(hidden_part)
+    weight_part = weight_grad_part(line, late_grad, columns)
+    hidden_blocks = exchange_line(hidden_part)
     grad_weight, hidden_blocks = sum_dp(weight_part, hidden_blocks)
-    hidden_grad = hidden_blocks.transpose(1, 0, 2).reshape(rows, -1)
+    hidden_grad = hidden_blocks.transpose(2, 1, 0, 3).reshape(rows, -1)
     return (
         tokens_out[None],
         beacons_out[None],

time: 116 us -> 111 us (0.957)
  blocking collectives: 56 us -> 17.7 us
  starting transfers between devices: 20.4 us -> 40.3 us
  waiting for transfers between devices: 15.5 us -> 26.5 us
  local copies, waits for them, and re-layouts: 2.97 us -> 6.13 us
  other arithmetic: 2 us -> 0.8 us
  Pallas kernels: 16.7 us -> 17.9 us
    all_to_all x4 -> x2, blocking collectives: 56 us -> 17.7 us  [exchange_line(): lax.all_to_all(blocks, 'ctx', 0, 0, axis_index_groups=groups, tiled=True)]
    ppermute x4 -> x10, starting transfers between devices: 9.53 us -> 17.4 us  [swap(): return lax.ppermute(rows, axis, pairs)]
    all_to_all x2 -> x3, starting transfers between devices: 10.9 us -> 17.4 us  [exchange(): return lax.all_to_all(blocks, 'ctx', 0, 0, tiled=True)]
    all_to_all x0 -> x1, starting transfers between devices: none -> 5.55 us  [exchange_line(): lax.all_to_all(blocks, 'ctx', 0, 0, axis_index_groups=groups, tiled=True)]
    all_to_all x0 -> x1, waiting for transfers between devices: none -> 4.7 us  [exchange_line(): lax.all_to_all(blocks, 'ctx', 0, 0, axis_index_groups=groups, tiled=True)]
    all_to_all x2 -> x3, waiting for transfers between devices: 12.2 us -> 16.2 us  [exchange(): return lax.all_to_all(blocks, 'ctx', 0, 0, tiled=True)]
    unnamed x12 -> x22, local copies, waits for them, and re-layouts: 0.03 us -> 2.53 us
    ppermute x4 -> x10, waiting for transfers between devices: 3.32 us -> 5.58 us  [swap(): return lax.ppermute(rows, axis, pairs)]
  transfers between devices with their start and end apart: 6 -> 14, of which waited for: 3 -> 8; matrix products, arithmetic and copies ran while one was open for 1% -> 1% of each run, Pallas kernels for 8% -> 8%
where the time goes in v8:
time: 111 us; the launch traced here: 110 us
  starting transfers between devices  40.3 us (36%)
  waiting for transfers between devices  26.5 us (24%)
  Pallas kernels  17.9 us (16%)
  blocking collectives  17.7 us (16%)
  local copies, waits for them, and re-layouts  6.13 us (6%)
    pallas_call x7, Pallas kernels, call(): pl.pallas_call(kernel, out_shape=outs, in_specs=specs, out_specs=tuple((V...  17.9 us
    all_to_all x2, blocking collectives, exchange_line(): lax.all_to_all(blocks, 'ctx', 0, 0, axis_index_groups=groups, tiled=True)  17.7 us
    all_to_all x3, starting transfers between devices, exchange(): return lax.all_to_all(blocks, 'ctx', 0, 0, tiled=True)  17.4 us
    ppermute x10, starting transfers between devices, swap(): return lax.ppermute(rows, axis, pairs)  17.4 us
    all_to_all x3, waiting for transfers between devices, exchange(): return lax.all_to_all(blocks, 'ctx', 0, 0, tiled=True)  16.2 us
    ppermute x10, waiting for transfers between devices, swap(): return lax.ppermute(rows, axis, pairs)  5.58 us
    all_to_all x1, starting transfers between devices, exchange_line(): lax.all_to_all(blocks, 'ctx', 0, 0, axis_index_groups=groups, tiled=True)  5.55 us
    all_to_all x1, waiting for transfers between devices, exchange_line(): lax.all_to_all(blocks, 'ctx', 0, 0, axis_index_groups=groups, tiled=True)  4.7 us
  transfers between devices with their start and end apart: 14, of which 8 were waited for; matrix products, arithmetic and copies ran while one was open for 1% of the time, Pallas kernels for 8%

profile of v8, /device:TPU:2, one launch (start us, length us, event | category | flops | bytes accessed | tf_op | source)
XLA Modules:
  0.0 110.2 jit_solution(4548850296559161270)
XLA Ops:
  0.6 1.1 reshape_squeeze.3
  1.7 0.0 copy-start.2
  1.7 0.7 copy.17
  2.5 0.2 copy-done.2
  2.6 3.0 %collective-permute-start.2 = (bf16[112,512]{1,0:T(8,128)(2,1)S(1)}, bf16[112,512]{1,0:T(8,128)(2,1)S(1)}, u32[]{:S(2)}, u32[]{:S(2)}) collective-permute-start(bf16[112,512]{1,0:T(8,128)(2,1)S(1)} %copy-done.2), channel_id=1, source_target_pairs={{0,24},{1,25},{2,26},{3,27},{4,28},{5,29},{6,30},{7,31},{8,16},{9,... | collective-permute-start | bytes 344072 | tf_op jit(solution)/shard_map/ppermute | solution.py:356
  5.7 0.6 collective-permute-start.1
  6.3 0.5 collective-permute-start
  6.7 5.6 %all-to-all-start = ((bf16[8,4,16,112]{3,2,1,0:T(8,128)(2,1)}), bf16[8,4,16,112]{3,2,1,0:T(8,128)(2,1)S(1)}, u32[]{:S(2)}, u32[]{:S(2)}) async-start(bf16[8,4,16,112]{3,2,1,0:T(8,128)(2,1)} %bitcast.20), calls=%async_computation | async-start | bytes 262144 | tf_op jit(solution)/shard_map/all_to_all | solution.py:351
  12.3 4.7 %all-to-all-done.hidden_ref = bf16[8,4,16,112]{3,2,1,0:T(8,128)(2,1)S(1)} async-done(((bf16[8,4,16,112]{3,2,1,0:T(8,128)(2,1)}), bf16[8,4,16,112]{3,2,1,0:T(8,128)(2,1)S(1)}, u32[]{:S(2)}, u32[]{:S(2)}) %all-to-all-start) | async-done | bytes 114720 | tf_op jit(solution)/shard_map/all_to_all | solution.py:351
  17.0 0.0 collective-permute-done.2.w3_ref
  17.0 0.0 copy-start.3
  17.0 0.3 shard_map.126
  17.3 0.0 copy-start.7
  17.3 0.0 copy-start.1
  17.3 8.6 %all_to_all.30 = bf16[8,16,512]{2,1,0:T(8,128)(2,1)S(1)} all-to-all(bf16[8,16,512]{2,1,0:T(8,128)(2,1)S(1)} %get-tuple-element.33), channel_id=1, replica_groups={{0,1,2,3,4,5,6,7},{8,9,10,11,12,13,14,15},{16,17,18,19,20,21,22,23},{24..., dimensions={0} | all-to-all | bytes 262144 | tf_op jit(solution)/shard_map/all_to_all | solution.py:351
  26.0 0.9 broadcast_in_dim.21
  26.9 6.1 %all-to-all-start.2 = ((bf16[32,16,512]{2,1,0:T(8,128)(2,1)}), bf16[32,16,512]{2,1,0:T(8,128)(2,1)S(1)}, u32[]{:S(2)}, u32[]{:S(2)}) async-start(bf16[32,16,512]{2,1,0:T(8,128)(2,1)} %broadcast_in_dim.21), calls=%async_computation.2 | async-start | bytes 1048576 | tf_op jit(solution)/shard_map/all_to_all | solution.py:345
  33.0 1.5 %shard_map.127.stats_ref = f32[3,2,8,256]{3,2,1,0:T(8,128)S(1)} custom-call(bf16[256,1792]{1,0:T(8,128)(2,1)S(1)} %bitcast.23, bf16[16,1792]{1,0:T(8,128)(2,1)S(1)} %bitcast.33, bf16[256,512]{1,0:T(8,128)(2,1)S(1)} %bitcast.31, bf16[256,1792]{1,0:T(8,128)(2,1)S(1)} %bitcast.26, bf16[16,1792]{1,0:T(8,128)(2,1)S(1)} %bitcast.36), custom_call_target="tpu_custom_call" | custom-call | flops 536870912 | bytes 4194304 | tf_op jit(solution)/shard_map/pallas_call | solution.py:202
  34.5 8.9 %all-to-all-done.2 = bf16[32,16,512]{2,1,0:T(8,128)(2,1)S(1)} async-done(((bf16[32,16,512]{2,1,0:T(8,128)(2,1)}), bf16[32,16,512]{2,1,0:T(8,128)(2,1)S(1)}, u32[]{:S(2)}, u32[]{:S(2)}) %all-to-all-start.2) | async-done | bytes 524320 | tf_op jit(solution)/shard_map/all_to_all | solution.py:345
  43.4 7.1 %shard_map.128 = (bf16[512,512]{1,0:T(8,128)(2,1)}, f32[2,2,8,256]{3,2,1,0:T(8,128)S(1)}) custom-call(s32[1]{0:T(128)} %bitcast.pos_ref, bf16[256,1792]{1,0:T(8,128)(2,1)S(1)} %bitcast.24, bf16[16,1792]{1,0:T(8,128)(2,1)S(1)} %bitcast.34, bf16[512,512]{1,0:T(8,128)(2,1)S(1)} %bitcast.29, bf16[256,1792]{1,0:T(8,128)(2,1)S(1)} %bitcast.27, ...), custom_call_target="tpu_custom_call" | custom-call | flops 2147483648 | bytes 4194304 | tf_op jit(solution)/shard_map/pallas_call | solution.py:202
  50.6 0.6 copy-done.9
  51.2 5.1 %all-to-all-start.3 = ((bf16[32,16,512]{2,1,0:T(8,128)(2,1)}), bf16[32,16,512]{2,1,0:T(8,128)(2,1)S(1)}, u32[]{:S(2)}, u32[]{:S(2)}) async-start(bf16[32,16,512]{2,1,0:T(8,128)(2,1)} %bitcast.9), calls=%async_computation.3 | async-start | bytes 1048576 | tf_op jit(solution)/shard_map/all_to_all | solution.py:345
  56.3 0.0 copy-start.4
  56.3 0.9 copy-done.4
  57.2 0.8 copy-done.10
  58.0 7.5 %shard_map.129 = (bf16[256,1792]{1,0:T(8,128)(2,1)}, bf16[16,1792]{1,0:T(8,128)(2,1)}, bf16[256,1792]{1,0:T(8,128)(2,1)}, bf16[16,1792]{1,0:T(8,128)(2,1)}, bf16[256,512]{1,0:T(8,128)(2,1)}) custom-call(s32[1]{0:T(128)} %bitcast.pos_ref, bf16[256,1792]{1,0:T(8,128)(2,1)S(1)} %bitcast.25, bf16[16,1792]{1,0:T(8,128)(2,1)S(1)} %bitcast.35, ...), custom_call_target="tpu_custom_call" | custom-call | flops 4026531840 | bytes 4194304 | tf_op jit(solution)/shard_map/pallas_call | solution.py:202
  65.5 1.4 %all-to-all-done.3.arrived_ref = bf16[32,16,512]{2,1,0:T(8,128)(2,1)S(1)} async-done(((bf16[32,16,512]{2,1,0:T(8,128)(2,1)}), bf16[32,16,512]{2,1,0:T(8,128)(2,1)S(1)}, u32[]{:S(2)}, u32[]{:S(2)}) %all-to-all-start.3) | async-done | bytes 524320 | tf_op jit(solution)/shard_map/all_to_all | solution.py:345
  66.9 0.9 shard_map.130
  67.8 6.2 %all-to-all-start.4 = ((bf16[32,16,512]{2,1,0:T(8,128)(2,1)}), bf16[32,16,512]{2,1,0:T(8,128)(2,1)S(1)}, u32[]{:S(2)}, u32[]{:S(2)}) async-start(bf16[32,16,512]{2,1,0:T(8,128)(2,1)} %shard_map.130), calls=%async_computation.4 | async-start | bytes 1048576 | tf_op jit(solution)/shard_map/all_to_all | solution.py:345
  74.0 1.6 %collective-permute-start.3 = (bf16[128,112]{1,0:T(8,128)(2,1)S(1)}, bf16[128,112]{1,0:T(8,128)(2,1)S(1)}, u32[]{:S(2)}, u32[]{:S(2)}) collective-permute-start(bf16[128,112]{1,0:T(8,128)(2,1)S(1)} %copy-done.8), channel_id=1, source_target_pairs={{0,8},{1,9},{2,10},{3,11},{4,12},{5,13},{6,14},{7,15},{8,0},{9,1},... | collective-permute-start | bytes 86024 | tf_op jit(solution)/shard_map/ppermute | solution.py:356
  75.6 2.7 %collective-permute-start.4 = (bf16[128,112]{1,0:T(8,128)(2,1)S(1)}, bf16[128,112]{1,0:T(8,128)(2,1)S(1)}, u32[]{:S(2)}, u32[]{:S(2)}) collective-permute-start(bf16[128,112]{1,0:T(8,128)(2,1)S(1)} %get-tuple-element.50), channel_id=1, source_target_pairs={{0,16},{1,17},{2,18},{3,19},{4,20},{5,21},{6,22},{7,23},{8,24},{9,... | collective-permute-start | bytes 86024 | tf_op jit(solution)/shard_map/ppermute | solution.py:356
  78.3 0.5 collective-permute-start.5
  78.8 5.9 %all-to-all-done.4 = bf16[32,16,512]{2,1,0:T(8,128)(2,1)S(1)} async-done(((bf16[32,16,512]{2,1,0:T(8,128)(2,1)}), bf16[32,16,512]{2,1,0:T(8,128)(2,1)S(1)}, u32[]{:S(2)}, u32[]{:S(2)}) %all-to-all-start.4) | async-done | bytes 524320 | tf_op jit(solution)/shard_map/all_to_all | solution.py:345
  84.7 0.3 shard_map.131
  85.0 0.1 collective-permute-done.4.h2_ref
  85.2 0.2 collective-permute-done.5.h3_ref
  85.3 0.3 shard_map.132
  85.7 5.9 %collective-permute-start.8 = (bf16[112,512]{1,0:T(8,128)(2,1)S(1)}, bf16[112,512]{1,0:T(8,128)(2,1)S(1)}, u32[]{:S(2)}, u32[]{:S(2)}) collective-permute-start(bf16[112,512]{1,0:T(8,128)(2,1)S(1)} %shard_map.132), channel_id=1, source_target_pairs={{0,224},{32,192},{64,160},{96,128},{128,96},{160,64},{192,32},{224... | collective-permute-start | bytes 344072 | tf_op jit(solution)/shard_map/ppermute | solution.py:356
  91.6 1.0 collective-permute-start.7
  92.6 1.5 %collective-permute-start.6 = (bf16[112,512]{1,0:T(8,128)(2,1)S(1)}, bf16[112,512]{1,0:T(8,128)(2,1)S(1)}, u32[]{:S(2)}, u32[]{:S(2)}) collective-permute-start(bf16[112,512]{1,0:T(8,128)(2,1)S(1)} %shard_map.132), channel_id=1, source_target_pairs={{0,64},{32,96},{64,0},{96,32},{128,192},{160,224},{192,128},{224,1... | collective-permute-start | bytes 344072 | tf_op jit(solution)/shard_map/ppermute | solution.py:356
  94.1 9.0 %all_to_all.31 = bf16[8,4,16,112]{3,2,1,0:T(8,128)(2,1)S(1)} all-to-all(bf16[8,4,16,112]{3,2,1,0:T(8,128)(2,1)S(1)} %shard_map.131), channel_id=1, replica_groups={{0,1,2,3,4,5,6,7},{8,9,10,11,12,13,14,15},{16,17,18,19,20,21,22,23},{24..., dimensions={0} | all-to-all | bytes 229376 | tf_op jit(solution)/shard_map/all_to_all | solution.py:351
  103.1 1.4 %collective-permute-done.6 = bf16[112,512]{1,0:T(8,128)(2,1)S(1)} collective-permute-done((bf16[112,512]{1,0:T(8,128)(2,1)S(1)}, bf16[112,512]{1,0:T(8,128)(2,1)S(1)}, u32[]{:S(2)}, u32[]{:S(2)}) %collective-permute-start.6) | collective-permute-done | bytes 114720 | tf_op jit(solution)/shard_map/ppermute | solution.py:356
  104.5 0.1 add_convert_fusion
  104.6 0.1 collective-permute-start.9
  104.7 0.1 copy.15
  104.8 0.8 broadcast_in_dim_reshape.3
  105.6 3.8 %collective-permute-done.9 = bf16[112,512]{1,0:T(8,128)(2,1)S(1)} collective-permute-done((bf16[112,512]{1,0:T(8,128)(2,1)S(1)}, bf16[112,512]{1,0:T(8,128)(2,1)S(1)}, u32[]{:S(2)}, u32[]{:S(2)}) %collective-permute-start.9) | collective-permute-done | bytes 114720 | tf_op jit(solution)/shard_map/ppermute | solution.py:356
  109.5 0.7 convert_add_fusion
  (19 shorter events, 0.1 us)
Async XLA Ops:
  1.7 0.9 copy-start.2
  2.6 14.4 %collective-permute-start.2 = (bf16[112,512]{1,0:T(8,128)(2,1)S(1)}, bf16[112,512]{1,0:T(8,128)(2,1)S(1)}, u32[]{:S(2)}, u32[]{:S(2)}) collective-permute-start(bf16[112,512]{1,0:T(8,128)(2,1)S(1)} %copy-done.2), channel_id=1, source_target_pairs={{0,24},{1,25},{2,26},{3,27},{4,28},{5,29},{6,30},{7,31},{8,16},{9,... | collective-permute-start | bytes 344072 | tf_op jit(solution)/shard_map/ppermute | solution.py:356
  5.7 11.3 %collective-permute-start.1 = (bf16[112,512]{1,0:T(8,128)(2,1)S(1)}, bf16[112,512]{1,0:T(8,128)(2,1)S(1)}, u32[]{:S(2)}, u32[]{:S(2)}) collective-permute-start(bf16[112,512]{1,0:T(8,128)(2,1)S(1)} %copy-done.2), channel_id=1, source_target_pairs={{0,16},{1,17},{2,18},{3,19},{4,20},{5,21},{6,22},{7,23},{8,24},{9,... | collective-permute-start | bytes 344072 | tf_op jit(solution)/shard_map/ppermute | solution.py:356
  6.3 10.7 %collective-permute-start = (bf16[112,512]{1,0:T(8,128)(2,1)S(1)}, bf16[112,512]{1,0:T(8,128)(2,1)S(1)}, u32[]{:S(2)}, u32[]{:S(2)}) collective-permute-start(bf16[112,512]{1,0:T(8,128)(2,1)S(1)} %copy-done.2), channel_id=1, source_target_pairs={{0,8},{1,9},{2,10},{3,11},{4,12},{5,13},{6,14},{7,15},{8,0},{9,1},... | collective-permute-start | bytes 344072 | tf_op jit(solution)/shard_map/ppermute | solution.py:356
  6.7 10.3 %all-to-all-start = ((bf16[8,4,16,112]{3,2,1,0:T(8,128)(2,1)}), bf16[8,4,16,112]{3,2,1,0:T(8,128)(2,1)S(1)}, u32[]{:S(2)}, u32[]{:S(2)}) async-start(bf16[8,4,16,112]{3,2,1,0:T(8,128)(2,1)} %bitcast.20), calls=%async_computation | async-start | bytes 262144 | tf_op jit(solution)/shard_map/all_to_all | solution.py:351
  17.0 16.0 %copy-start.3 = (bf16[1,256,512]{2,1,0:T(8,128)(2,1)S(1)}, bf16[1,256,512]{2,1,0:T(8,128)(2,1)}, u32[]{:S(2)}) copy-start(bf16[1,256,512]{2,1,0:T(8,128)(2,1)} %param.8) | copy-start | bytes 786436
  17.3 8.7 %copy-start.7 = (bf16[128,112]{1,0:T(8,128)(2,1)}, bf16[128,112]{1,0:T(8,128)(2,1)S(1)}, u32[]{:S(2)}) copy-start(bf16[128,112]{1,0:T(8,128)(2,1)S(1)} %get-tuple-element.49) | copy-start | bytes 86020
  17.3 15.6 %copy-start.1 = (bf16[1,256,1792]{2,1,0:T(8,128)(2,1)S(1)}, bf16[1,256,1792]{2,1,0:T(8,128)(2,1)}, u32[]{:S(2)}) copy-start(bf16[1,256,1792]{2,1,0:T(8,128)(2,1)} %param.12) | copy-start | bytes 2752516
  26.0 7.0 %copy-start = (bf16[1,256,1792]{2,1,0:T(8,128)(2,1)S(1)}, bf16[1,256,1792]{2,1,0:T(8,128)(2,1)}, u32[]{:S(2)}) copy-start(bf16[1,256,1792]{2,1,0:T(8,128)(2,1)} %param.7) | copy-start | bytes 2752516
  26.9 6.1 %copy-start.5 = (bf16[1,16,1792]{2,1,0:T(8,128)(2,1)S(1)}, bf16[1,16,1792]{2,1,0:T(8,128)(2,1)}, u32[]{:S(2)}) copy-start(bf16[1,16,1792]{2,1,0:T(8,128)(2,1)} %param.9) | copy-start | bytes 172036
  26.9 6.1 %copy-start.6 = (bf16[1,16,1792]{2,1,0:T(8,128)(2,1)S(1)}, bf16[1,16,1792]{2,1,0:T(8,128)(2,1)}, u32[]{:S(2)}) copy-start(bf16[1,16,1792]{2,1,0:T(8,128)(2,1)} %param.13) | copy-start | bytes 172036
  26.9 16.6 %all-to-all-start.2 = ((bf16[32,16,512]{2,1,0:T(8,128)(2,1)}), bf16[32,16,512]{2,1,0:T(8,128)(2,1)S(1)}, u32[]{:S(2)}, u32[]{:S(2)}) async-start(bf16[32,16,512]{2,1,0:T(8,128)(2,1)} %broadcast_in_dim.21), calls=%async_computation.2 | async-start | bytes 1048576 | tf_op jit(solution)/shard_map/all_to_all | solution.py:345
  50.6 0.6 copy-start.9
  51.2 15.7 %all-to-all-start.3 = ((bf16[32,16,512]{2,1,0:T(8,128)(2,1)}), bf16[32,16,512]{2,1,0:T(8,128)(2,1)S(1)}, u32[]{:S(2)}, u32[]{:S(2)}) async-start(bf16[32,16,512]{2,1,0:T(8,128)(2,1)} %bitcast.9), calls=%async_computation.3 | async-start | bytes 1048576 | tf_op jit(solution)/shard_map/all_to_all | solution.py:345
  56.3 1.0 copy-start.4
  57.2 0.8 copy-start.10
  67.8 6.2 %copy-start.8 = (bf16[128,112]{1,0:T(8,128)(2,1)S(1)}, bf16[128,112]{1,0:T(8,128)(2,1)}, u32[]{:S(2)}) copy-start(bf16[128,112]{1,0:T(8,128)(2,1)} %copy-done.7) | copy-start | bytes 86020
  67.8 16.9 %all-to-all-start.4 = ((bf16[32,16,512]{2,1,0:T(8,128)(2,1)}), bf16[32,16,512]{2,1,0:T(8,128)(2,1)S(1)}, u32[]{:S(2)}, u32[]{:S(2)}) async-start(bf16[32,16,512]{2,1,0:T(8,128)(2,1)} %shard_map.130), calls=%async_computation.4 | async-start | bytes 1048576 | tf_op jit(solution)/shard_map/all_to_all | solution.py:345
  74.0 11.0 %collective-permute-start.3 = (bf16[128,112]{1,0:T(8,128)(2,1)S(1)}, bf16[128,112]{1,0:T(8,128)(2,1)S(1)}, u32[]{:S(2)}, u32[]{:S(2)}) collective-permute-start(bf16[128,112]{1,0:T(8,128)(2,1)S(1)} %copy-done.8), channel_id=1, source_target_pairs={{0,8},{1,9},{2,10},{3,11},{4,12},{5,13},{6,14},{7,15},{8,0},{9,1},... | collective-permute-start | bytes 86024 | tf_op jit(solution)/shard_map/ppermute | solution.py:356
  75.6 9.6 %collective-permute-start.4 = (bf16[128,112]{1,0:T(8,128)(2,1)S(1)}, bf16[128,112]{1,0:T(8,128)(2,1)S(1)}, u32[]{:S(2)}, u32[]{:S(2)}) collective-permute-start(bf16[128,112]{1,0:T(8,128)(2,1)S(1)} %get-tuple-element.50), channel_id=1, source_target_pairs={{0,16},{1,17},{2,18},{3,19},{4,20},{5,21},{6,22},{7,23},{8,24},{9,... | collective-permute-start | bytes 86024 | tf_op jit(solution)/shard_map/ppermute | solution.py:356
  78.3 7.0 %collective-permute-start.5 = (bf16[128,112]{1,0:T(8,128)(2,1)S(1)}, bf16[128,112]{1,0:T(8,128)(2,1)S(1)}, u32[]{:S(2)}, u32[]{:S(2)}) collective-permute-start(bf16[128,112]{1,0:T(8,128)(2,1)S(1)} %get-tuple-element.51), channel_id=1, source_target_pairs={{0,24},{1,25},{2,26},{3,27},{4,28},{5,29},{6,30},{7,31},{8,16},{9,... | collective-permute-start | bytes 86024 | tf_op jit(solution)/shard_map/ppermute | solution.py:356
  85.7 17.4 %collective-permute-start.8 = (bf16[112,512]{1,0:T(8,128)(2,1)S(1)}, bf16[112,512]{1,0:T(8,128)(2,1)S(1)}, u32[]{:S(2)}, u32[]{:S(2)}) collective-permute-start(bf16[112,512]{1,0:T(8,128)(2,1)S(1)} %shard_map.132), channel_id=1, source_target_pairs={{0,224},{32,192},{64,160},{96,128},{128,96},{160,64},{192,32},{224... | collective-permute-start | bytes 344072 | tf_op jit(solution)/shard_map/ppermute | solution.py:356
  91.6 11.5 %collective-permute-start.7 = (bf16[112,512]{1,0:T(8,128)(2,1)S(1)}, bf16[112,512]{1,0:T(8,128)(2,1)S(1)}, u32[]{:S(2)}, u32[]{:S(2)}) collective-permute-start(bf16[112,512]{1,0:T(8,128)(2,1)S(1)} %shard_map.132), channel_id=1, source_target_pairs={{0,160},{32,128},{64,224},{96,192},{128,32},{160,0},{192,96},{224,... | collective-permute-start | bytes 344072 | tf_op jit(solution)/shard_map/ppermute | solution.py:356
  92.6 11.9 %collective-permute-start.6 = (bf16[112,512]{1,0:T(8,128)(2,1)S(1)}, bf16[112,512]{1,0:T(8,128)(2,1)S(1)}, u32[]{:S(2)}, u32[]{:S(2)}) collective-permute-start(bf16[112,512]{1,0:T(8,128)(2,1)S(1)} %shard_map.132), channel_id=1, source_target_pairs={{0,64},{32,96},{64,0},{96,32},{128,192},{160,224},{192,128},{224,1... | collective-permute-start | bytes 344072 | tf_op jit(solution)/shard_map/ppermute | solution.py:356
  104.6 4.9 %collective-permute-start.9 = (bf16[112,512]{1,0:T(8,128)(2,1)S(1)}, bf16[112,512]{1,0:T(8,128)(2,1)S(1)}, u32[]{:S(2)}, u32[]{:S(2)}) collective-permute-start(bf16[112,512]{1,0:T(8,128)(2,1)S(1)} %add_convert_fusion), channel_id=1, source_target_pairs={{0,32},{32,0},{64,96},{96,64},{128,160},{160,128},{192,224},{224,1... | collective-permute-start | bytes 344072 | tf_op jit(solution)/shard_map/ppermute | solution.py:356

commit v9 on v8

--- a/solution.py
+++ b/solution.py
@@ -1,3 +1,5 @@
+import functools
+
 import jax
 import jax.numpy as jnp
 from jax import lax
@@ -258,8 +260,8 @@
     )
 
 
-def partial_kernel(line_ref, hidden_ref, w0_ref, w1_ref, w2_ref, w3_ref, part_ref, *block_refs):
-    line = line_ref[0]
+def partial_kernel(pos_ref, hidden_ref, w0_ref, w1_ref, w2_ref, w3_ref, part_ref, *block_refs):
+    line = lax.div(pos_ref[0], jnp.int32(hidden_ref.shape[0]))
     rows = hidden_ref.shape[0] * hidden_ref.shape[2]
     total = jnp.zeros((rows, w0_ref.shape[1]), jnp.float32)
     for step, w_ref in enumerate((w0_ref, w1_ref, w2_ref, w3_ref)):
@@ -269,7 +271,7 @@
     part_ref[...] = total.astype(jnp.bfloat16).reshape(part_ref.shape)
 
 
-def partial_kv(line, hidden, weights):
+def partial_kv(pos, hidden, weights):
     size, _, rows, depth = hidden.shape
     block = jax.ShapeDtypeStruct((size * rows, depth), jnp.bfloat16)
     part = jax.ShapeDtypeStruct((size, rows, weights[0].shape[1]), jnp.bfloat16)
@@ -278,13 +280,13 @@
         (part,) + (block,) * LINES,
         [],
         [SM] + [VM] * (1 + LINES),
-        (line, hidden) + tuple(weights),
+        (pos, hidden) + tuple(weights),
         2 * LINES * size * rows * depth * weights[0].shape[1],
     )
 
 
-def hidden_grad_kernel(line_ref, grad_ref, w0_ref, w1_ref, w2_ref, w3_ref, out_ref):
-    line = line_ref[0]
+def hidden_grad_kernel(pos_ref, grad_ref, w0_ref, w1_ref, w2_ref, w3_ref, out_ref):
+    line = lax.div(pos_ref[0], jnp.int32(out_ref.shape[0]))
     rows = grad_ref.shape[0] // LINES
     grad = grad_ref[pl.ds(pl.multiple_of(line * rows, rows), rows), :]
     for step, w_ref in enumerate((w0_ref, w1_ref, w2_ref, w3_ref)):
@@ -292,7 +294,7 @@
         out_ref[:, line ^ step] = part.reshape(out_ref.shape[0], out_ref.shape[2], -1)
 
 
-def hidden_grad_part(line, all_grad, weights, size):
+def hidden_grad_part(pos, all_grad, weights, size):
     total, width = all_grad.shape
     depth = weights[0].shape[0]
     return call(
@@ -300,13 +302,13 @@
         (jax.ShapeDtypeStruct((size, LINES, total // (LINES * size), depth), jnp.bfloat16),),
         [],
         [SM] + [VM] * (1 + LINES),
-        (line, all_grad) + tuple(weights),
+        (pos, all_grad) + tuple(weights),
         2 * total * width * depth,
     )[0]
 
 
-def weight_grad_kernel(line_ref, grad_ref, h0_ref, h1_ref, h2_ref, h3_ref, out_ref):
-    line = line_ref[0]
+def weight_grad_kernel(size, pos_ref, grad_ref, h0_ref, h1_ref, h2_ref, h3_ref, out_ref):
+    line = lax.div(pos_ref[0], jnp.int32(size))
     rows = grad_ref.shape[0] // LINES
     total = jnp.zeros(out_ref.shape, jnp.float32)
     for step, h_ref in enumerate((h0_ref, h1_ref, h2_ref, h3_ref)):
@@ -320,25 +322,15 @@
     out_ref[...] = total.astype(jnp.bfloat16)
 
 
-def weight_grad_part(line, all_grad, hiddens):
-    return call(
-        weight_grad_kernel,
+def weight_grad_part(pos, all_grad, hiddens, size):
+    return call(
+        functools.partial(weight_grad_kernel, size),
         (jax.ShapeDtypeStruct((hiddens[0].shape[1], all_grad.shape[1]), jnp.bfloat16),),
         [],
         [SM] + [VM] * (1 + LINES),
-        (line, all_grad) + tuple(hiddens),
+        (pos, all_grad) + tuple(hiddens),
         10**9,
     )[0]
-
-
-def sum_kernel(arrived_ref, spread_ref):
-    own = jnp.sum(arrived_ref[...].astype(jnp.float32), 0).astype(jnp.bfloat16)
-    spread_ref[...] = jnp.broadcast_to(own[None], spread_ref.shape)
-
-
-def sum_and_spread(arrived):
-    shape = jax.ShapeDtypeStruct(arrived.shape, jnp.bfloat16)
-    return call(sum_kernel, (shape,), [], [VM], (arrived,), 1024)[0]
 
 
 def exchange(blocks):
@@ -368,9 +360,7 @@
 ):
     count = lax.axis_size("ctx")
     size = count // LINES
-    index = lax.axis_index("ctx").astype(jnp.int32)
-    pos = index.reshape(1)
-    line = (index // size).reshape(1)
+    pos = lax.axis_index("ctx").astype(jnp.int32).reshape(1)
     rows = beacon_hidden.shape[1]
     stats = token_stats(
         query[0], beacon_query[0], keys_values[0], grad_tokens[0], grad_beacons[0]
@@ -382,13 +372,15 @@
     weights = [beacon_weight] + [
         swap(late_weight, "ctx", step * size) for step in range(1, LINES)
     ]
-    part_kv, *blocks = partial_kv(line, hidden, weights)
+    part_kv, *blocks = partial_kv(pos, hidden, weights)
+    part_kv, stats = lax.optimization_barrier((part_kv, stats))
     own_kv = jnp.sum(exchange_line(part_kv).astype(jnp.float32), 0).astype(jnp.bfloat16)
     all_kv = exchange(jnp.broadcast_to(own_kv[None], (count,) + own_kv.shape))
     all_kv = all_kv.reshape(rows * count, -1)
     columns = [blocks[0]] + [
         swap(blocks[step], "ctx", step * size) for step in range(1, LINES)
     ]
+    all_kv, columns = lax.optimization_barrier((all_kv, columns))
 
     contrib, row_stats = beacon_grads(
         pos, query[0], beacon_query[0], all_kv, grad_tokens[0], grad_beacons[0], stats
@@ -399,11 +391,14 @@
     arrived = exchange(contrib.reshape(count, rows, -1))
     arrived, others = lax.optimization_barrier((arrived, others))
     tokens_out, beacons_out, query_grad, beacon_qgrad, token_kvgrad = others
-    all_grad = exchange(sum_and_spread(arrived)).reshape(rows * count, -1)
-
-    hidden_part = hidden_grad_part(line, all_grad, weights, size)
+    own_grad = jnp.sum(arrived.astype(jnp.float32), 0).astype(jnp.bfloat16)
+    own_grad = lax.optimization_barrier(own_grad)
+    all_grad = exchange(jnp.broadcast_to(own_grad[None], (count,) + own_grad.shape))
+    all_grad = all_grad.reshape(rows * count, -1)
+
+    hidden_part = hidden_grad_part(pos, all_grad, weights, size)
     hidden_part, late_grad = lax.optimization_barrier((hidden_part, all_grad))
-    weight_part = weight_grad_part(line, late_grad, columns)
+    weight_part = weight_grad_part(pos, late_grad, columns, size)
     hidden_blocks = exchange_line(hidden_part)
     grad_weight, hidden_blocks = sum_dp(weight_part, hidden_blocks)
     hidden_grad = hidden_blocks.transpose(2, 1, 0, 3).reshape(rows, -1)

time: 111 us -> 110 us (level)
  blocking collectives: 17.7 us -> 32.4 us
  waiting for transfers between devices: 26.5 us -> 16.5 us
  starting transfers between devices: 40.3 us -> 34.3 us
  other arithmetic: 0.8 us -> 1.93 us
    all_to_all x0 -> x1, blocking collectives: none -> 15.2 us  [exchange(): return lax.all_to_all(blocks, 'ctx', 0, 0, tiled=True)]
    all_to_all x3 -> x2, waiting for transfers between devices: 16.2 us -> 3.03 us  [exchange(): return lax.all_to_all(blocks, 'ctx', 0, 0, tiled=True)]
    ppermute x10, waiting for transfers between devices: 5.58 us -> 12.7 us  [swap(): return lax.ppermute(rows, axis, pairs)]
    all_to_all x3 -> x2, starting transfers between devices: 17.4 us -> 11.4 us  [exchange(): return lax.all_to_all(blocks, 'ctx', 0, 0, tiled=True)]
    all_to_all x1, waiting for transfers between devices: 4.7 us -> 0.82 us  [exchange_line(): lax.all_to_all(blocks, 'ctx', 0, 0, axis_index_groups=groups, tiled=True)]
    reduce_sum x0 -> x1, other arithmetic: none -> 1.13 us  [shards(): own_grad = jnp.sum(arrived.astype(jnp.float32), 0).astype(jnp.bfloat16)]
    pallas_call x7 -> x6, Pallas kernels: 17.9 us -> 17 us  [call(): pl.pallas_call(kernel, out_shape=outs, in_specs=specs, out_specs=tuple((V...]
    unnamed x22 -> x16, local copies, waits for them, and re-layouts: 2.53 us -> 2.55 us
  transfers between devices with their start and end apart: 14 -> 13, of which waited for: 8 -> 7; matrix products, arithmetic and copies ran while one was open for 1% -> 1% of each run, Pallas kernels for 8% -> 8%
where the time goes in v9:
time: 110 us; the launch traced here: 109 us
  starting transfers between devices  34.3 us (31%)
  blocking collectives  32.4 us (29%)
  Pallas kernels  17 us (15%)
  waiting for transfers between devices  16.5 us (15%)
  local copies, waits for them, and re-layouts  6.19 us (6%)
  other arithmetic  1.93 us (2%)
    ppermute x10, starting transfers between devices, swap(): return lax.ppermute(rows, axis, pairs)  17.4 us
    all_to_all x2, blocking collectives, exchange_line(): lax.all_to_all(blocks, 'ctx', 0, 0, axis_index_groups=groups, tiled=True)  17.2 us
    pallas_call x6, Pallas kernels, call(): pl.pallas_call(kernel, out_shape=outs, in_specs=specs, out_specs=tuple((V...  17 us
    all_to_all x1, blocking collectives, exchange(): return lax.all_to_all(blocks, 'ctx', 0, 0, tiled=True)  15.2 us
    ppermute x10, waiting for transfers between devices, swap(): return lax.ppermute(rows, axis, pairs)  12.7 us
    all_to_all x2, starting transfers between devices, exchange(): return lax.all_to_all(blocks, 'ctx', 0, 0, tiled=True)  11.4 us
    all_to_all x1, starting transfers between devices, exchange_line(): lax.all_to_all(blocks, 'ctx', 0, 0, axis_index_groups=groups, tiled=True)  5.55 us
    all_to_all x2, waiting for transfers between devices, exchange(): return lax.all_to_all(blocks, 'ctx', 0, 0, tiled=True)  3.03 us
  transfers between devices with their start and end apart: 13, of which 7 were waited for; matrix products, arithmetic and copies ran while one was open for 1% of the time, Pallas kernels for 8%

profile of v9, /device:TPU:2, one launch (start us, length us, event | category | flops | bytes accessed | tf_op | source)
XLA Modules:
  0.0 109.1 jit_solution(7134447211571799139)
XLA Ops:
  0.6 1.1 %reshape_squeeze.3 = bf16[16,4,8,112]{3,2,1,0:T(8,128)(2,1)S(1)} reshape(bf16[1,16,3584]{2,1,0:T(8,128)(2,1)} %param.10) | data formatting | bytes 229376 | tf_op jit(solution)/shard_map/reshape;squeeze | solution.py:369
  1.7 0.0 copy-start.4
  1.7 0.0 copy-start.5
  1.8 0.7 copy.17
  2.5 0.2 copy-done.4
  2.6 3.0 %collective-permute-start.2 = (bf16[112,512]{1,0:T(8,128)(2,1)S(1)}, bf16[112,512]{1,0:T(8,128)(2,1)S(1)}, u32[]{:S(2)}, u32[]{:S(2)}) collective-permute-start(bf16[112,512]{1,0:T(8,128)(2,1)S(1)} %copy-done.4), channel_id=1, source_target_pairs={{0,24},{1,25},{2,26},{3,27},{4,28},{5,29},{6,30},{7,31},{8,16},{9,... | collective-permute-start | bytes 344072 | tf_op jit(solution)/shard_map/ppermute | solution.py:348
  5.7 0.6 collective-permute-start.1
  6.3 0.5 collective-permute-start
  6.7 5.6 %all-to-all-start = ((bf16[8,4,16,112]{3,2,1,0:T(8,128)(2,1)}), bf16[8,4,16,112]{3,2,1,0:T(8,128)(2,1)S(1)}, u32[]{:S(2)}, u32[]{:S(2)}) async-start(bf16[8,4,16,112]{3,2,1,0:T(8,128)(2,1)} %bitcast.19), calls=%async_computation | async-start | bytes 262144 | tf_op jit(solution)/shard_map/all_to_all | solution.py:343
  12.3 0.0 copy-start
  12.3 1.2 %copy-done = bf16[1,256,1792]{2,1,0:T(8,128)(2,1)S(1)} copy-done((bf16[1,256,1792]{2,1,0:T(8,128)(2,1)S(1)}, bf16[1,256,1792]{2,1,0:T(8,128)(2,1)}, u32[]{:S(2)}) %copy-start) | copy-done | bytes 917528
  13.5 1.2 %copy-done.2 = bf16[1,256,1792]{2,1,0:T(8,128)(2,1)S(1)} copy-done((bf16[1,256,1792]{2,1,0:T(8,128)(2,1)S(1)}, bf16[1,256,1792]{2,1,0:T(8,128)(2,1)}, u32[]{:S(2)}) %copy-start.2) | copy-done | bytes 917528
  14.7 1.5 %shard_map.127.stats_ref = f32[3,2,8,256]{3,2,1,0:T(8,128)S(1)} custom-call(bf16[256,1792]{1,0:T(8,128)(2,1)S(1)} %bitcast.22, bf16[16,1792]{1,0:T(8,128)(2,1)S(1)} %bitcast.32, bf16[256,512]{1,0:T(8,128)(2,1)S(1)} %bitcast.30, bf16[256,1792]{1,0:T(8,128)(2,1)S(1)} %bitcast.25, bf16[16,1792]{1,0:T(8,128)(2,1)S(1)} %bitcast.35), custom_call_target="tpu_custom_call" | custom-call | flops 536870912 | bytes 4194304 | tf_op jit(solution)/shard_map/pallas_call | solution.py:204
  16.2 0.8 all-to-all-done.hidden_ref
  17.0 0.3 shard_map.126
  17.3 0.0 copy-start.3
  17.3 8.6 %all_to_all.30 = bf16[8,16,512]{2,1,0:T(8,128)(2,1)S(1)} all-to-all(bf16[8,16,512]{2,1,0:T(8,128)(2,1)S(1)} %get-tuple-element.41), channel_id=1, replica_groups={{0,1,2,3,4,5,6,7},{8,9,10,11,12,13,14,15},{16,17,18,19,20,21,22,23},{24..., dimensions={0} | all-to-all | bytes 262144 | tf_op jit(solution)/shard_map/all_to_all | solution.py:343
  26.0 0.9 broadcast_in_dim.27
  26.8 5.9 %all-to-all-start.2 = ((bf16[32,16,512]{2,1,0:T(8,128)(2,1)}), bf16[32,16,512]{2,1,0:T(8,128)(2,1)S(1)}, u32[]{:S(2)}, u32[]{:S(2)}) async-start(bf16[32,16,512]{2,1,0:T(8,128)(2,1)} %broadcast_in_dim.27), calls=%async_computation.2 | async-start | bytes 1048576 | tf_op jit(solution)/shard_map/all_to_all | solution.py:337
  32.8 1.6 %collective-permute-start.3 = (bf16[128,112]{1,0:T(8,128)(2,1)S(1)}, bf16[128,112]{1,0:T(8,128)(2,1)S(1)}, u32[]{:S(2)}, u32[]{:S(2)}) collective-permute-start(bf16[128,112]{1,0:T(8,128)(2,1)S(1)} %get-tuple-element.43), channel_id=1, source_target_pairs={{0,8},{1,9},{2,10},{3,11},{4,12},{5,13},{6,14},{7,15},{8,0},{9,1},... | collective-permute-start | bytes 86024 | tf_op jit(solution)/shard_map/ppermute | solution.py:348
  34.3 2.7 %collective-permute-start.4 = (bf16[128,112]{1,0:T(8,128)(2,1)S(1)}, bf16[128,112]{1,0:T(8,128)(2,1)S(1)}, u32[]{:S(2)}, u32[]{:S(2)}) collective-permute-start(bf16[128,112]{1,0:T(8,128)(2,1)S(1)} %get-tuple-element.44), channel_id=1, source_target_pairs={{0,16},{1,17},{2,18},{3,19},{4,20},{5,21},{6,22},{7,23},{8,24},{9,... | collective-permute-start | bytes 86024 | tf_op jit(solution)/shard_map/ppermute | solution.py:348
  37.1 0.5 collective-permute-start.5
  37.6 4.1 %collective-permute-done.3.h1_ref = bf16[128,112]{1,0:T(8,128)(2,1)S(1)} collective-permute-done((bf16[128,112]{1,0:T(8,128)(2,1)S(1)}, bf16[128,112]{1,0:T(8,128)(2,1)S(1)}, u32[]{:S(2)}, u32[]{:S(2)}) %collective-permute-start.3) | collective-permute-done | bytes 28704 | tf_op jit(solution)/shard_map/ppermute | solution.py:348
  41.7 2.3 %collective-permute-done.4.h2_ref = bf16[128,112]{1,0:T(8,128)(2,1)S(1)} collective-permute-done((bf16[128,112]{1,0:T(8,128)(2,1)S(1)}, bf16[128,112]{1,0:T(8,128)(2,1)S(1)}, u32[]{:S(2)}, u32[]{:S(2)}) %collective-permute-start.4) | collective-permute-done | bytes 28704 | tf_op jit(solution)/shard_map/ppermute | solution.py:348
  43.9 0.2 collective-permute-done.5.h3_ref
  44.1 0.0 all-to-all-done.2
  44.1 7.1 %shard_map.128 = (bf16[512,512]{1,0:T(8,128)(2,1)}, f32[2,2,8,256]{3,2,1,0:T(8,128)S(1)}) custom-call(s32[1]{0:T(128)} %bitcast.pos_ref, bf16[256,1792]{1,0:T(8,128)(2,1)S(1)} %bitcast.23, bf16[16,1792]{1,0:T(8,128)(2,1)S(1)} %bitcast.33, bf16[512,512]{1,0:T(8,128)(2,1)S(1)} %bitcast.28, bf16[256,1792]{1,0:T(8,128)(2,1)S(1)} %bitcast.26, ...), custom_call_target="tpu_custom_call" | custom-call | flops 2147483648 | bytes 4194304 | tf_op jit(solution)/shard_map/pallas_call | solution.py:204
  51.2 5.4 %all-to-all-start.3 = ((bf16[32,16,512]{2,1,0:T(8,128)(2,1)}), bf16[32,16,512]{2,1,0:T(8,128)(2,1)}, u32[]{:S(2)}, u32[]{:S(2)}) async-start(bf16[32,16,512]{2,1,0:T(8,128)(2,1)} %bitcast.8), calls=%async_computation.3 | async-start | bytes 1048576 | tf_op jit(solution)/shard_map/all_to_all | solution.py:337
  56.7 7.5 %shard_map.129 = (bf16[256,1792]{1,0:T(8,128)(2,1)}, bf16[16,1792]{1,0:T(8,128)(2,1)}, bf16[256,1792]{1,0:T(8,128)(2,1)}, bf16[16,1792]{1,0:T(8,128)(2,1)}, bf16[256,512]{1,0:T(8,128)(2,1)}) custom-call(s32[1]{0:T(128)} %bitcast.pos_ref, bf16[256,1792]{1,0:T(8,128)(2,1)S(1)} %bitcast.24, bf16[16,1792]{1,0:T(8,128)(2,1)S(1)} %bitcast.34, ...), custom_call_target="tpu_custom_call" | custom-call | flops 4026531840 | bytes 4194304 | tf_op jit(solution)/shard_map/pallas_call | solution.py:204
  64.2 3.0 %all-to-all-done.3 = bf16[32,16,512]{2,1,0:T(8,128)(2,1)} async-done(((bf16[32,16,512]{2,1,0:T(8,128)(2,1)}), bf16[32,16,512]{2,1,0:T(8,128)(2,1)}, u32[]{:S(2)}, u32[]{:S(2)}) %all-to-all-start.3) | async-done | bytes 524320 | tf_op jit(solution)/shard_map/all_to_all | solution.py:337
  67.2 1.1 %reduce_sum.25 = bf16[16,512]{1,0:T(8,128)(2,1)S(1)} reduce(bf16[32,16,512]{2,1,0:T(8,128)(2,1)} %all-to-all-done.3, bf16[]{:T(256)} %constant.7.clone.1), dimensions={0}, to_apply=%region_1.0 | reduce | flops 253952 | bytes 540674 | tf_op jit(solution)/shard_map/reduce_sum | solution.py:394
  68.3 0.1 broadcast_in_dim.33
  68.4 15.2 %all_to_all.31 = bf16[32,16,512]{2,1,0:T(8,128)(2,1)S(1)} all-to-all(bf16[32,16,512]{2,1,0:T(8,128)(2,1)S(1)} %broadcast_in_dim.33), channel_id=1, replica_groups=mesh['dp'=8,'ctx'=32] {'ctx'}, dimensions={0} | all-to-all | bytes 1048576 | tf_op jit(solution)/shard_map/all_to_all | solution.py:337
  83.6 0.3 shard_map.130
  83.9 0.3 shard_map.131
  84.2 6.0 %collective-permute-start.8 = (bf16[112,512]{1,0:T(8,128)(2,1)S(1)}, bf16[112,512]{1,0:T(8,128)(2,1)S(1)}, u32[]{:S(2)}, u32[]{:S(2)}) collective-permute-start(bf16[112,512]{1,0:T(8,128)(2,1)S(1)} %shard_map.131), channel_id=1, source_target_pairs={{0,224},{32,192},{64,160},{96,128},{128,96},{160,64},{192,32},{224... | collective-permute-start | bytes 344072 | tf_op jit(solution)/shard_map/ppermute | solution.py:348
  90.2 1.0 collective-permute-start.7
  91.2 1.5 %collective-permute-start.6 = (bf16[112,512]{1,0:T(8,128)(2,1)S(1)}, bf16[112,512]{1,0:T(8,128)(2,1)S(1)}, u32[]{:S(2)}, u32[]{:S(2)}) collective-permute-start(bf16[112,512]{1,0:T(8,128)(2,1)S(1)} %shard_map.131), channel_id=1, source_target_pairs={{0,64},{32,96},{64,0},{96,32},{128,192},{160,224},{192,128},{224,1... | collective-permute-start | bytes 344072 | tf_op jit(solution)/shard_map/ppermute | solution.py:348
  92.6 8.5 %all_to_all.32 = bf16[8,4,16,112]{3,2,1,0:T(8,128)(2,1)S(1)} all-to-all(bf16[8,4,16,112]{3,2,1,0:T(8,128)(2,1)S(1)} %shard_map.130), channel_id=1, replica_groups={{0,1,2,3,4,5,6,7},{8,9,10,11,12,13,14,15},{16,17,18,19,20,21,22,23},{24..., dimensions={0} | all-to-all | bytes 229376 | tf_op jit(solution)/shard_map/all_to_all | solution.py:343
  101.2 0.0 collective-permute-done.8
  101.2 0.0 collective-permute-done.7
  101.2 2.3 %collective-permute-done.6 = bf16[112,512]{1,0:T(8,128)(2,1)S(1)} collective-permute-done((bf16[112,512]{1,0:T(8,128)(2,1)S(1)}, bf16[112,512]{1,0:T(8,128)(2,1)S(1)}, u32[]{:S(2)}, u32[]{:S(2)}) %collective-permute-start.6) | collective-permute-done | bytes 114720 | tf_op jit(solution)/shard_map/ppermute | solution.py:348
  103.5 0.1 add_convert_fusion
  103.5 0.1 collective-permute-start.9
  103.7 0.1 copy.15
  103.7 0.8 broadcast_in_dim_reshape.3
  104.6 3.8 %collective-permute-done.9 = bf16[112,512]{1,0:T(8,128)(2,1)S(1)} collective-permute-done((bf16[112,512]{1,0:T(8,128)(2,1)S(1)}, bf16[112,512]{1,0:T(8,128)(2,1)S(1)}, u32[]{:S(2)}, u32[]{:S(2)}) %collective-permute-start.9) | collective-permute-done | bytes 114720 | tf_op jit(solution)/shard_map/ppermute | solution.py:348
  108.4 0.7 convert_add_fusion
  (13 shorter events, 0.0 us)
Async XLA Ops:
  1.7 0.9 copy-start.4
  1.7 10.5 %copy-start.5 = (bf16[1,256,512]{2,1,0:T(8,128)(2,1)S(1)}, bf16[1,256,512]{2,1,0:T(8,128)(2,1)}, u32[]{:S(2)}) copy-start(bf16[1,256,512]{2,1,0:T(8,128)(2,1)} %param.8) | copy-start | bytes 786436
  2.6 9.7 %copy-start.6 = (bf16[1,16,1792]{2,1,0:T(8,128)(2,1)S(1)}, bf16[1,16,1792]{2,1,0:T(8,128)(2,1)}, u32[]{:S(2)}) copy-start(bf16[1,16,1792]{2,1,0:T(8,128)(2,1)} %param.9) | copy-start | bytes 172036
  2.6 9.7 %copy-start.7 = (bf16[1,16,1792]{2,1,0:T(8,128)(2,1)S(1)}, bf16[1,16,1792]{2,1,0:T(8,128)(2,1)}, u32[]{:S(2)}) copy-start(bf16[1,16,1792]{2,1,0:T(8,128)(2,1)} %param.13) | copy-start | bytes 172036
  2.6 14.4 %collective-permute-start.2 = (bf16[112,512]{1,0:T(8,128)(2,1)S(1)}, bf16[112,512]{1,0:T(8,128)(2,1)S(1)}, u32[]{:S(2)}, u32[]{:S(2)}) collective-permute-start(bf16[112,512]{1,0:T(8,128)(2,1)S(1)} %copy-done.4), channel_id=1, source_target_pairs={{0,24},{1,25},{2,26},{3,27},{4,28},{5,29},{6,30},{7,31},{8,16},{9,... | collective-permute-start | bytes 344072 | tf_op jit(solution)/shard_map/ppermute | solution.py:348
  5.7 11.3 %collective-permute-start.1 = (bf16[112,512]{1,0:T(8,128)(2,1)S(1)}, bf16[112,512]{1,0:T(8,128)(2,1)S(1)}, u32[]{:S(2)}, u32[]{:S(2)}) collective-permute-start(bf16[112,512]{1,0:T(8,128)(2,1)S(1)} %copy-done.4), channel_id=1, source_target_pairs={{0,16},{1,17},{2,18},{3,19},{4,20},{5,21},{6,22},{7,23},{8,24},{9,... | collective-permute-start | bytes 344072 | tf_op jit(solution)/shard_map/ppermute | solution.py:348
  6.3 10.7 %collective-permute-start = (bf16[112,512]{1,0:T(8,128)(2,1)S(1)}, bf16[112,512]{1,0:T(8,128)(2,1)S(1)}, u32[]{:S(2)}, u32[]{:S(2)}) collective-permute-start(bf16[112,512]{1,0:T(8,128)(2,1)S(1)} %copy-done.4), channel_id=1, source_target_pairs={{0,8},{1,9},{2,10},{3,11},{4,12},{5,13},{6,14},{7,15},{8,0},{9,1},... | collective-permute-start | bytes 344072 | tf_op jit(solution)/shard_map/ppermute | solution.py:348
  6.7 10.3 %all-to-all-start = ((bf16[8,4,16,112]{3,2,1,0:T(8,128)(2,1)}), bf16[8,4,16,112]{3,2,1,0:T(8,128)(2,1)S(1)}, u32[]{:S(2)}, u32[]{:S(2)}) async-start(bf16[8,4,16,112]{3,2,1,0:T(8,128)(2,1)} %bitcast.19), calls=%async_computation | async-start | bytes 262144 | tf_op jit(solution)/shard_map/all_to_all | solution.py:343
  12.3 1.2 %copy-start = (bf16[1,256,1792]{2,1,0:T(8,128)(2,1)S(1)}, bf16[1,256,1792]{2,1,0:T(8,128)(2,1)}, u32[]{:S(2)}) copy-start(bf16[1,256,1792]{2,1,0:T(8,128)(2,1)} %param.7) | copy-start | bytes 2752516
  13.5 1.2 %copy-start.2 = (bf16[1,256,1792]{2,1,0:T(8,128)(2,1)S(1)}, bf16[1,256,1792]{2,1,0:T(8,128)(2,1)}, u32[]{:S(2)}) copy-start(bf16[1,256,1792]{2,1,0:T(8,128)(2,1)} %param.12) | copy-start | bytes 2752516
  17.3 26.8 %copy-start.3 = (bf16[1,256,1792]{2,1,0:T(8,128)(2,1)S(1)}, bf16[1,256,1792]{2,1,0:T(8,128)(2,1)}, u32[]{:S(2)}) copy-start(bf16[1,256,1792]{2,1,0:T(8,128)(2,1)} %param.12) | copy-start | bytes 2752516
  26.0 18.2 %copy-start.1 = (bf16[1,256,1792]{2,1,0:T(8,128)(2,1)S(1)}, bf16[1,256,1792]{2,1,0:T(8,128)(2,1)}, u32[]{:S(2)}) copy-start(bf16[1,256,1792]{2,1,0:T(8,128)(2,1)} %param.7) | copy-start | bytes 2752516
  26.8 17.3 %all-to-all-start.2 = ((bf16[32,16,512]{2,1,0:T(8,128)(2,1)}), bf16[32,16,512]{2,1,0:T(8,128)(2,1)S(1)}, u32[]{:S(2)}, u32[]{:S(2)}) async-start(bf16[32,16,512]{2,1,0:T(8,128)(2,1)} %broadcast_in_dim.27), calls=%async_computation.2 | async-start | bytes 1048576 | tf_op jit(solution)/shard_map/all_to_all | solution.py:337
  32.8 8.9 %collective-permute-start.3 = (bf16[128,112]{1,0:T(8,128)(2,1)S(1)}, bf16[128,112]{1,0:T(8,128)(2,1)S(1)}, u32[]{:S(2)}, u32[]{:S(2)}) collective-permute-start(bf16[128,112]{1,0:T(8,128)(2,1)S(1)} %get-tuple-element.43), channel_id=1, source_target_pairs={{0,8},{1,9},{2,10},{3,11},{4,12},{5,13},{6,14},{7,15},{8,0},{9,1},... | collective-permute-start | bytes 86024 | tf_op jit(solution)/shard_map/ppermute | solution.py:348
  34.3 9.6 %collective-permute-start.4 = (bf16[128,112]{1,0:T(8,128)(2,1)S(1)}, bf16[128,112]{1,0:T(8,128)(2,1)S(1)}, u32[]{:S(2)}, u32[]{:S(2)}) collective-permute-start(bf16[128,112]{1,0:T(8,128)(2,1)S(1)} %get-tuple-element.44), channel_id=1, source_target_pairs={{0,16},{1,17},{2,18},{3,19},{4,20},{5,21},{6,22},{7,23},{8,24},{9,... | collective-permute-start | bytes 86024 | tf_op jit(solution)/shard_map/ppermute | solution.py:348
  37.1 7.0 %collective-permute-start.5 = (bf16[128,112]{1,0:T(8,128)(2,1)S(1)}, bf16[128,112]{1,0:T(8,128)(2,1)S(1)}, u32[]{:S(2)}, u32[]{:S(2)}) collective-permute-start(bf16[128,112]{1,0:T(8,128)(2,1)S(1)} %get-tuple-element.45), channel_id=1, source_target_pairs={{0,24},{1,25},{2,26},{3,27},{4,28},{5,29},{6,30},{7,31},{8,16},{9,... | collective-permute-start | bytes 86024 | tf_op jit(solution)/shard_map/ppermute | solution.py:348
  51.2 16.0 %all-to-all-start.3 = ((bf16[32,16,512]{2,1,0:T(8,128)(2,1)}), bf16[32,16,512]{2,1,0:T(8,128)(2,1)}, u32[]{:S(2)}, u32[]{:S(2)}) async-start(bf16[32,16,512]{2,1,0:T(8,128)(2,1)} %bitcast.8), calls=%async_computation.3 | async-start | bytes 1048576 | tf_op jit(solution)/shard_map/all_to_all | solution.py:337
  84.2 17.0 %collective-permute-start.8 = (bf16[112,512]{1,0:T(8,128)(2,1)S(1)}, bf16[112,512]{1,0:T(8,128)(2,1)S(1)}, u32[]{:S(2)}, u32[]{:S(2)}) collective-permute-start(bf16[112,512]{1,0:T(8,128)(2,1)S(1)} %shard_map.131), channel_id=1, source_target_pairs={{0,224},{32,192},{64,160},{96,128},{128,96},{160,64},{192,32},{224... | collective-permute-start | bytes 344072 | tf_op jit(solution)/shard_map/ppermute | solution.py:348
  90.2 11.0 %collective-permute-start.7 = (bf16[112,512]{1,0:T(8,128)(2,1)S(1)}, bf16[112,512]{1,0:T(8,128)(2,1)S(1)}, u32[]{:S(2)}, u32[]{:S(2)}) collective-permute-start(bf16[112,512]{1,0:T(8,128)(2,1)S(1)} %shard_map.131), channel_id=1, source_target_pairs={{0,160},{32,128},{64,224},{96,192},{128,32},{160,0},{192,96},{224,... | collective-permute-start | bytes 344072 | tf_op jit(solution)/shard_map/ppermute | solution.py:348
  91.2 12.3 %collective-permute-start.6 = (bf16[112,512]{1,0:T(8,128)(2,1)S(1)}, bf16[112,512]{1,0:T(8,128)(2,1)S(1)}, u32[]{:S(2)}, u32[]{:S(2)}) collective-permute-start(bf16[112,512]{1,0:T(8,128)(2,1)S(1)} %shard_map.131), channel_id=1, source_target_pairs={{0,64},{32,96},{64,0},{96,32},{128,192},{160,224},{192,128},{224,1... | collective-permute-start | bytes 344072 | tf_op jit(solution)/shard_map/ppermute | solution.py:348
  103.5 4.9 %collective-permute-start.9 = (bf16[112,512]{1,0:T(8,128)(2,1)S(1)}, bf16[112,512]{1,0:T(8,128)(2,1)S(1)}, u32[]{:S(2)}, u32[]{:S(2)}) collective-permute-start(bf16[112,512]{1,0:T(8,128)(2,1)S(1)} %add_convert_fusion), channel_id=1, source_target_pairs={{0,32},{32,0},{64,96},{96,64},{128,160},{160,128},{192,224},{224,1... | collective-permute-start | bytes 344072 | tf_op jit(solution)/shard_map/ppermute | solution.py:348

commit v10 on v9

--- a/solution.py
+++ b/solution.py
@@ -349,7 +349,7 @@
 
 
 def sum_dp(sent, beside):
-    near, far, wide = [swap(sent, "dp", mask).astype(jnp.float32) for mask in (2, 5, 7)]
+    near, far, wide = [swap(sent, "dp", mask).astype(jnp.float32) for mask in (3, 5, 6)]
     sent, beside = lax.optimization_barrier((sent, beside))
     sent = ((sent.astype(jnp.float32) + near) + (far + wide)).astype(jnp.bfloat16)
     return sent.astype(jnp.float32) + swap(sent, "dp", 1).astype(jnp.float32), beside

time: 110 us -> 109 us (level)
  waiting for transfers between devices: 16.5 us -> 13.5 us
  starting transfers between devices: 34.3 us -> 36.3 us
    ppermute x10, waiting for transfers between devices: 12.7 us -> 9.69 us  [swap(): return lax.ppermute(rows, axis, pairs)]
    ppermute x10, starting transfers between devices: 17.4 us -> 19.4 us  [swap(): return lax.ppermute(rows, axis, pairs)]
  transfers between devices with their start and end apart: 13 -> 13, of which waited for: 7 -> 8; matrix products, arithmetic and copies ran while one was open for 1% -> 1% of each run, Pallas kernels for 8% -> 8%
where the time goes in v10:
time: 109 us; the launch traced here: 108 us
  starting transfers between devices  36.3 us (33%)
  blocking collectives  32.4 us (30%)
  Pallas kernels  17 us (16%)
  waiting for transfers between devices  13.5 us (12%)
  local copies, waits for them, and re-layouts  6.19 us (6%)
  other arithmetic  1.93 us (2%)
    ppermute x10, starting transfers between devices, swap(): return lax.ppermute(rows, axis, pairs)  19.4 us
    all_to_all x2, blocking collectives, exchange_line(): lax.all_to_all(blocks, 'ctx', 0, 0, axis_index_groups=groups, tiled=True)  17.2 us
    pallas_call x6, Pallas kernels, call(): pl.pallas_call(kernel, out_shape=outs, in_specs=specs, out_specs=tuple((V...  17 us
    all_to_all x1, blocking collectives, exchange(): return lax.all_to_all(blocks, 'ctx', 0, 0, tiled=True)  15.2 us
    all_to_all x2, starting transfers between devices, exchange(): return lax.all_to_all(blocks, 'ctx', 0, 0, tiled=True)  11.4 us
    ppermute x10, waiting for transfers between devices, swap(): return lax.ppermute(rows, axis, pairs)  9.69 us
    all_to_all x1, starting transfers between devices, exchange_line(): lax.all_to_all(blocks, 'ctx', 0, 0, axis_index_groups=groups, tiled=True)  5.55 us
    all_to_all x2, waiting for transfers between devices, exchange(): return lax.all_to_all(blocks, 'ctx', 0, 0, tiled=True)  3.03 us
  transfers between devices with their start and end apart: 13, of which 8 were waited for; matrix products, arithmetic and copies ran while one was open for 1% of the time, Pallas kernels for 8%

profile of v10, /device:TPU:2, one launch (start us, length us, event | category | flops | bytes accessed | tf_op | source)
XLA Modules:
  0.0 108.1 jit_solution(13975771524125557016)
XLA Ops:
  0.6 1.1 %reshape_squeeze.3 = bf16[16,4,8,112]{3,2,1,0:T(8,128)(2,1)S(1)} reshape(bf16[1,16,3584]{2,1,0:T(8,128)(2,1)} %param.10) | data formatting | bytes 229376 | tf_op jit(solution)/shard_map/reshape;squeeze | solution.py:369
  1.7 0.0 copy-start.4
  1.7 0.0 copy-start.5
  1.8 0.7 copy.17
  2.5 0.2 copy-done.4
  2.6 3.0 %collective-permute-start.2 = (bf16[112,512]{1,0:T(8,128)(2,1)S(1)}, bf16[112,512]{1,0:T(8,128)(2,1)S(1)}, u32[]{:S(2)}, u32[]{:S(2)}) collective-permute-start(bf16[112,512]{1,0:T(8,128)(2,1)S(1)} %copy-done.4), channel_id=1, source_target_pairs={{0,24},{1,25},{2,26},{3,27},{4,28},{5,29},{6,30},{7,31},{8,16},{9,... | collective-permute-start | bytes 344072 | tf_op jit(solution)/shard_map/ppermute | solution.py:348
  5.7 0.6 collective-permute-start.1
  6.3 0.5 collective-permute-start
  6.7 5.6 %all-to-all-start = ((bf16[8,4,16,112]{3,2,1,0:T(8,128)(2,1)}), bf16[8,4,16,112]{3,2,1,0:T(8,128)(2,1)S(1)}, u32[]{:S(2)}, u32[]{:S(2)}) async-start(bf16[8,4,16,112]{3,2,1,0:T(8,128)(2,1)} %bitcast.19), calls=%async_computation | async-start | bytes 262144 | tf_op jit(solution)/shard_map/all_to_all | solution.py:343
  12.3 0.0 copy-start
  12.3 1.2 %copy-done = bf16[1,256,1792]{2,1,0:T(8,128)(2,1)S(1)} copy-done((bf16[1,256,1792]{2,1,0:T(8,128)(2,1)S(1)}, bf16[1,256,1792]{2,1,0:T(8,128)(2,1)}, u32[]{:S(2)}) %copy-start) | copy-done | bytes 917528
  13.5 1.2 %copy-done.2 = bf16[1,256,1792]{2,1,0:T(8,128)(2,1)S(1)} copy-done((bf16[1,256,1792]{2,1,0:T(8,128)(2,1)S(1)}, bf16[1,256,1792]{2,1,0:T(8,128)(2,1)}, u32[]{:S(2)}) %copy-start.2) | copy-done | bytes 917528
  14.7 1.5 %shard_map.127.stats_ref = f32[3,2,8,256]{3,2,1,0:T(8,128)S(1)} custom-call(bf16[256,1792]{1,0:T(8,128)(2,1)S(1)} %bitcast.22, bf16[16,1792]{1,0:T(8,128)(2,1)S(1)} %bitcast.32, bf16[256,512]{1,0:T(8,128)(2,1)S(1)} %bitcast.30, bf16[256,1792]{1,0:T(8,128)(2,1)S(1)} %bitcast.25, bf16[16,1792]{1,0:T(8,128)(2,1)S(1)} %bitcast.35), custom_call_target="tpu_custom_call" | custom-call | flops 536870912 | bytes 4194304 | tf_op jit(solution)/shard_map/pallas_call | solution.py:204
  16.2 0.8 all-to-all-done.hidden_ref
  17.0 0.0 collective-permute-done.2.w3_ref
  17.0 0.0 collective-permute-done.1.w2_ref
  17.0 0.3 shard_map.126
  17.3 0.0 copy-start.3
  17.3 8.6 %all_to_all.30 = bf16[8,16,512]{2,1,0:T(8,128)(2,1)S(1)} all-to-all(bf16[8,16,512]{2,1,0:T(8,128)(2,1)S(1)} %get-tuple-element.41), channel_id=1, replica_groups={{0,1,2,3,4,5,6,7},{8,9,10,11,12,13,14,15},{16,17,18,19,20,21,22,23},{24..., dimensions={0} | all-to-all | bytes 262144 | tf_op jit(solution)/shard_map/all_to_all | solution.py:343
  26.0 0.9 broadcast_in_dim.27
  26.8 5.9 %all-to-all-start.2 = ((bf16[32,16,512]{2,1,0:T(8,128)(2,1)}), bf16[32,16,512]{2,1,0:T(8,128)(2,1)S(1)}, u32[]{:S(2)}, u32[]{:S(2)}) async-start(bf16[32,16,512]{2,1,0:T(8,128)(2,1)} %broadcast_in_dim.27), calls=%async_computation.2 | async-start | bytes 1048576 | tf_op jit(solution)/shard_map/all_to_all | solution.py:337
  32.8 1.6 %collective-permute-start.3 = (bf16[128,112]{1,0:T(8,128)(2,1)S(1)}, bf16[128,112]{1,0:T(8,128)(2,1)S(1)}, u32[]{:S(2)}, u32[]{:S(2)}) collective-permute-start(bf16[128,112]{1,0:T(8,128)(2,1)S(1)} %get-tuple-element.43), channel_id=1, source_target_pairs={{0,8},{1,9},{2,10},{3,11},{4,12},{5,13},{6,14},{7,15},{8,0},{9,1},... | collective-permute-start | bytes 86024 | tf_op jit(solution)/shard_map/ppermute | solution.py:348
  34.3 2.7 %collective-permute-start.4 = (bf16[128,112]{1,0:T(8,128)(2,1)S(1)}, bf16[128,112]{1,0:T(8,128)(2,1)S(1)}, u32[]{:S(2)}, u32[]{:S(2)}) collective-permute-start(bf16[128,112]{1,0:T(8,128)(2,1)S(1)} %get-tuple-element.44), channel_id=1, source_target_pairs={{0,16},{1,17},{2,18},{3,19},{4,20},{5,21},{6,22},{7,23},{8,24},{9,... | collective-permute-start | bytes 86024 | tf_op jit(solution)/shard_map/ppermute | solution.py:348
  37.1 0.5 collective-permute-start.5
  37.6 4.1 %collective-permute-done.3.h1_ref = bf16[128,112]{1,0:T(8,128)(2,1)S(1)} collective-permute-done((bf16[128,112]{1,0:T(8,128)(2,1)S(1)}, bf16[128,112]{1,0:T(8,128)(2,1)S(1)}, u32[]{:S(2)}, u32[]{:S(2)}) %collective-permute-start.3) | collective-permute-done | bytes 28704 | tf_op jit(solution)/shard_map/ppermute | solution.py:348
  41.7 2.3 %collective-permute-done.4.h2_ref = bf16[128,112]{1,0:T(8,128)(2,1)S(1)} collective-permute-done((bf16[128,112]{1,0:T(8,128)(2,1)S(1)}, bf16[128,112]{1,0:T(8,128)(2,1)S(1)}, u32[]{:S(2)}, u32[]{:S(2)}) %collective-permute-start.4) | collective-permute-done | bytes 28704 | tf_op jit(solution)/shard_map/ppermute | solution.py:348
  43.9 0.2 collective-permute-done.5.h3_ref
  44.1 7.1 %shard_map.128 = (bf16[512,512]{1,0:T(8,128)(2,1)}, f32[2,2,8,256]{3,2,1,0:T(8,128)S(1)}) custom-call(s32[1]{0:T(128)} %bitcast.pos_ref, bf16[256,1792]{1,0:T(8,128)(2,1)S(1)} %bitcast.23, bf16[16,1792]{1,0:T(8,128)(2,1)S(1)} %bitcast.33, bf16[512,512]{1,0:T(8,128)(2,1)S(1)} %bitcast.28, bf16[256,1792]{1,0:T(8,128)(2,1)S(1)} %bitcast.26, ...), custom_call_target="tpu_custom_call" | custom-call | flops 2147483648 | bytes 4194304 | tf_op jit(solution)/shard_map/pallas_call | solution.py:204
  51.2 5.4 %all-to-all-start.3 = ((bf16[32,16,512]{2,1,0:T(8,128)(2,1)}), bf16[32,16,512]{2,1,0:T(8,128)(2,1)}, u32[]{:S(2)}, u32[]{:S(2)}) async-start(bf16[32,16,512]{2,1,0:T(8,128)(2,1)} %bitcast.8), calls=%async_computation.3 | async-start | bytes 1048576 | tf_op jit(solution)/shard_map/all_to_all | solution.py:337
  56.7 7.5 %shard_map.129 = (bf16[256,1792]{1,0:T(8,128)(2,1)}, bf16[16,1792]{1,0:T(8,128)(2,1)}, bf16[256,1792]{1,0:T(8,128)(2,1)}, bf16[16,1792]{1,0:T(8,128)(2,1)}, bf16[256,512]{1,0:T(8,128)(2,1)}) custom-call(s32[1]{0:T(128)} %bitcast.pos_ref, bf16[256,1792]{1,0:T(8,128)(2,1)S(1)} %bitcast.24, bf16[16,1792]{1,0:T(8,128)(2,1)S(1)} %bitcast.34, ...), custom_call_target="tpu_custom_call" | custom-call | flops 4026531840 | bytes 4194304 | tf_op jit(solution)/shard_map/pallas_call | solution.py:204
  64.2 3.0 %all-to-all-done.3 = bf16[32,16,512]{2,1,0:T(8,128)(2,1)} async-done(((bf16[32,16,512]{2,1,0:T(8,128)(2,1)}), bf16[32,16,512]{2,1,0:T(8,128)(2,1)}, u32[]{:S(2)}, u32[]{:S(2)}) %all-to-all-start.3) | async-done | bytes 524320 | tf_op jit(solution)/shard_map/all_to_all | solution.py:337
  67.2 1.1 %reduce_sum.25 = bf16[16,512]{1,0:T(8,128)(2,1)S(1)} reduce(bf16[32,16,512]{2,1,0:T(8,128)(2,1)} %all-to-all-done.3, bf16[]{:T(256)} %constant.7.clone.1), dimensions={0}, to_apply=%region_1.0 | reduce | flops 253952 | bytes 540674 | tf_op jit(solution)/shard_map/reduce_sum | solution.py:394
  68.3 0.1 broadcast_in_dim.33
  68.4 15.2 %all_to_all.31 = bf16[32,16,512]{2,1,0:T(8,128)(2,1)S(1)} all-to-all(bf16[32,16,512]{2,1,0:T(8,128)(2,1)S(1)} %broadcast_in_dim.33), channel_id=1, replica_groups=mesh['dp'=8,'ctx'=32] {'ctx'}, dimensions={0} | all-to-all | bytes 1048576 | tf_op jit(solution)/shard_map/all_to_all | solution.py:337
  83.6 0.3 shard_map.130
  83.9 0.3 shard_map.131
  84.2 6.4 %collective-permute-start.8 = (bf16[112,512]{1,0:T(8,128)(2,1)S(1)}, bf16[112,512]{1,0:T(8,128)(2,1)S(1)}, u32[]{:S(2)}, u32[]{:S(2)}) collective-permute-start(bf16[112,512]{1,0:T(8,128)(2,1)S(1)} %shard_map.131), channel_id=1, source_target_pairs={{0,192},{32,224},{64,128},{96,160},{128,64},{160,96},{192,0},{224,... | collective-permute-start | bytes 344072 | tf_op jit(solution)/shard_map/ppermute | solution.py:348
  90.6 1.0 collective-permute-start.7
  91.6 1.5 %collective-permute-start.6 = (bf16[112,512]{1,0:T(8,128)(2,1)S(1)}, bf16[112,512]{1,0:T(8,128)(2,1)S(1)}, u32[]{:S(2)}, u32[]{:S(2)}) collective-permute-start(bf16[112,512]{1,0:T(8,128)(2,1)S(1)} %shard_map.131), channel_id=1, source_target_pairs={{0,96},{32,64},{64,32},{96,0},{128,224},{160,192},{192,160},{224,1... | collective-permute-start | bytes 344072 | tf_op jit(solution)/shard_map/ppermute | solution.py:348
  93.1 8.5 %all_to_all.32 = bf16[8,4,16,112]{3,2,1,0:T(8,128)(2,1)S(1)} all-to-all(bf16[8,4,16,112]{3,2,1,0:T(8,128)(2,1)S(1)} %shard_map.130), channel_id=1, replica_groups={{0,1,2,3,4,5,6,7},{8,9,10,11,12,13,14,15},{16,17,18,19,20,21,22,23},{24..., dimensions={0} | all-to-all | bytes 229376 | tf_op jit(solution)/shard_map/all_to_all | solution.py:343
  101.6 0.5 collective-permute-done.7
  102.1 0.4 collective-permute-done.6
  102.5 0.1 add_convert_fusion
  102.5 1.6 %collective-permute-start.9 = (bf16[112,512]{1,0:T(8,128)(2,1)S(1)}, bf16[112,512]{1,0:T(8,128)(2,1)S(1)}, u32[]{:S(2)}, u32[]{:S(2)}) collective-permute-start(bf16[112,512]{1,0:T(8,128)(2,1)S(1)} %add_convert_fusion), channel_id=1, source_target_pairs={{0,32},{32,0},{64,96},{96,64},{128,160},{160,128},{192,224},{224,1... | collective-permute-start | bytes 344072 | tf_op jit(solution)/shard_map/ppermute | solution.py:348
  104.2 0.1 copy.15
  104.3 0.8 broadcast_in_dim_reshape.3
  105.1 2.3 %collective-permute-done.9 = bf16[112,512]{1,0:T(8,128)(2,1)S(1)} collective-permute-done((bf16[112,512]{1,0:T(8,128)(2,1)S(1)}, bf16[112,512]{1,0:T(8,128)(2,1)S(1)}, u32[]{:S(2)}, u32[]{:S(2)}) %collective-permute-start.9) | collective-permute-done | bytes 114720 | tf_op jit(solution)/shard_map/ppermute | solution.py:348
  107.4 0.7 convert_add_fusion
  (13 shorter events, 0.0 us)
Async XLA Ops:
  1.7 0.9 copy-start.4
  1.7 10.5 %copy-start.5 = (bf16[1,256,512]{2,1,0:T(8,128)(2,1)S(1)}, bf16[1,256,512]{2,1,0:T(8,128)(2,1)}, u32[]{:S(2)}) copy-start(bf16[1,256,512]{2,1,0:T(8,128)(2,1)} %param.8) | copy-start | bytes 786436
  2.6 9.7 %copy-start.6 = (bf16[1,16,1792]{2,1,0:T(8,128)(2,1)S(1)}, bf16[1,16,1792]{2,1,0:T(8,128)(2,1)}, u32[]{:S(2)}) copy-start(bf16[1,16,1792]{2,1,0:T(8,128)(2,1)} %param.9) | copy-start | bytes 172036
  2.6 9.7 %copy-start.7 = (bf16[1,16,1792]{2,1,0:T(8,128)(2,1)S(1)}, bf16[1,16,1792]{2,1,0:T(8,128)(2,1)}, u32[]{:S(2)}) copy-start(bf16[1,16,1792]{2,1,0:T(8,128)(2,1)} %param.13) | copy-start | bytes 172036
  2.6 14.4 %collective-permute-start.2 = (bf16[112,512]{1,0:T(8,128)(2,1)S(1)}, bf16[112,512]{1,0:T(8,128)(2,1)S(1)}, u32[]{:S(2)}, u32[]{:S(2)}) collective-permute-start(bf16[112,512]{1,0:T(8,128)(2,1)S(1)} %copy-done.4), channel_id=1, source_target_pairs={{0,24},{1,25},{2,26},{3,27},{4,28},{5,29},{6,30},{7,31},{8,16},{9,... | collective-permute-start | bytes 344072 | tf_op jit(solution)/shard_map/ppermute | solution.py:348
  5.7 11.3 %collective-permute-start.1 = (bf16[112,512]{1,0:T(8,128)(2,1)S(1)}, bf16[112,512]{1,0:T(8,128)(2,1)S(1)}, u32[]{:S(2)}, u32[]{:S(2)}) collective-permute-start(bf16[112,512]{1,0:T(8,128)(2,1)S(1)} %copy-done.4), channel_id=1, source_target_pairs={{0,16},{1,17},{2,18},{3,19},{4,20},{5,21},{6,22},{7,23},{8,24},{9,... | collective-permute-start | bytes 344072 | tf_op jit(solution)/shard_map/ppermute | solution.py:348
  6.3 10.7 %collective-permute-start = (bf16[112,512]{1,0:T(8,128)(2,1)S(1)}, bf16[112,512]{1,0:T(8,128)(2,1)S(1)}, u32[]{:S(2)}, u32[]{:S(2)}) collective-permute-start(bf16[112,512]{1,0:T(8,128)(2,1)S(1)} %copy-done.4), channel_id=1, source_target_pairs={{0,8},{1,9},{2,10},{3,11},{4,12},{5,13},{6,14},{7,15},{8,0},{9,1},... | collective-permute-start | bytes 344072 | tf_op jit(solution)/shard_map/ppermute | solution.py:348
  6.7 10.3 %all-to-all-start = ((bf16[8,4,16,112]{3,2,1,0:T(8,128)(2,1)}), bf16[8,4,16,112]{3,2,1,0:T(8,128)(2,1)S(1)}, u32[]{:S(2)}, u32[]{:S(2)}) async-start(bf16[8,4,16,112]{3,2,1,0:T(8,128)(2,1)} %bitcast.19), calls=%async_computation | async-start | bytes 262144 | tf_op jit(solution)/shard_map/all_to_all | solution.py:343
  12.3 1.2 %copy-start = (bf16[1,256,1792]{2,1,0:T(8,128)(2,1)S(1)}, bf16[1,256,1792]{2,1,0:T(8,128)(2,1)}, u32[]{:S(2)}) copy-start(bf16[1,256,1792]{2,1,0:T(8,128)(2,1)} %param.7) | copy-start | bytes 2752516
  13.5 1.2 %copy-start.2 = (bf16[1,256,1792]{2,1,0:T(8,128)(2,1)S(1)}, bf16[1,256,1792]{2,1,0:T(8,128)(2,1)}, u32[]{:S(2)}) copy-start(bf16[1,256,1792]{2,1,0:T(8,128)(2,1)} %param.12) | copy-start | bytes 2752516
  17.3 26.8 %copy-start.3 = (bf16[1,256,1792]{2,1,0:T(8,128)(2,1)S(1)}, bf16[1,256,1792]{2,1,0:T(8,128)(2,1)}, u32[]{:S(2)}) copy-start(bf16[1,256,1792]{2,1,0:T(8,128)(2,1)} %param.12) | copy-start | bytes 2752516
  26.0 18.2 %copy-start.1 = (bf16[1,256,1792]{2,1,0:T(8,128)(2,1)S(1)}, bf16[1,256,1792]{2,1,0:T(8,128)(2,1)}, u32[]{:S(2)}) copy-start(bf16[1,256,1792]{2,1,0:T(8,128)(2,1)} %param.7) | copy-start | bytes 2752516
  26.8 17.3 %all-to-all-start.2 = ((bf16[32,16,512]{2,1,0:T(8,128)(2,1)}), bf16[32,16,512]{2,1,0:T(8,128)(2,1)S(1)}, u32[]{:S(2)}, u32[]{:S(2)}) async-start(bf16[32,16,512]{2,1,0:T(8,128)(2,1)} %broadcast_in_dim.27), calls=%async_computation.2 | async-start | bytes 1048576 | tf_op jit(solution)/shard_map/all_to_all | solution.py:337
  32.8 8.9 %collective-permute-start.3 = (bf16[128,112]{1,0:T(8,128)(2,1)S(1)}, bf16[128,112]{1,0:T(8,128)(2,1)S(1)}, u32[]{:S(2)}, u32[]{:S(2)}) collective-permute-start(bf16[128,112]{1,0:T(8,128)(2,1)S(1)} %get-tuple-element.43), channel_id=1, source_target_pairs={{0,8},{1,9},{2,10},{3,11},{4,12},{5,13},{6,14},{7,15},{8,0},{9,1},... | collective-permute-start | bytes 86024 | tf_op jit(solution)/shard_map/ppermute | solution.py:348
  34.3 9.6 %collective-permute-start.4 = (bf16[128,112]{1,0:T(8,128)(2,1)S(1)}, bf16[128,112]{1,0:T(8,128)(2,1)S(1)}, u32[]{:S(2)}, u32[]{:S(2)}) collective-permute-start(bf16[128,112]{1,0:T(8,128)(2,1)S(1)} %get-tuple-element.44), channel_id=1, source_target_pairs={{0,16},{1,17},{2,18},{3,19},{4,20},{5,21},{6,22},{7,23},{8,24},{9,... | collective-permute-start | bytes 86024 | tf_op jit(solution)/shard_map/ppermute | solution.py:348
  37.1 7.0 %collective-permute-start.5 = (bf16[128,112]{1,0:T(8,128)(2,1)S(1)}, bf16[128,112]{1,0:T(8,128)(2,1)S(1)}, u32[]{:S(2)}, u32[]{:S(2)}) collective-permute-start(bf16[128,112]{1,0:T(8,128)(2,1)S(1)} %get-tuple-element.45), channel_id=1, source_target_pairs={{0,24},{1,25},{2,26},{3,27},{4,28},{5,29},{6,30},{7,31},{8,16},{9,... | collective-permute-start | bytes 86024 | tf_op jit(solution)/shard_map/ppermute | solution.py:348
  51.2 16.0 %all-to-all-start.3 = ((bf16[32,16,512]{2,1,0:T(8,128)(2,1)}), bf16[32,16,512]{2,1,0:T(8,128)(2,1)}, u32[]{:S(2)}, u32[]{:S(2)}) async-start(bf16[32,16,512]{2,1,0:T(8,128)(2,1)} %bitcast.8), calls=%async_computation.3 | async-start | bytes 1048576 | tf_op jit(solution)/shard_map/all_to_all | solution.py:337
  84.2 17.4 %collective-permute-start.8 = (bf16[112,512]{1,0:T(8,128)(2,1)S(1)}, bf16[112,512]{1,0:T(8,128)(2,1)S(1)}, u32[]{:S(2)}, u32[]{:S(2)}) collective-permute-start(bf16[112,512]{1,0:T(8,128)(2,1)S(1)} %shard_map.131), channel_id=1, source_target_pairs={{0,192},{32,224},{64,128},{96,160},{128,64},{160,96},{192,0},{224,... | collective-permute-start | bytes 344072 | tf_op jit(solution)/shard_map/ppermute | solution.py:348
  90.6 11.5 %collective-permute-start.7 = (bf16[112,512]{1,0:T(8,128)(2,1)S(1)}, bf16[112,512]{1,0:T(8,128)(2,1)S(1)}, u32[]{:S(2)}, u32[]{:S(2)}) collective-permute-start(bf16[112,512]{1,0:T(8,128)(2,1)S(1)} %shard_map.131), channel_id=1, source_target_pairs={{0,160},{32,128},{64,224},{96,192},{128,32},{160,0},{192,96},{224,... | collective-permute-start | bytes 344072 | tf_op jit(solution)/shard_map/ppermute | solution.py:348
  91.6 10.8 %collective-permute-start.6 = (bf16[112,512]{1,0:T(8,128)(2,1)S(1)}, bf16[112,512]{1,0:T(8,128)(2,1)S(1)}, u32[]{:S(2)}, u32[]{:S(2)}) collective-permute-start(bf16[112,512]{1,0:T(8,128)(2,1)S(1)} %shard_map.131), channel_id=1, source_target_pairs={{0,96},{32,64},{64,32},{96,0},{128,224},{160,192},{192,160},{224,1... | collective-permute-start | bytes 344072 | tf_op jit(solution)/shard_map/ppermute | solution.py:348
  102.5 4.9 %collective-permute-start.9 = (bf16[112,512]{1,0:T(8,128)(2,1)S(1)}, bf16[112,512]{1,0:T(8,128)(2,1)S(1)}, u32[]{:S(2)}, u32[]{:S(2)}) collective-permute-start(bf16[112,512]{1,0:T(8,128)(2,1)S(1)} %add_convert_fusion), channel_id=1, source_target_pairs={{0,32},{32,0},{64,96},{96,64},{128,160},{160,128},{192,224},{224,1... | collective-permute-start | bytes 344072 | tf_op jit(solution)/shard_map/ppermute | solution.py:348

commit v11 on v10

--- a/solution.py
+++ b/solution.py
@@ -115,10 +115,10 @@
         total_sum = shift * sum_tok + jnp.sum(expo, 0, keepdims=True)
         inverse = 1.0 / total_sum
         centre = inverse * (shift * cen_tok + jnp.sum(expo * dweights, 0, keepdims=True))
-        probs = expo * inverse
-        dscores = (probs * (dweights - centre)).astype(jnp.bfloat16)
+        weights = (expo * inverse).astype(jnp.bfloat16)
+        dscores = weights * (dweights - centre).astype(jnp.bfloat16)
         key_grad = key_grad + dot_nn(dscores, query)
-        val_grad = val_grad + dot_nn(probs.astype(jnp.bfloat16), cot)
+        val_grad = val_grad + dot_nn(weights, cot)
         rows_ref[0, group, head : head + 1, :width] = top + jnp.log(total_sum) * LOG2E
         rows_ref[1, group, head : head + 1, :width] = centre
         if head == GROUP:
@@ -173,9 +173,8 @@
                 scores = scores + (bias_ref if head < GROUP else bbias_ref)[...]
             elif head < GROUP:
                 scores = scores + tbias_ref[...]
-            probs = jnp.exp2(scores)
-            dscores = (probs * (pairs[side][1] - centre)).astype(jnp.bfloat16)
-            weights = probs.astype(jnp.bfloat16)
+            weights = jnp.exp2(scores).astype(jnp.bfloat16)
+            dscores = weights * (pairs[side][1] - centre).astype(jnp.bfloat16)
             out = out + dot_nn(vals_t, weights)
             dquery = dquery + dot_nn(keys_t, dscores)
             if side == 1:

time: 109 us -> 109 us (level)
  no operation moved by 1% of the time
where the time goes in v11:
time: 109 us; the launch traced here: 108 us
  starting transfers between devices  36.3 us (33%)
  blocking collectives  32.4 us (30%)
  Pallas kernels  16.6 us (15%)
  waiting for transfers between devices  13.8 us (13%)
  local copies, waits for them, and re-layouts  6.19 us (6%)
  other arithmetic  1.93 us (2%)
    ppermute x10, starting transfers between devices, swap(): return lax.ppermute(rows, axis, pairs)  19.4 us
    all_to_all x2, blocking collectives, exchange_line(): lax.all_to_all(blocks, 'ctx', 0, 0, axis_index_groups=groups, tiled=True)  17.2 us
    pallas_call x6, Pallas kernels, call(): pl.pallas_call(kernel, out_shape=outs, in_specs=specs, out_specs=tuple((V...  16.6 us
    all_to_all x1, blocking collectives, exchange(): return lax.all_to_all(blocks, 'ctx', 0, 0, tiled=True)  15.2 us
    all_to_all x2, starting transfers between devices, exchange(): return lax.all_to_all(blocks, 'ctx', 0, 0, tiled=True)  11.4 us
    ppermute x10, waiting for transfers between devices, swap(): return lax.ppermute(rows, axis, pairs)  9.67 us
    all_to_all x1, starting transfers between devices, exchange_line(): lax.all_to_all(blocks, 'ctx', 0, 0, axis_index_groups=groups, tiled=True)  5.55 us
    all_to_all x2, waiting for transfers between devices, exchange(): return lax.all_to_all(blocks, 'ctx', 0, 0, tiled=True)  3.27 us
  transfers between devices with their start and end apart: 13, of which 8 were waited for; matrix products, arithmetic and copies ran while one was open for 1% of the time, Pallas kernels for 8%

profile of v11, /device:TPU:2, one launch (start us, length us, event | category | flops | bytes accessed | tf_op | source)
XLA Modules:
  0.0 107.9 jit_solution(16184187580037134700)
XLA Ops:
  0.6 1.1 %reshape_squeeze.3 = bf16[16,4,8,112]{3,2,1,0:T(8,128)(2,1)S(1)} reshape(bf16[1,16,3584]{2,1,0:T(8,128)(2,1)} %param.10) | data formatting | bytes 229376 | tf_op jit(solution)/shard_map/reshape;squeeze | solution.py:368
  1.7 0.0 copy-start.4
  1.7 0.0 copy-start.5
  1.8 0.7 copy.17
  2.5 0.2 copy-done.4
  2.6 3.0 %collective-permute-start.2 = (bf16[112,512]{1,0:T(8,128)(2,1)S(1)}, bf16[112,512]{1,0:T(8,128)(2,1)S(1)}, u32[]{:S(2)}, u32[]{:S(2)}) collective-permute-start(bf16[112,512]{1,0:T(8,128)(2,1)S(1)} %copy-done.4), channel_id=1, source_target_pairs={{0,24},{1,25},{2,26},{3,27},{4,28},{5,29},{6,30},{7,31},{8,16},{9,... | collective-permute-start | bytes 344072 | tf_op jit(solution)/shard_map/ppermute | solution.py:347
  5.7 0.6 collective-permute-start.1
  6.3 0.5 collective-permute-start
  6.7 5.6 %all-to-all-start = ((bf16[8,4,16,112]{3,2,1,0:T(8,128)(2,1)}), bf16[8,4,16,112]{3,2,1,0:T(8,128)(2,1)S(1)}, u32[]{:S(2)}, u32[]{:S(2)}) async-start(bf16[8,4,16,112]{3,2,1,0:T(8,128)(2,1)} %bitcast.19), calls=%async_computation | async-start | bytes 262144 | tf_op jit(solution)/shard_map/all_to_all | solution.py:342
  12.3 0.0 copy-start
  12.3 1.2 %copy-done = bf16[1,256,1792]{2,1,0:T(8,128)(2,1)S(1)} copy-done((bf16[1,256,1792]{2,1,0:T(8,128)(2,1)S(1)}, bf16[1,256,1792]{2,1,0:T(8,128)(2,1)}, u32[]{:S(2)}) %copy-start) | copy-done | bytes 917528
  13.5 1.2 %copy-done.2 = bf16[1,256,1792]{2,1,0:T(8,128)(2,1)S(1)} copy-done((bf16[1,256,1792]{2,1,0:T(8,128)(2,1)S(1)}, bf16[1,256,1792]{2,1,0:T(8,128)(2,1)}, u32[]{:S(2)}) %copy-start.2) | copy-done | bytes 917528
  14.7 1.5 %shard_map.127.stats_ref = f32[3,2,8,256]{3,2,1,0:T(8,128)S(1)} custom-call(bf16[256,1792]{1,0:T(8,128)(2,1)S(1)} %bitcast.22, bf16[16,1792]{1,0:T(8,128)(2,1)S(1)} %bitcast.32, bf16[256,512]{1,0:T(8,128)(2,1)S(1)} %bitcast.30, bf16[256,1792]{1,0:T(8,128)(2,1)S(1)} %bitcast.25, bf16[16,1792]{1,0:T(8,128)(2,1)S(1)} %bitcast.35), custom_call_target="tpu_custom_call" | custom-call | flops 536870912 | bytes 4194304 | tf_op jit(solution)/shard_map/pallas_call | solution.py:203
  16.2 0.8 all-to-all-done.hidden_ref
  17.0 0.0 collective-permute-done.2.w3_ref
  17.0 0.3 shard_map.126
  17.3 0.0 copy-start.3
  17.3 8.6 %all_to_all.30 = bf16[8,16,512]{2,1,0:T(8,128)(2,1)S(1)} all-to-all(bf16[8,16,512]{2,1,0:T(8,128)(2,1)S(1)} %get-tuple-element.41), channel_id=1, replica_groups={{0,1,2,3,4,5,6,7},{8,9,10,11,12,13,14,15},{16,17,18,19,20,21,22,23},{24..., dimensions={0} | all-to-all | bytes 262144 | tf_op jit(solution)/shard_map/all_to_all | solution.py:342
  26.0 0.9 broadcast_in_dim.27
  26.8 5.9 %all-to-all-start.2 = ((bf16[32,16,512]{2,1,0:T(8,128)(2,1)}), bf16[32,16,512]{2,1,0:T(8,128)(2,1)S(1)}, u32[]{:S(2)}, u32[]{:S(2)}) async-start(bf16[32,16,512]{2,1,0:T(8,128)(2,1)} %broadcast_in_dim.27), calls=%async_computation.2 | async-start | bytes 1048576 | tf_op jit(solution)/shard_map/all_to_all | solution.py:336
  32.8 1.6 %collective-permute-start.3 = (bf16[128,112]{1,0:T(8,128)(2,1)S(1)}, bf16[128,112]{1,0:T(8,128)(2,1)S(1)}, u32[]{:S(2)}, u32[]{:S(2)}) collective-permute-start(bf16[128,112]{1,0:T(8,128)(2,1)S(1)} %get-tuple-element.43), channel_id=1, source_target_pairs={{0,8},{1,9},{2,10},{3,11},{4,12},{5,13},{6,14},{7,15},{8,0},{9,1},... | collective-permute-start | bytes 86024 | tf_op jit(solution)/shard_map/ppermute | solution.py:347
  34.3 2.7 %collective-permute-start.4 = (bf16[128,112]{1,0:T(8,128)(2,1)S(1)}, bf16[128,112]{1,0:T(8,128)(2,1)S(1)}, u32[]{:S(2)}, u32[]{:S(2)}) collective-permute-start(bf16[128,112]{1,0:T(8,128)(2,1)S(1)} %get-tuple-element.44), channel_id=1, source_target_pairs={{0,16},{1,17},{2,18},{3,19},{4,20},{5,21},{6,22},{7,23},{8,24},{9,... | collective-permute-start | bytes 86024 | tf_op jit(solution)/shard_map/ppermute | solution.py:347
  37.1 0.5 collective-permute-start.5
  37.6 4.1 %collective-permute-done.3.h1_ref = bf16[128,112]{1,0:T(8,128)(2,1)S(1)} collective-permute-done((bf16[128,112]{1,0:T(8,128)(2,1)S(1)}, bf16[128,112]{1,0:T(8,128)(2,1)S(1)}, u32[]{:S(2)}, u32[]{:S(2)}) %collective-permute-start.3) | collective-permute-done | bytes 28704 | tf_op jit(solution)/shard_map/ppermute | solution.py:347
  41.7 2.3 %collective-permute-done.4.h2_ref = bf16[128,112]{1,0:T(8,128)(2,1)S(1)} collective-permute-done((bf16[128,112]{1,0:T(8,128)(2,1)S(1)}, bf16[128,112]{1,0:T(8,128)(2,1)S(1)}, u32[]{:S(2)}, u32[]{:S(2)}) %collective-permute-start.4) | collective-permute-done | bytes 28704 | tf_op jit(solution)/shard_map/ppermute | solution.py:347
  43.9 0.2 collective-permute-done.5.h3_ref
  44.1 0.0 all-to-all-done.2
  44.1 6.9 %shard_map.128 = (bf16[512,512]{1,0:T(8,128)(2,1)}, f32[2,2,8,256]{3,2,1,0:T(8,128)S(1)}) custom-call(s32[1]{0:T(128)} %bitcast.pos_ref, bf16[256,1792]{1,0:T(8,128)(2,1)S(1)} %bitcast.23, bf16[16,1792]{1,0:T(8,128)(2,1)S(1)} %bitcast.33, bf16[512,512]{1,0:T(8,128)(2,1)S(1)} %bitcast.28, bf16[256,1792]{1,0:T(8,128)(2,1)S(1)} %bitcast.26, ...), custom_call_target="tpu_custom_call" | custom-call | flops 2147483648 | bytes 4194304 | tf_op jit(solution)/shard_map/pallas_call | solution.py:203
  51.0 5.4 %all-to-all-start.3 = ((bf16[32,16,512]{2,1,0:T(8,128)(2,1)}), bf16[32,16,512]{2,1,0:T(8,128)(2,1)}, u32[]{:S(2)}, u32[]{:S(2)}) async-start(bf16[32,16,512]{2,1,0:T(8,128)(2,1)} %bitcast.8), calls=%async_computation.3 | async-start | bytes 1048576 | tf_op jit(solution)/shard_map/all_to_all | solution.py:336
  56.4 7.3 %shard_map.129 = (bf16[256,1792]{1,0:T(8,128)(2,1)}, bf16[16,1792]{1,0:T(8,128)(2,1)}, bf16[256,1792]{1,0:T(8,128)(2,1)}, bf16[16,1792]{1,0:T(8,128)(2,1)}, bf16[256,512]{1,0:T(8,128)(2,1)}) custom-call(s32[1]{0:T(128)} %bitcast.pos_ref, bf16[256,1792]{1,0:T(8,128)(2,1)S(1)} %bitcast.24, bf16[16,1792]{1,0:T(8,128)(2,1)S(1)} %bitcast.34, ...), custom_call_target="tpu_custom_call" | custom-call | flops 4026531840 | bytes 4194304 | tf_op jit(solution)/shard_map/pallas_call | solution.py:203
  63.7 3.3 %all-to-all-done.3 = bf16[32,16,512]{2,1,0:T(8,128)(2,1)} async-done(((bf16[32,16,512]{2,1,0:T(8,128)(2,1)}), bf16[32,16,512]{2,1,0:T(8,128)(2,1)}, u32[]{:S(2)}, u32[]{:S(2)}) %all-to-all-start.3) | async-done | bytes 524320 | tf_op jit(solution)/shard_map/all_to_all | solution.py:336
  67.0 1.1 %reduce_sum.25 = bf16[16,512]{1,0:T(8,128)(2,1)S(1)} reduce(bf16[32,16,512]{2,1,0:T(8,128)(2,1)} %all-to-all-done.3, bf16[]{:T(256)} %constant.7.clone.1), dimensions={0}, to_apply=%region_1.0 | reduce | flops 253952 | bytes 540674 | tf_op jit(solution)/shard_map/reduce_sum | solution.py:393
  68.1 0.1 broadcast_in_dim.33
  68.2 15.2 %all_to_all.31 = bf16[32,16,512]{2,1,0:T(8,128)(2,1)S(1)} all-to-all(bf16[32,16,512]{2,1,0:T(8,128)(2,1)S(1)} %broadcast_in_dim.33), channel_id=1, replica_groups=mesh['dp'=8,'ctx'=32] {'ctx'}, dimensions={0} | all-to-all | bytes 1048576 | tf_op jit(solution)/shard_map/all_to_all | solution.py:336
  83.4 0.3 shard_map.130
  83.7 0.3 shard_map.131
  84.0 6.4 %collective-permute-start.8 = (bf16[112,512]{1,0:T(8,128)(2,1)S(1)}, bf16[112,512]{1,0:T(8,128)(2,1)S(1)}, u32[]{:S(2)}, u32[]{:S(2)}) collective-permute-start(bf16[112,512]{1,0:T(8,128)(2,1)S(1)} %shard_map.131), channel_id=1, source_target_pairs={{0,192},{32,224},{64,128},{96,160},{128,64},{160,96},{192,0},{224,... | collective-permute-start | bytes 344072 | tf_op jit(solution)/shard_map/ppermute | solution.py:347
  90.4 1.0 collective-permute-start.7
  91.4 1.5 %collective-permute-start.6 = (bf16[112,512]{1,0:T(8,128)(2,1)S(1)}, bf16[112,512]{1,0:T(8,128)(2,1)S(1)}, u32[]{:S(2)}, u32[]{:S(2)}) collective-permute-start(bf16[112,512]{1,0:T(8,128)(2,1)S(1)} %shard_map.131), channel_id=1, source_target_pairs={{0,96},{32,64},{64,32},{96,0},{128,224},{160,192},{192,160},{224,1... | collective-permute-start | bytes 344072 | tf_op jit(solution)/shard_map/ppermute | solution.py:347
  92.9 8.5 %all_to_all.32 = bf16[8,4,16,112]{3,2,1,0:T(8,128)(2,1)S(1)} all-to-all(bf16[8,4,16,112]{3,2,1,0:T(8,128)(2,1)S(1)} %shard_map.130), channel_id=1, replica_groups={{0,1,2,3,4,5,6,7},{8,9,10,11,12,13,14,15},{16,17,18,19,20,21,22,23},{24..., dimensions={0} | all-to-all | bytes 229376 | tf_op jit(solution)/shard_map/all_to_all | solution.py:342
  101.4 0.5 collective-permute-done.7
  101.9 0.4 collective-permute-done.6
  102.2 0.1 add_convert_fusion
  102.3 1.6 %collective-permute-start.9 = (bf16[112,512]{1,0:T(8,128)(2,1)S(1)}, bf16[112,512]{1,0:T(8,128)(2,1)S(1)}, u32[]{:S(2)}, u32[]{:S(2)}) collective-permute-start(bf16[112,512]{1,0:T(8,128)(2,1)S(1)} %add_convert_fusion), channel_id=1, source_target_pairs={{0,32},{32,0},{64,96},{96,64},{128,160},{160,128},{192,224},{224,1... | collective-permute-start | bytes 344072 | tf_op jit(solution)/shard_map/ppermute | solution.py:347
  103.9 0.1 copy.15
  104.0 0.8 broadcast_in_dim_reshape.3
  104.9 2.3 %collective-permute-done.9 = bf16[112,512]{1,0:T(8,128)(2,1)S(1)} collective-permute-done((bf16[112,512]{1,0:T(8,128)(2,1)S(1)}, bf16[112,512]{1,0:T(8,128)(2,1)S(1)}, u32[]{:S(2)}, u32[]{:S(2)}) %collective-permute-start.9) | collective-permute-done | bytes 114720 | tf_op jit(solution)/shard_map/ppermute | solution.py:347
  107.2 0.7 convert_add_fusion
  (13 shorter events, 0.0 us)
Async XLA Ops:
  1.7 0.9 copy-start.4
  1.7 10.5 %copy-start.5 = (bf16[1,256,512]{2,1,0:T(8,128)(2,1)S(1)}, bf16[1,256,512]{2,1,0:T(8,128)(2,1)}, u32[]{:S(2)}) copy-start(bf16[1,256,512]{2,1,0:T(8,128)(2,1)} %param.8) | copy-start | bytes 786436
  2.6 9.7 %copy-start.6 = (bf16[1,16,1792]{2,1,0:T(8,128)(2,1)S(1)}, bf16[1,16,1792]{2,1,0:T(8,128)(2,1)}, u32[]{:S(2)}) copy-start(bf16[1,16,1792]{2,1,0:T(8,128)(2,1)} %param.9) | copy-start | bytes 172036
  2.6 9.7 %copy-start.7 = (bf16[1,16,1792]{2,1,0:T(8,128)(2,1)S(1)}, bf16[1,16,1792]{2,1,0:T(8,128)(2,1)}, u32[]{:S(2)}) copy-start(bf16[1,16,1792]{2,1,0:T(8,128)(2,1)} %param.13) | copy-start | bytes 172036
  2.6 14.4 %collective-permute-start.2 = (bf16[112,512]{1,0:T(8,128)(2,1)S(1)}, bf16[112,512]{1,0:T(8,128)(2,1)S(1)}, u32[]{:S(2)}, u32[]{:S(2)}) collective-permute-start(bf16[112,512]{1,0:T(8,128)(2,1)S(1)} %copy-done.4), channel_id=1, source_target_pairs={{0,24},{1,25},{2,26},{3,27},{4,28},{5,29},{6,30},{7,31},{8,16},{9,... | collective-permute-start | bytes 344072 | tf_op jit(solution)/shard_map/ppermute | solution.py:347
  5.7 11.3 %collective-permute-start.1 = (bf16[112,512]{1,0:T(8,128)(2,1)S(1)}, bf16[112,512]{1,0:T(8,128)(2,1)S(1)}, u32[]{:S(2)}, u32[]{:S(2)}) collective-permute-start(bf16[112,512]{1,0:T(8,128)(2,1)S(1)} %copy-done.4), channel_id=1, source_target_pairs={{0,16},{1,17},{2,18},{3,19},{4,20},{5,21},{6,22},{7,23},{8,24},{9,... | collective-permute-start | bytes 344072 | tf_op jit(solution)/shard_map/ppermute | solution.py:347
  6.3 10.7 %collective-permute-start = (bf16[112,512]{1,0:T(8,128)(2,1)S(1)}, bf16[112,512]{1,0:T(8,128)(2,1)S(1)}, u32[]{:S(2)}, u32[]{:S(2)}) collective-permute-start(bf16[112,512]{1,0:T(8,128)(2,1)S(1)} %copy-done.4), channel_id=1, source_target_pairs={{0,8},{1,9},{2,10},{3,11},{4,12},{5,13},{6,14},{7,15},{8,0},{9,1},... | collective-permute-start | bytes 344072 | tf_op jit(solution)/shard_map/ppermute | solution.py:347
  6.7 10.3 %all-to-all-start = ((bf16[8,4,16,112]{3,2,1,0:T(8,128)(2,1)}), bf16[8,4,16,112]{3,2,1,0:T(8,128)(2,1)S(1)}, u32[]{:S(2)}, u32[]{:S(2)}) async-start(bf16[8,4,16,112]{3,2,1,0:T(8,128)(2,1)} %bitcast.19), calls=%async_computation | async-start | bytes 262144 | tf_op jit(solution)/shard_map/all_to_all | solution.py:342
  12.3 1.2 %copy-start = (bf16[1,256,1792]{2,1,0:T(8,128)(2,1)S(1)}, bf16[1,256,1792]{2,1,0:T(8,128)(2,1)}, u32[]{:S(2)}) copy-start(bf16[1,256,1792]{2,1,0:T(8,128)(2,1)} %param.7) | copy-start | bytes 2752516
  13.5 1.2 %copy-start.2 = (bf16[1,256,1792]{2,1,0:T(8,128)(2,1)S(1)}, bf16[1,256,1792]{2,1,0:T(8,128)(2,1)}, u32[]{:S(2)}) copy-start(bf16[1,256,1792]{2,1,0:T(8,128)(2,1)} %param.12) | copy-start | bytes 2752516
  17.3 26.8 %copy-start.3 = (bf16[1,256,1792]{2,1,0:T(8,128)(2,1)S(1)}, bf16[1,256,1792]{2,1,0:T(8,128)(2,1)}, u32[]{:S(2)}) copy-start(bf16[1,256,1792]{2,1,0:T(8,128)(2,1)} %param.12) | copy-start | bytes 2752516
  26.0 18.2 %copy-start.1 = (bf16[1,256,1792]{2,1,0:T(8,128)(2,1)S(1)}, bf16[1,256,1792]{2,1,0:T(8,128)(2,1)}, u32[]{:S(2)}) copy-start(bf16[1,256,1792]{2,1,0:T(8,128)(2,1)} %param.7) | copy-start | bytes 2752516
  26.8 17.3 %all-to-all-start.2 = ((bf16[32,16,512]{2,1,0:T(8,128)(2,1)}), bf16[32,16,512]{2,1,0:T(8,128)(2,1)S(1)}, u32[]{:S(2)}, u32[]{:S(2)}) async-start(bf16[32,16,512]{2,1,0:T(8,128)(2,1)} %broadcast_in_dim.27), calls=%async_computation.2 | async-start | bytes 1048576 | tf_op jit(solution)/shard_map/all_to_all | solution.py:336
  32.8 8.9 %collective-permute-start.3 = (bf16[128,112]{1,0:T(8,128)(2,1)S(1)}, bf16[128,112]{1,0:T(8,128)(2,1)S(1)}, u32[]{:S(2)}, u32[]{:S(2)}) collective-permute-start(bf16[128,112]{1,0:T(8,128)(2,1)S(1)} %get-tuple-element.43), channel_id=1, source_target_pairs={{0,8},{1,9},{2,10},{3,11},{4,12},{5,13},{6,14},{7,15},{8,0},{9,1},... | collective-permute-start | bytes 86024 | tf_op jit(solution)/shard_map/ppermute | solution.py:347
  34.3 9.6 %collective-permute-start.4 = (bf16[128,112]{1,0:T(8,128)(2,1)S(1)}, bf16[128,112]{1,0:T(8,128)(2,1)S(1)}, u32[]{:S(2)}, u32[]{:S(2)}) collective-permute-start(bf16[128,112]{1,0:T(8,128)(2,1)S(1)} %get-tuple-element.44), channel_id=1, source_target_pairs={{0,16},{1,17},{2,18},{3,19},{4,20},{5,21},{6,22},{7,23},{8,24},{9,... | collective-permute-start | bytes 86024 | tf_op jit(solution)/shard_map/ppermute | solution.py:347
  37.1 7.0 %collective-permute-start.5 = (bf16[128,112]{1,0:T(8,128)(2,1)S(1)}, bf16[128,112]{1,0:T(8,128)(2,1)S(1)}, u32[]{:S(2)}, u32[]{:S(2)}) collective-permute-start(bf16[128,112]{1,0:T(8,128)(2,1)S(1)} %get-tuple-element.45), channel_id=1, source_target_pairs={{0,24},{1,25},{2,26},{3,27},{4,28},{5,29},{6,30},{7,31},{8,16},{9,... | collective-permute-start | bytes 86024 | tf_op jit(solution)/shard_map/ppermute | solution.py:347
  51.0 16.0 %all-to-all-start.3 = ((bf16[32,16,512]{2,1,0:T(8,128)(2,1)}), bf16[32,16,512]{2,1,0:T(8,128)(2,1)}, u32[]{:S(2)}, u32[]{:S(2)}) async-start(bf16[32,16,512]{2,1,0:T(8,128)(2,1)} %bitcast.8), calls=%async_computation.3 | async-start | bytes 1048576 | tf_op jit(solution)/shard_map/all_to_all | solution.py:336
  84.0 17.4 %collective-permute-start.8 = (bf16[112,512]{1,0:T(8,128)(2,1)S(1)}, bf16[112,512]{1,0:T(8,128)(2,1)S(1)}, u32[]{:S(2)}, u32[]{:S(2)}) collective-permute-start(bf16[112,512]{1,0:T(8,128)(2,1)S(1)} %shard_map.131), channel_id=1, source_target_pairs={{0,192},{32,224},{64,128},{96,160},{128,64},{160,96},{192,0},{224,... | collective-permute-start | bytes 344072 | tf_op jit(solution)/shard_map/ppermute | solution.py:347
  90.4 11.5 %collective-permute-start.7 = (bf16[112,512]{1,0:T(8,128)(2,1)S(1)}, bf16[112,512]{1,0:T(8,128)(2,1)S(1)}, u32[]{:S(2)}, u32[]{:S(2)}) collective-permute-start(bf16[112,512]{1,0:T(8,128)(2,1)S(1)} %shard_map.131), channel_id=1, source_target_pairs={{0,160},{32,128},{64,224},{96,192},{128,32},{160,0},{192,96},{224,... | collective-permute-start | bytes 344072 | tf_op jit(solution)/shard_map/ppermute | solution.py:347
  91.4 10.8 %collective-permute-start.6 = (bf16[112,512]{1,0:T(8,128)(2,1)S(1)}, bf16[112,512]{1,0:T(8,128)(2,1)S(1)}, u32[]{:S(2)}, u32[]{:S(2)}) collective-permute-start(bf16[112,512]{1,0:T(8,128)(2,1)S(1)} %shard_map.131), channel_id=1, source_target_pairs={{0,96},{32,64},{64,32},{96,0},{128,224},{160,192},{192,160},{224,1... | collective-permute-start | bytes 344072 | tf_op jit(solution)/shard_map/ppermute | solution.py:347
  102.3 4.9 %collective-permute-start.9 = (bf16[112,512]{1,0:T(8,128)(2,1)S(1)}, bf16[112,512]{1,0:T(8,128)(2,1)S(1)}, u32[]{:S(2)}, u32[]{:S(2)}) collective-permute-start(bf16[112,512]{1,0:T(8,128)(2,1)S(1)} %add_convert_fusion), channel_id=1, source_target_pairs={{0,32},{32,0},{64,96},{96,64},{128,160},{160,128},{192,224},{224,1... | collective-permute-start | bytes 344072 | tf_op jit(solution)/shard_map/ppermute | solution.py:347
